TPU v7x, 32 devices: a whole 2x2x4 slice. The times are simulated.
32 devices in a mesh: dp: 4 (over y, x), mp: 8 (over z, core).
Axes of the slice: x: 2, y: 2, z: 4, core: 2. Of those that a mesh axis runs over, the one named last changes fastest.
Arguments:
- tokens: bfloat16 [3072, 2048], P(('dp', 'mp')), may hold values from -6 to 6
- lengths: int32 [4, 3], P('dp'), may hold values from 64 to 624, as said below
- first_gain: float32 [2048], replicated, may hold values from 0.25 to 1.75
- branch_gate: bfloat16 [2048, 2560], P(None, 'mp'), may hold values from -0.125 to 0.125
- branch_input: bfloat16 [2048, 2560], P(None, 'mp'), may hold values from -0.125 to 0.125
- conv_weight: float32 [4, 2560], P(None, 'mp'), may hold values from -3 to 3
- conv_bias: float32 [2560], P('mp'), may hold values from -3 to 3
- rate_weight: bfloat16 [16, 160, 160], P('mp'), may hold values from -0.5 to 0.5
- rate_bias: float32 [2560], P('mp'), may hold values from -3 to 3
- inlet_weight: bfloat16 [16, 160, 160], P('mp'), may hold values from -0.5 to 0.5
- inlet_bias: float32 [2560], P('mp'), may hold values from -3 to 3
- decay_param: float32 [2560], P('mp'), may hold values from -9 to -1
- block_out: bfloat16 [2560, 2048], P('mp'), may hold values from -0.3125 to 0.3125
- second_gain: float32 [2048], replicated, may hold values from 0.25 to 1.75
- gate_weight: bfloat16 [2048, 6144], P(None, 'mp'), may hold values from -0.125 to 0.125
- up_weight: bfloat16 [2048, 6144], P(None, 'mp'), may hold values from -0.125 to 0.125
- down_weight: bfloat16 [6144, 2048], P('mp'), may hold values from -0.125 to 0.125
- out_grad: bfloat16 [3072, 2048], P(('dp', 'mp')), may hold values from -6 to 6
Outputs:
- output: bfloat16 [3072, 2048], P(('dp', 'mp'))
- input_grad: float32 [3072, 2048], P(('dp', 'mp'))
- first_gain_grad: float32 [2048], replicated
- branch_gate_grad: float32 [2048, 2560], P(None, 'mp')
- branch_input_grad: float32 [2048, 2560], P(None, 'mp')
- conv_weight_grad: float32 [4, 2560], P(None, 'mp')
- conv_bias_grad: float32 [2560], P('mp')
- rate_weight_grad: float32 [16, 160, 160], P('mp')
- rate_bias_grad: float32 [2560], P('mp')
- inlet_weight_grad: float32 [16, 160, 160], P('mp')
- inlet_bias_grad: float32 [2560], P('mp')
- decay_param_grad: float32 [2560], P('mp')
- block_out_grad: float32 [2560, 2048], P('mp')
- second_gain_grad: float32 [2048], replicated
- gate_weight_grad: float32 [2048, 6144], P(None, 'mp')
- up_weight_grad: float32 [2048, 6144], P(None, 'mp')
- down_weight_grad: float32 [6144, 2048], P('mp')
Inputs may be any that keep to these rules, and one draw needn't show every extreme that they name: Each row lists in order the lengths of the 3 sequences packed into one bucket of 768 rows; they sum to 768; the middle one has 624 tokens, and the first and last have 96 * 2 // 3 and 80 tokens, in either order.
All inputs are finite; a program needn't handle non-finite values.
Results may differ from a plain program's by a relative error of at most 0.018.
Values may be sent and summed in bfloat16 or wider, within the bound.
No kernel may reach another device: no remote copies, remote signals or barrier semaphores. Data moves between devices by JAX's collectives and lax.ppermute only.
A program may use at most 256 MiB of HBM per device.

v0:
```python
import jax
import jax.numpy as jnp
from jax import lax
from jax.sharding import PartitionSpec as P

EPS = 1e-06
DECAY_SCALE = 8.0


def root_norm(values, gain):
    return values * lax.rsqrt(jnp.mean(values * values, axis=-1, keepdims=True) + EPS) * gain


def sequence_positions(lengths_row, count):
    ends = jnp.cumsum(lengths_row)
    starts = ends - lengths_row
    places = jnp.arange(count, dtype=jnp.int32)
    inside = places[:, None] >= starts[None, :]
    first = jnp.max(jnp.where(inside, starts[None, :], 0), axis=1)
    return places - first


def temporal_mix(input_pre, conv_weight, conv_bias, positions):
    total = conv_bias[None, :] + conv_weight[0][None, :] * input_pre
    for delay_steps in range(1, conv_weight.shape[0]):
        moved = jnp.pad(input_pre, ((delay_steps, 0), (0, 0)))[:-delay_steps]
        keep = (positions >= delay_steps)[:, None]
        total = total + jnp.where(keep, conv_weight[delay_steps][None, :] * moved, 0.0)
    return total


def combine_steps(early, late):
    return (early[0] * late[0], late[0] * early[1] + late[1])


def gated_recurrence(rate_pre, inlet_pre, conv_in, decay_param, positions):
    rate = jax.nn.sigmoid(rate_pre)
    inlet = jax.nn.sigmoid(inlet_pre)
    log_a = -DECAY_SCALE * rate * jax.nn.softplus(decay_param)[None, :]
    fresh = (positions == 0)[:, None]
    carry = jnp.where(fresh, 0.0, jnp.exp(log_a))
    scale = jnp.where(fresh, 1.0, jnp.sqrt(-jnp.expm1(2.0 * log_a)))
    drive = scale * inlet * conv_in
    return lax.associative_scan(combine_steps, (carry, drive), axis=0)[1]


def product(left, right):
    return jnp.dot(left, right, preferred_element_type=jnp.float32)


def times_transposed(left, right):
    return lax.dot_general(
        left, right, (((1,), (1,)), ((), ())), preferred_element_type=jnp.float32
    )


def transposed_times(left, right):
    return lax.dot_general(
        left, right, (((0,), (0,)), ((), ())), preferred_element_type=jnp.float32
    )


def block_product(values, weights):
    rows = values.reshape(values.shape[0], weights.shape[0], weights.shape[1])
    mixed = jnp.einsum("thi,hij->thj", rows, weights, preferred_element_type=jnp.float32)
    return mixed.reshape(values.shape[0], -1)


def block_return(grads, weights):
    rows = grads.reshape(grads.shape[0], weights.shape[0], weights.shape[1])
    mixed = jnp.einsum("thj,hij->thi", rows, weights, preferred_element_type=jnp.float32)
    return mixed.reshape(grads.shape[0], -1)


def block_gradient(values, grads, weights):
    left = values.reshape(values.shape[0], weights.shape[0], weights.shape[1])
    right = grads.reshape(grads.shape[0], weights.shape[0], weights.shape[1])
    return jnp.einsum("thi,thj->hij", left, right, preferred_element_type=jnp.float32)


def local(
    tokens,
    lengths,
    first_gain,
    branch_gate,
    branch_input,
    conv_weight,
    conv_bias,
    rate_weight,
    rate_bias,
    inlet_weight,
    inlet_bias,
    decay_param,
    block_out,
    second_gain,
    gate_weight,
    up_weight,
    down_weight,
    out_grad,
):
    own_count = tokens.shape[0]
    bucket = own_count * lax.axis_size("mp")
    positions = sequence_positions(lengths[0], bucket)
    own_input = tokens.astype(jnp.float32)

    def convolve(values, weight, bias):
        return temporal_mix(values, weight, bias, positions)

    def recurrence(rate_value, inlet_value, conv_value, decay_value, gate_value):
        state = gated_recurrence(rate_value, inlet_value, conv_value, decay_value, positions)
        return state * jax.nn.gelu(gate_value)

    own_first = root_norm(own_input, first_gain).astype(jnp.bfloat16)
    first_rows = lax.all_gather(own_first, "mp", axis=0, tiled=True)
    gate_pre = product(first_rows, branch_gate)
    input_pre = product(first_rows, branch_input)
    conv_full, conv_pull = jax.vjp(convolve, input_pre, conv_weight, conv_bias)
    conv_low = conv_full.astype(jnp.bfloat16)
    rate_pre = block_product(conv_low, rate_weight) + rate_bias
    inlet_pre = block_product(conv_low, inlet_weight) + inlet_bias
    mixed_full, mixed_pull = jax.vjp(
        recurrence, rate_pre, inlet_pre, conv_low.astype(jnp.float32), decay_param, gate_pre
    )
    mixed, conv_low, conv_pull, mixed_pull = (
        mixed_full.astype(jnp.bfloat16),
        conv_low,
        conv_pull,
        mixed_pull,
    )
    own_middle = own_input + lax.psum_scatter(
        product(mixed, block_out), "mp", scatter_dimension=0, tiled=True
    )
    own_second = root_norm(own_middle, second_gain).astype(jnp.bfloat16)
    second_rows = lax.all_gather(own_second, "mp", axis=0, tiled=True)
    gate_act = product(second_rows, gate_weight)
    up_act = product(second_rows, up_weight)

    def activation(gate_value, up_value):
        return jax.nn.gelu(gate_value) * up_value

    hidden_full, hidden_pull = jax.vjp(activation, gate_act, up_act)
    hidden = hidden_full.astype(jnp.bfloat16)
    output = (
        own_middle
        + lax.psum_scatter(
            product(hidden, down_weight).astype(jnp.bfloat16), "mp", scatter_dimension=0, tiled=True
        ).astype(jnp.float32)
    ).astype(jnp.bfloat16)
    grad_rows = lax.all_gather(out_grad, "mp", axis=0, tiled=True)
    down_weight_grad = transposed_times(hidden, grad_rows)
    gate_back, up_back = hidden_pull(times_transposed(grad_rows, down_weight))
    gate_low = gate_back.astype(jnp.bfloat16)
    up_low = up_back.astype(jnp.bfloat16)
    gate_weight_grad = transposed_times(second_rows, gate_low)
    up_weight_grad = transposed_times(second_rows, up_low)
    second_input = lax.psum_scatter(
        times_transposed(gate_low, gate_weight) + times_transposed(up_low, up_weight),
        "mp",
        scatter_dimension=0,
        tiled=True,
    )
    second_pull = jax.vjp(root_norm, own_middle, second_gain)[1]
    middle_part, second_gain_grad = second_pull(second_input)
    middle_grad = out_grad.astype(jnp.float32) + middle_part
    middle_rows = lax.all_gather(middle_grad.astype(jnp.bfloat16), "mp", axis=0, tiled=True)
    block_out_grad = transposed_times(mixed, middle_rows)
    rate_back, inlet_back, conv_back, decay_param_grad, gate_pre_back = mixed_pull(
        times_transposed(middle_rows, block_out)
    )
    rate_low = rate_back.astype(jnp.bfloat16)
    inlet_low = inlet_back.astype(jnp.bfloat16)
    gate_pre_low = gate_pre_back.astype(jnp.bfloat16)
    rate_weight_grad = block_gradient(conv_low, rate_low, rate_weight)
    inlet_weight_grad = block_gradient(conv_low, inlet_low, inlet_weight)
    rate_bias_grad = jnp.sum(rate_low.astype(jnp.float32), axis=0)
    inlet_bias_grad = jnp.sum(inlet_low.astype(jnp.float32), axis=0)
    conv_total = (
        conv_back + block_return(rate_low, rate_weight) + block_return(inlet_low, inlet_weight)
    )
    input_back, conv_weight_grad, conv_bias_grad = conv_pull(conv_total)
    input_low = input_back.astype(jnp.bfloat16)
    branch_gate_grad = transposed_times(first_rows, gate_pre_low)
    branch_input_grad = transposed_times(first_rows, input_low)
    first_input = lax.psum_scatter(
        (
            times_transposed(gate_pre_low, branch_gate) + times_transposed(input_low, branch_input)
        ).astype(jnp.bfloat16),
        "mp",
        scatter_dimension=0,
        tiled=True,
    ).astype(jnp.float32)
    first_pull = jax.vjp(root_norm, own_input, first_gain)[1]
    first_part, first_gain_grad = first_pull(first_input)
    input_grad = middle_grad + first_part
    first_gain_grad, second_gain_grad = lax.psum((first_gain_grad, second_gain_grad), ("dp", "mp"))
    summed = lax.psum(
        (
            branch_gate_grad,
            branch_input_grad,
            conv_weight_grad,
            conv_bias_grad,
            rate_weight_grad,
            rate_bias_grad,
            inlet_weight_grad,
            inlet_bias_grad,
            decay_param_grad,
            block_out_grad,
            gate_weight_grad,
            up_weight_grad,
            down_weight_grad,
        ),
        "dp",
    )
    return (
        output,
        input_grad,
        first_gain_grad,
        summed[0],
        summed[1],
        summed[2],
        summed[3],
        summed[4],
        summed[5],
        summed[6],
        summed[7],
        summed[8],
        summed[9],
        second_gain_grad,
        summed[10],
        summed[11],
        summed[12],
    )


def solution(mesh):
    in_specs = (
        P(("dp", "mp"), None),
        P("dp", None),
        P(),
        P(None, "mp"),
        P(None, "mp"),
        P(None, "mp"),
        P("mp"),
        P("mp", None, None),
        P("mp"),
        P("mp", None, None),
        P("mp"),
        P("mp"),
        P("mp", None),
        P(),
        P(None, "mp"),
        P(None, "mp"),
        P("mp", None),
        P(("dp", "mp"), None),
    )
    out_specs = (
        P(("dp", "mp"), None),
        P(("dp", "mp"), None),
        P(),
        P(None, "mp"),
        P(None, "mp"),
        P(None, "mp"),
        P("mp"),
        P("mp", None, None),
        P("mp"),
        P("mp", None, None),
        P("mp"),
        P("mp"),
        P("mp", None),
        P(),
        P(None, "mp"),
        P(None, "mp"),
        P("mp", None),
    )
    return jax.shard_map(local, mesh=mesh, in_specs=in_specs, out_specs=out_specs, check_vma=False)
```

profile of v0, /device:TPU:0, one launch (start us, length us, event | category | flops | bytes accessed | tf_op | source)
XLA Modules:
  0.0 1891.5 jit_solution(11660720443163587653)
XLA Ops:
  15.6 37.3 %all-gather.5.cloned.1.call-done = bf16[768,2048]{1,0:T(8,128)(2,1)} async-done(((bf16[96,2048]{1,0:T(8,128)(2,1)}), bf16[768,2048]{1,0:T(8,128)(2,1)}) %all-gather.5.cloned.1.call-update) | async-done | bytes 3145744 | tf_op jit(solution)/shard_map/all_gather | solution.py:114
  60.3 18.0 slice.313
  78.4 17.9 slice.318
  96.3 18.0 slice.314
  116.6 5.0 convert_multiply_fusion.5
  121.6 18.1 slice.380
  139.7 17.9 slice.316
  157.6 17.9 slice.315
  178.1 10.6 slice.324
  188.7 9.7 slice.320
  198.4 10.4 slice.322
  208.8 10.2 slice.321
  221.1 5.7 slice.325
  226.7 5.8 slice.330
  232.6 5.7 slice.326
  238.3 5.7 slice.376
  244.0 5.7 slice.328
  249.8 5.7 slice.327
  329.0 10.2 slice.378
  339.2 10.6 slice.319
  418.5 6.5 pad.401
  426.8 10.7 pad.403
  440.5 10.6 pad.402
  455.7 19.2 %pad.404 = f32[768,320]{0,1:T(8,128)} pad(f32[384,320]{0,1:T(8,128)} %pad_maximum_fusion, f32[]{:T(128)} %constant.22.clone.1), padding=0_1_1x0_0_0 | pad | bytes 1474564 | tf_op jit(solution)/shard_map/jvp()/pad | solution.py:44
  474.9 19.3 %pad.405 = f32[768,320]{0,1:T(8,128)} pad(f32[384,320]{0,1:T(8,128)} %add.455, f32[]{:T(128)} %constant.22.clone.1), padding=1_0_1x0_0_0 | pad | bytes 1474564 | tf_op jit(solution)/shard_map/jvp()/pad | solution.py:44
  494.2 5.6 multiply_convert_fusion.2
  505.2 68.8 %reduce-scatter.5.cloned.1.call-done = f32[96,2048]{1,0:T(8,128)} async-done(((f32[768,2048]{1,0:T(8,128)}), f32[96,2048]{1,0:T(8,128)}) %reduce-scatter.5.cloned.1.call-update) | async-done | bytes 786448 | tf_op jit(solution)/shard_map/reduce_scatter | solution.py:130
  578.4 35.7 %all-gather.7.cloned.1.call-done = bf16[768,2048]{1,0:T(8,128)(2,1)} async-done(((bf16[96,2048]{1,0:T(8,128)(2,1)}), bf16[768,2048]{1,0:T(8,128)(2,1)}) %all-gather.7.cloned.1.call-update) | async-done | bytes 3145744 | tf_op jit(solution)/shard_map/all_gather | solution.py:134
  614.1 7.0 fusion.108
  625.2 27.7 %all-gather.9.cloned.1.call-done = bf16[768,2048]{1,0:T(8,128)(2,1)} async-done(((bf16[96,2048]{1,0:T(8,128)(2,1)}), bf16[768,2048]{1,0:T(8,128)(2,1)}) %all-gather.9.cloned.1.call-update) | async-done | bytes 3145744 | tf_op jit(solution)/shard_map/all_gather | solution.py:149
  652.8 8.7 multiply_convert_fusion
  668.8 68.8 %reduce-scatter.9.cloned.1.call-done = f32[96,2048]{1,0:T(8,128)} async-done(((f32[768,2048]{1,0:T(8,128)}), f32[96,2048]{1,0:T(8,128)}) %reduce-scatter.9.cloned.1.call-update) | async-done | bytes 786448 | tf_op jit(solution)/shard_map/reduce_scatter | solution.py:156
  743.6 36.7 %all-gather.11.cloned.1.call-done = bf16[768,2048]{1,0:T(8,128)(2,1)} async-done(((bf16[96,2048]{1,0:T(8,128)(2,1)}), bf16[768,2048]{1,0:T(8,128)(2,1)}) %all-gather.11.cloned.1.call-update) | async-done | bytes 3145744 | tf_op jit(solution)/shard_map/all_gather | solution.py:165
  780.3 5.4 fusion.40
  787.3 18.1 slice.382
  805.4 17.9 slice.381
  827.2 10.2 slice.383
  847.6 10.4 slice.384
  860.1 5.7 slice.386
  865.8 5.7 slice.385
  981.5 6.4 pad.462
  987.9 6.5 pad.461
  994.4 6.4 pad.418
  1003.0 10.6 pad.464
  1013.6 10.7 pad.463
  1024.3 10.6 pad.413
  1094.0 6.4 pad.488
  1100.4 6.5 pad.469
  1106.9 6.5 pad.487
  1115.9 10.7 pad.490
  1126.6 10.6 pad.468
  1137.2 10.7 pad.489
  1150.4 19.5 %pad.465 = f32[768,320]{0,1:T(8,128)} pad(f32[384,320]{0,1:T(8,128)} %get-tuple-element.51, f32[]{:T(128)} %constant.22.clone.1), padding=1_0_1x0_0_0 | pad | bytes 1474564 | tf_op jit(solution)/shard_map/transpose(jvp())/pad | solution.py:44
  1172.9 19.2 %pad.492 = f32[768,320]{0,1:T(8,128)} pad(f32[384,320]{0,1:T(8,128)} %get-tuple-element.83, f32[]{:T(128)} %constant.22.clone.1), padding=0_1_1x0_0_0 | pad | bytes 1474564 | tf_op jit(solution)/shard_map/transpose(jvp())/pad | solution.py:44
  1192.2 19.5 %pad.467 = f32[768,320]{0,1:T(8,128)} pad(f32[383,320]{0,1:T(8,128)} %get-tuple-element.95, f32[]{:T(128)} %constant.22.clone.1), padding=2_1_1x0_0_0 | pad | bytes 1473284 | tf_op jit(solution)/shard_map/transpose(jvp())/pad | solution.py:44
  1211.6 19.2 %pad.491 = f32[768,320]{0,1:T(8,128)} pad(f32[384,320]{0,1:T(8,128)} %get-tuple-element.82, f32[]{:T(128)} %constant.22.clone.1), padding=1_0_1x0_0_0 | pad | bytes 1474564 | tf_op jit(solution)/shard_map/transpose(jvp())/pad | solution.py:44
  1230.9 19.5 %pad.466 = f32[768,320]{0,1:T(8,128)} pad(f32[384,320]{0,1:T(8,128)} %get-tuple-element.50, f32[]{:T(128)} %constant.22.clone.1), padding=0_1_1x0_0_0 | pad | bytes 1474564 | tf_op jit(solution)/shard_map/transpose(jvp())/pad | solution.py:44
  1250.4 19.2 %pad.408 = f32[768,320]{0,1:T(8,128)} pad(f32[383,320]{0,1:T(8,128)} %get-tuple-element.93, f32[]{:T(128)} %constant.22.clone.1), padding=2_1_1x0_0_0 | pad | bytes 1473284 | tf_op jit(solution)/shard_map/transpose(jvp())/pad | solution.py:44
  1269.7 5.9 fusion.21
  1289.3 5.3 convolution_convert_fusion
  1294.7 7.7 fusion.115
  1328.5 17.2 all-reduce.99
  1347.7 39.5 %all-reduce.98 = (f32[2048]{0:T(1024)}, f32[2048]{0:T(1024)}) all-reduce(f32[2048]{0:T(1024)} %get-tuple-element.24, f32[2048]{0:T(1024)} %get-tuple-element.21), channel_id=1, replica_groups=mesh['dp'=4,'mp'=8] {'dp','mp'}, use_global_device_ids=true, to_apply=%region_11.12 | all-reduce | flops 4096 | bytes 32768 | tf_op jit(solution)/shard_map/psum | solution.py:195
  1391.6 471.9 %all-reduce.103.cloned.1.call-done = (f32[2048,320]{0,1:T(8,128)}, f32[2048,320]{0,1:T(8,128)}, f32[2,160,160]{2,1,0:T(8,128)}, f32[2,160,160]{2,1,0:T(8,128)}, ...) async-done(((f32[2048,320]{0,1:T(8,128)}, f32[2048,320]{0,1:T(8,128)}, f32[2,160,160]{2,1,0:T(8,128)}, ...) | async-done | bytes 27148304 | tf_op jit(solution)/shard_map/psum | solution.py:196
  (446 shorter events, 465.2 us)
Async XLA Ops:
  7.2 645.6 %copy-start = (bf16[768,2048]{1,0:T(8,128)(2,1)S(1)}, bf16[768,2048]{1,0:T(8,128)(2,1)}, u32[]{:S(2)}) copy-start(bf16[768,2048]{1,0:T(8,128)(2,1)} %param.34) | copy-start | bytes 9437188
  7.2 45.6 %all-gather.5.cloned.1.call-start = ((), (), s32[]{:S(2)}) async-start(), calls=%async_computation.4 | async-start | bytes 3538944 | tf_op jit(solution)/shard_map/all_gather | solution.py:114
  11.7 562.3 %reduce-scatter.5.cloned.1.call-start = ((), (), s32[]{:S(2)}) async-start(), calls=%async_computation.5 | async-start | bytes 7077888 | tf_op jit(solution)/shard_map/reduce_scatter | solution.py:130
  13.4 102.2 %copy-start.53 = (f32[320]{0:T(512)}, f32[320]{0:T(512)S(1)}, u32[]{:S(2)}) copy-start(f32[320]{0:T(512)S(1)} %get-tuple-element.28) | copy-start | bytes 3844
  13.4 102.2 %copy-start.55 = (f32[320]{0:T(512)}, f32[320]{0:T(512)S(1)}, u32[]{:S(2)}) copy-start(f32[320]{0:T(512)S(1)} %get-tuple-element.29) | copy-start | bytes 3844
  15.5 100.2 %copy-start.57 = (f32[320]{0:T(512)}, f32[320]{0:T(512)S(1)}, u32[]{:S(2)}) copy-start(f32[320]{0:T(512)S(1)} %get-tuple-element.168) | copy-start | bytes 3844
  15.5 100.2 %copy-start.59 = (pred[768]{0:T(1024)(128)(4,1)}, pred[768]{0:T(1024)(128)(4,1)S(1)}, u32[]{:S(2)}) copy-start(pred[768]{0:T(1024)(128)(4,1)S(1)} %get-tuple-element.164) | copy-start | bytes 2308
  15.5 100.2 %copy-start.61 = (pred[768]{0:T(1024)(128)(4,1)}, pred[768]{0:T(1024)(128)(4,1)S(1)}, u32[]{:S(2)}) copy-start(pred[768]{0:T(1024)(128)(4,1)S(1)} %get-tuple-element.165) | copy-start | bytes 2308
  15.5 100.2 %copy-start.63 = (pred[768]{0:T(1024)(128)(4,1)}, pred[768]{0:T(1024)(128)(4,1)S(1)}, u32[]{:S(2)}) copy-start(pred[768]{0:T(1024)(128)(4,1)S(1)} %get-tuple-element.166) | copy-start | bytes 2308
  15.5 100.2 %copy-start.65 = (pred[768]{0:T(1024)(128)(4,1)}, pred[768]{0:T(1024)(128)(4,1)S(1)}, u32[]{:S(2)}) copy-start(pred[768]{0:T(1024)(128)(4,1)S(1)} %get-tuple-element.163) | copy-start | bytes 2308
  15.5 40.8 %copy-start.67 = (f32[320]{0:T(512)S(1)}, f32[320]{0:T(512)}, u32[]{:S(2)}) copy-start(f32[320]{0:T(512)} %param.24) | copy-start | bytes 3844
  15.6 42.7 %copy-start.45 = (bf16[2,160,160]{2,1,0:T(8,128)(2,1)S(1)}, bf16[2,160,160]{2,1,0:T(8,128)(2,1)}, u32[]{:S(2)}) copy-start(bf16[2,160,160]{2,1,0:T(8,128)(2,1)} %param.25) | copy-start | bytes 307204
  58.7 55.6 %copy-start.47 = (bf16[2,160,160]{2,1,0:T(8,128)(2,1)S(1)}, bf16[2,160,160]{2,1,0:T(8,128)(2,1)}, u32[]{:S(2)}) copy-start(bf16[2,160,160]{2,1,0:T(8,128)(2,1)} %param.27) | copy-start | bytes 307204
  60.3 56.3 %copy-start.69 = (f32[320]{0:T(512)S(1)}, f32[320]{0:T(512)}, u32[]{:S(2)}) copy-start(f32[320]{0:T(512)} %param.28) | copy-start | bytes 3844
  198.4 57.0 %copy-start.14 = (f32[192,320]{0,1:T(8,128)}, f32[192,320]{0,1:T(8,128)S(1)}, u32[]{:S(2)}) copy-start(f32[192,320]{0,1:T(8,128)S(1)} %slice.320) | copy-start | bytes 737284
  264.1 20.0 %copy-start.35 = (f32[48,320]{0,1:T(8,128)}, f32[48,320]{0,1:T(8,128)S(1)}, u32[]{:S(2)}) copy-start(f32[48,320]{0,1:T(8,128)S(1)} %slice.332) | copy-start | bytes 184324
  273.2 24.0 %copy-start.24 = (f32[48,320]{0,1:T(8,128)}, f32[48,320]{0,1:T(8,128)S(1)}, u32[]{:S(2)}) copy-start(f32[48,320]{0,1:T(8,128)S(1)} %get-tuple-element.160) | copy-start | bytes 184324
  306.8 43.0 %copy-start.21 = (f32[6,320]{0,1:T(8,128)}, f32[6,320]{0,1:T(8,128)S(1)}, u32[]{:S(2)}) copy-start(f32[6,320]{0,1:T(8,128)S(1)} %get-tuple-element.154) | copy-start | bytes 23044
  353.5 24.4 %copy-start.19 = (f32[1,320]{0,1:T(8,128)}, f32[1,320]{0,1:T(8,128)S(1)}, u32[]{:S(2)}) copy-start(f32[1,320]{0,1:T(8,128)S(1)} %get-tuple-element.73) | copy-start | bytes 3844
  374.5 17.6 copy-start.25
  384.6 20.6 %copy-start.23 = (f32[96,320]{0,1:T(8,128)S(1)}, f32[96,320]{0,1:T(8,128)}, u32[]{:S(2)}) copy-start(f32[96,320]{0,1:T(8,128)} %get-tuple-element.162) | copy-start | bytes 368644
  394.8 17.0 copy-start.33
  418.5 18.9 %copy-start.13 = (f32[192,320]{0,1:T(8,128)}, f32[192,320]{0,1:T(8,128)S(1)}, u32[]{:S(2)}) copy-start(f32[192,320]{0,1:T(8,128)S(1)} %pad.400) | copy-start | bytes 737284
  438.7 16.0 slice-start.2
  494.2 6.4 copy-start.41
  505.1 68.9 %copy-start.10 = (bf16[96,2048]{1,0:T(8,128)(2,1)S(1)}, bf16[96,2048]{1,0:T(8,128)(2,1)}, u32[]{:S(2)}) copy-start(bf16[96,2048]{1,0:T(8,128)(2,1)} %param.18) | copy-start | bytes 1179652
  505.1 71.4 %copy-start.51 = (f32[2048]{0:T(1024)S(1)}, f32[2048]{0:T(1024)}, u32[]{:S(2)}) copy-start(f32[2048]{0:T(1024)} %param.31) | copy-start | bytes 24580
  505.1 109.0 %all-gather.7.cloned.1.call-start = ((), (), s32[]{:S(2)}) async-start(), calls=%async_computation.6 | async-start | bytes 3538944 | tf_op jit(solution)/shard_map/all_gather | solution.py:134
  577.4 75.4 %all-gather.9.cloned.1.call-start = ((), (), s32[]{:S(2)}) async-start(), calls=%async_computation.8 | async-start | bytes 3538944 | tf_op jit(solution)/shard_map/all_gather | solution.py:149
  577.9 159.7 %reduce-scatter.9.cloned.1.call-start = ((), (), s32[]{:S(2)}) async-start(), calls=%async_computation.9 | async-start | bytes 7077888 | tf_op jit(solution)/shard_map/reduce_scatter | solution.py:156
  614.1 7.0 copy-start.79
  614.1 7.0 copy-start.81
  652.8 8.7 copy-start.78
  668.8 111.6 %all-gather.11.cloned.1.call-start = ((), (), s32[]{:S(2)}) async-start(), calls=%async_computation.10 | async-start | bytes 3538944 | tf_op jit(solution)/shard_map/all_gather | solution.py:165
  743.6 602.2 %reduce-scatter.11.cloned.1.call-start = ((), (), s32[]{:S(2)}) async-start(), calls=%async_computation.11 | async-start | bytes 3538944 | tf_op jit(solution)/shard_map/reduce_scatter | solution.py:184
  837.4 5.7 copy-start.38
  837.4 5.7 copy-start.42
  1269.6 6.1 copy-start.1
  1269.6 6.1 copy-start.3
  1269.6 6.1 copy-start.5
  1269.6 6.1 copy-start.27
  1269.6 6.1 copy-start.28
  1269.6 6.1 copy-start.29
  1269.6 6.1 copy-start.54
  1269.6 6.1 copy-start.56
  1269.7 6.1 copy-start.58
  1269.7 6.1 copy-start.60
  1269.7 6.1 copy-start.62
  1269.7 6.1 copy-start.64
  1269.7 6.1 copy-start.66
  1269.7 6.1 copy-start.68
  1269.7 6.1 copy-start.70
  1275.6 5.8 copy-start.11
  1289.3 99.2 %reduce-scatter.7.cloned.1.call-start = ((), (), s32[]{:S(2)}) async-start(), calls=%async_computation.7 | async-start | bytes 3538944 | tf_op jit(solution)/shard_map/reduce_scatter | solution.py:145
  1294.6 568.9 %all-reduce.103.cloned.1.call-start = ((), (), s32[]{:S(2)}) async-start(), calls=%async_computation.12 | async-start | bytes 54788096 | tf_op jit(solution)/shard_map/psum | solution.py:196
  1294.7 7.8 copy-start.82
  1294.7 7.8 copy-start.84
  1307.3 5.6 copy-start.12
  1307.4 6.6 copy-start.7
  1322.1 23.7 %copy-start.52 = (f32[2048]{0:T(1024)S(1)}, f32[2048]{0:T(1024)}, u32[]{:S(2)}) copy-start(f32[2048]{0:T(1024)} %param.20) | copy-start | bytes 24580
  1863.5 7.4 copy-start.50
  1863.5 10.3 slice-start.7
  1867.2 6.6 slice-start.8
  1873.9 7.6 slice-start.3
  (40 other events, 101.4 us)
Sparse Core Ops, SparseCore 0:
  11.8 40.9 all-gather.4
  505.2 68.6 reduce-scatter.4
  577.5 36.6 all-gather.6
  615.6 37.1 all-gather.8
  668.9 68.6 reduce-scatter.8
  743.7 36.6 all-gather.10
  1289.4 39.1 reduce-scatter.10
  1330.9 39.8 reduce-scatter.6
  1377.2 486.2 all-reduce.102
where the time goes:
time: 1900 us; the launch traced here: 1890 us
  local copies, waits for them, and re-layouts  826 us (43%)
  waiting for transfers between devices  748 us (39%)
  other arithmetic  156 us (8%)
  matrix products  88.7 us (5%)
  blocking collectives  56.8 us (3%)
    psum x1, waiting for transfers between devices, local(): lax.psum((branch_gate_grad, branch_input_grad, conv_weight_grad, conv_bia...  472 us
    pad x73, local copies, waits for them, and re-layouts, gated_recurrence(): return lax.associative_scan(combine_steps, (carry, drive), axis=0)[1]  420 us
    slice x69, local copies, waits for them, and re-layouts, gated_recurrence(): return lax.associative_scan(combine_steps, (carry, drive), axis=0)[1]  364 us
    reduce_scatter x1, waiting for transfers between devices, local(): lax.psum_scatter(product(mixed, block_out), 'mp', scatter_dimension=0, ti...  68.8 us
    reduce_scatter x1, waiting for transfers between devices, local(): lax.psum_scatter(times_transposed(gate_low, gate_weight) + times_transpos...  68.8 us
    psum x1, blocking collectives, local(): lax.psum((first_gain_grad, second_gain_grad), ('dp', 'mp'))  39.5 us
  transfers between devices with their start and end apart: 9, of which 7 were waited for; matrix products, arithmetic and copies ran while one was open for 3% of the time, Pallas kernels for 0%

commit v1 on v0

v1 whole, which is shorter than its diff:
```python
import jax
import jax.numpy as jnp
from jax import lax
from jax.experimental import pallas as pl
from jax.experimental.pallas import tpu as pltpu
from jax.sharding import PartitionSpec as P

EPS = 1e-06
DECAY_SCALE = 8.0
GELU_RATE = 0.7978845608028654
GELU_CUBE = 0.044715
CHUNK = 48
SUB = 8
LOW = jnp.bfloat16
WIDE = jnp.float32


def times(left, right):
    return jnp.dot(left, right, preferred_element_type=WIDE)


def times_transposed(left, right):
    return lax.dot_general(left, right, (((1,), (1,)), ((), ())), preferred_element_type=WIDE)


def transposed_times(left, right):
    return lax.dot_general(left, right, (((0,), (0,)), ((), ())), preferred_element_type=WIDE)


def gelu(v):
    return 0.5 * v * (1.0 + jnp.tanh(GELU_RATE * (v + GELU_CUBE * v * v * v)))


def gelu_pair(v):
    square = v * v
    bend = jnp.tanh(GELU_RATE * v * (1.0 + GELU_CUBE * square))
    half = 0.5 * (1.0 + bend)
    slope = half + 0.5 * v * (1.0 - bend * bend) * (GELU_RATE + 3.0 * GELU_RATE * GELU_CUBE * square)
    return v * half, slope


def norm_scale(values):
    return lax.rsqrt(jnp.mean(values * values, axis=-1, keepdims=True) + EPS)


def norm_back(values, scale, gain, grad):
    unit = values * scale
    lifted = gain * grad
    back = scale * (lifted - unit * jnp.mean(lifted * unit, axis=-1, keepdims=True))
    return back, jnp.sum(grad * unit, axis=0)


def one_minus_exp(y):
    series = 1.0 - y * (1.0 / 9.0)
    for order in range(8, 1, -1):
        series = 1.0 - y * (1.0 / order) * series
    return jnp.where(y < 0.5, y * series, 1.0 - jnp.exp(-y))


def row_positions(lengths_ref, base, rows, width):
    places = base + lax.broadcasted_iota(jnp.int32, (rows, width), 0)
    first = jnp.zeros_like(places)
    start = jnp.int32(0)
    for at in range(lengths_ref.shape[1] - 1):
        start = start + lengths_ref[0, at]
        first = jnp.where(places >= start, start, first)
    return places - first


def gates(rate, inlet, soft, fresh):
    log_a = -rate * soft
    carry = jnp.where(fresh, 0.0, jnp.exp(log_a))
    scale = jnp.where(fresh, 1.0, jnp.sqrt(one_minus_exp(-2.0 * log_a)))
    return carry, scale


def forward_kernel(
    lengths_ref, gate_ref, input_ref, taps_ref, rate_w_ref, inlet_w_ref, extra_ref,
    mixed_ref, conv_ref, rate_ref, inlet_ref, state_ref, padded_ref,
):
    count, width = input_ref.shape
    padded_ref[pl.ds(0, SUB), :] = jnp.zeros((SUB, width), WIDE)
    padded_ref[pl.ds(SUB, count), :] = input_ref[...]
    state_ref[pl.ds(0, SUB), :] = jnp.zeros((SUB, width), WIDE)
    taps = taps_ref[...]
    bias, rate_b, inlet_b, soft = (extra_ref[k : k + 1, :] for k in range(4))
    lanes = lax.broadcasted_iota(jnp.int32, (CHUNK, width), 0) % SUB

    def step(at, before):
        base = pl.multiple_of(at * CHUNK, SUB)
        pos = row_positions(lengths_ref, base, CHUNK, width)
        window = padded_ref[pl.ds(base, CHUNK + SUB), :]
        total = bias + taps[0:1] * window[SUB:]
        for k in range(1, taps.shape[0]):
            moved = window[SUB - k : SUB - k + CHUNK]
            total = total + jnp.where(pos >= k, taps[k : k + 1] * moved, 0.0)
        low = total.astype(LOW)
        conv_ref[pl.ds(base, CHUNK), :] = low
        rate = jax.nn.sigmoid(times(low, rate_w_ref[...]) + rate_b)
        inlet = jax.nn.sigmoid(times(low, inlet_w_ref[...]) + inlet_b)
        rate_ref[pl.ds(base, CHUNK), :] = rate
        inlet_ref[pl.ds(base, CHUNK), :] = inlet
        a, scale = gates(rate, inlet, soft, pos == 0)
        b = scale * inlet * low.astype(WIDE)
        for k in (1, 2, 4):
            inside = lanes >= k
            b = b + jnp.where(inside, a * pltpu.roll(b, k, 0), 0.0)
            a = jnp.where(inside, a * pltpu.roll(a, k, 0), a)
        tiles = []
        for j in range(CHUNK // SUB):
            part = slice(j * SUB, (j + 1) * SUB)
            tile = a[part] * before + b[part]
            before = tile[SUB - 1 : SUB]
            tiles.append(tile)
        state = jnp.concatenate(tiles, axis=0)
        state_ref[pl.ds(base + SUB, CHUNK), :] = state
        mixed_ref[pl.ds(base, CHUNK), :] = (state * gelu(gate_ref[pl.ds(base, CHUNK), :])).astype(LOW)
        return before

    lax.fori_loop(0, count // CHUNK, step, jnp.zeros((1, width), WIDE))


def backward_kernel(
    lengths_ref, grad_ref, gate_ref, input_ref, conv_ref, rate_ref, inlet_ref, state_ref,
    taps_ref, rate_w_ref, inlet_w_ref, extra_ref,
    gate_back_ref, input_back_ref, rate_w_grad_ref, inlet_w_grad_ref, small_ref,
    padded_ref, rate_low_ref, inlet_low_ref,
):
    count, width = input_ref.shape
    padded_ref[pl.ds(0, SUB), :] = jnp.zeros((SUB, width), WIDE)
    padded_ref[pl.ds(SUB, count), :] = input_ref[...]
    taps = taps_ref[...]
    soft = extra_ref[3:4, :]
    slope = extra_ref[4:5, :]
    lanes = lax.broadcasted_iota(jnp.int32, (CHUNK, width), 0) % SUB
    steps = count // CHUNK
    zero = jnp.zeros((1, width), WIDE)

    def column(values):
        return jnp.sum(values, axis=0, keepdims=True)

    def step(turn, held):
        after, late, beyond, sums = held
        base = pl.multiple_of((steps - 1 - turn) * CHUNK, SUB)
        here = pl.ds(base, CHUNK)
        wide_pos = row_positions(lengths_ref, base, CHUNK + SUB, width)
        pos = wide_pos[:CHUNK]
        fresh = pos == 0
        grad = grad_ref[here, :]
        value, bend = gelu_pair(gate_ref[here, :])
        window = state_ref[pl.ds(base, CHUNK + SUB), :]
        state = window[SUB:]
        earlier = window[SUB - 1 : SUB - 1 + CHUNK]
        gate_back_ref[here, :] = (grad * state * bend).astype(LOW)
        rate = rate_ref[here, :]
        inlet = inlet_ref[here, :]
        conv = conv_ref[here, :]
        conv_wide = conv.astype(WIDE)
        carry, scale = gates(rate, inlet, soft, fresh)
        b = grad * value
        a = jnp.concatenate([carry[1:], late], axis=0)
        for k in (1, 2, 4):
            inside = lanes < SUB - k
            b = b + jnp.where(inside, a * pltpu.roll(b, CHUNK - k, 0), 0.0)
            a = jnp.where(inside, a * pltpu.roll(a, CHUNK - k, 0), a)
        tiles = []
        for j in reversed(range(CHUNK // SUB)):
            part = slice(j * SUB, (j + 1) * SUB)
            tile = a[part] * after + b[part]
            after = tile[0:1]
            tiles.append(tile)
        total = jnp.concatenate(tiles[::-1], axis=0)
        late = carry[0:1]
        scaled = total * scale
        d_inlet = scaled * conv_wide
        d_scale = total * inlet * conv_wide
        d_log = jnp.where(fresh, 0.0, total * earlier * carry - d_scale * (carry * carry) / scale)
        leak = rate * d_log
        rate_low = (-soft * leak * (1.0 - rate)).astype(LOW)
        inlet_low = (d_inlet * inlet * (1.0 - inlet)).astype(LOW)
        rate_low_ref[here, :] = rate_low
        inlet_low_ref[here, :] = inlet_low
        spread = (
            scaled * inlet
            + times_transposed(rate_low, rate_w_ref[...])
            + times_transposed(inlet_low, inlet_w_ref[...])
        )
        ahead = jnp.concatenate([spread, beyond], axis=0)
        back = taps[0:1] * spread
        source = padded_ref[pl.ds(base, CHUNK + SUB), :]
        new = [column(spread), column(rate_low.astype(WIDE)), column(inlet_low.astype(WIDE)), column(leak)]
        new.append(column(spread * source[SUB:]))
        for k in range(1, taps.shape[0]):
            kept = jnp.where(wide_pos >= k, ahead, 0.0)
            back = back + taps[k : k + 1] * kept[k : k + CHUNK]
            new.append(column(kept[:CHUNK] * source[SUB - k : SUB - k + CHUNK]))
        input_back_ref[here, :] = back.astype(LOW)
        return after, late, spread[:SUB], tuple(x + y for x, y in zip(sums, new))

    start = tuple(zero for _ in range(4 + taps.shape[0]))
    sums = lax.fori_loop(0, steps, step, (zero, zero, jnp.zeros((SUB, width), WIDE), start))[3]
    rows = list(sums)
    rows[3] = -slope * rows[3]
    small_ref[...] = jnp.concatenate(rows, axis=0)
    rate_w_grad_ref[...] = transposed_times(conv_ref[...], rate_low_ref[...])
    inlet_w_grad_ref[...] = transposed_times(conv_ref[...], inlet_low_ref[...])


def in_vmem():
    return pl.BlockSpec(memory_space=pltpu.VMEM)


def run_kernel(body, outs, scratch, operands, cost):
    return pl.pallas_call(
        body,
        in_specs=[pl.BlockSpec(memory_space=pltpu.SMEM)] + [in_vmem()] * (len(operands) - 1),
        out_specs=[in_vmem()] * len(outs),
        out_shape=outs,
        scratch_shapes=scratch,
        compiler_params=pltpu.CompilerParams(vmem_limit_bytes=48 * 1024 * 1024),
        cost_estimate=cost,
    )(*operands)


def forward_mix(lengths, gate_pre, input_pre, taps, rate_w, inlet_w, extra):
    count, width = input_pre.shape
    wide = jax.ShapeDtypeStruct((count, width), WIDE)
    low = jax.ShapeDtypeStruct((count, width), LOW)
    state = jax.ShapeDtypeStruct((count + SUB, width), WIDE)
    cost = pl.CostEstimate(
        flops=60 * count * width + 4 * count * width * width,
        bytes_accessed=26 * count * width,
        transcendentals=5 * count * width,
    )
    return run_kernel(
        forward_kernel,
        [low, low, wide, wide, state],
        [pltpu.VMEM((count + SUB, width), WIDE)],
        (lengths, gate_pre, input_pre, taps, rate_w, inlet_w, extra),
        cost,
    )


def backward_mix(lengths, grad, gate_pre, input_pre, conv, rate, inlet, state, taps, rate_w, inlet_w, extra):
    count, width = input_pre.shape
    low = jax.ShapeDtypeStruct((count, width), LOW)
    square = jax.ShapeDtypeStruct((width, width), WIDE)
    small = jax.ShapeDtypeStruct((4 + taps.shape[0], width), WIDE)
    cost = pl.CostEstimate(
        flops=150 * count * width + 8 * count * width * width,
        bytes_accessed=30 * count * width,
        transcendentals=5 * count * width,
    )
    padded = pltpu.VMEM((count + SUB, width), WIDE)
    narrow = pltpu.VMEM((count, width), LOW)
    return run_kernel(
        backward_kernel,
        [low, low, square, square, small],
        [padded, narrow, narrow],
        (lengths, grad, gate_pre, input_pre, conv, rate, inlet, state, taps, rate_w, inlet_w, extra),
        cost,
    )


def spread_blocks(weights):
    heads, size, _ = weights.shape
    full = jnp.zeros((heads, size, heads, size), weights.dtype)
    for h in range(heads):
        full = full.at[h, :, h, :].set(weights[h])
    return full.reshape(heads * size, heads * size)


def pick_blocks(full, heads):
    size = full.shape[0] // heads
    return jnp.stack([full[h * size : (h + 1) * size, h * size : (h + 1) * size] for h in range(heads)])


def sum_rows(values):
    return lax.psum_scatter(values.astype(LOW), "mp", scatter_dimension=0, tiled=True).astype(WIDE)


def all_rows(values):
    return lax.all_gather(values, "mp", axis=0, tiled=True)


def sum_buckets(values):
    return lax.psum(values.astype(LOW), "dp").astype(WIDE)


def local(
    tokens,
    lengths,
    first_gain,
    branch_gate,
    branch_input,
    conv_weight,
    conv_bias,
    rate_weight,
    rate_bias,
    inlet_weight,
    inlet_bias,
    decay_param,
    block_out,
    second_gain,
    gate_weight,
    up_weight,
    down_weight,
    out_grad,
):
    heads = rate_weight.shape[0]
    width = decay_param.shape[0]
    features = tokens.shape[1]
    taps_count = conv_weight.shape[0]
    own_input = tokens.astype(WIDE)
    own_grad = out_grad.astype(WIDE)
    first_scale = norm_scale(own_input)
    first_rows = all_rows((own_input * first_scale * first_gain).astype(LOW))
    grad_rows = all_rows(out_grad)
    soft = DECAY_SCALE * jax.nn.softplus(decay_param)
    slope = DECAY_SCALE * jax.nn.sigmoid(decay_param)
    extra = jnp.stack([conv_bias, rate_bias, inlet_bias, soft, slope])
    rate_w = spread_blocks(rate_weight)
    inlet_w = spread_blocks(inlet_weight)

    gate_pre = times(first_rows, branch_gate)
    input_pre = times(first_rows, branch_input)
    mixed, conv, rate, inlet, state = forward_mix(
        lengths, gate_pre, input_pre, conv_weight, rate_w, inlet_w, extra
    )
    own_middle = own_input + sum_rows(times(mixed, block_out))
    second_scale = norm_scale(own_middle)
    second_rows = all_rows((own_middle * second_scale * second_gain).astype(LOW))
    d_hidden = times_transposed(grad_rows, down_weight)
    gate_act = times(second_rows, gate_weight)
    up_act = times(second_rows, up_weight)
    value, bend = gelu_pair(gate_act)
    hidden = (value * up_act).astype(LOW)
    gate_low = (d_hidden * up_act * bend).astype(LOW)
    up_low = (d_hidden * value).astype(LOW)
    second_input = sum_rows(times_transposed(gate_low, gate_weight) + times_transposed(up_low, up_weight))
    down_grad = transposed_times(hidden, grad_rows)
    gate_grad = transposed_times(second_rows, gate_low)
    up_grad = transposed_times(second_rows, up_low)
    part, second_gain_grad = norm_back(own_middle, second_scale, second_gain, second_input)
    middle_grad = own_grad + part
    middle_rows = all_rows(middle_grad.astype(LOW))
    d_mixed = times_transposed(middle_rows, block_out)
    block_grad = transposed_times(mixed, middle_rows)
    output = (own_middle + sum_rows(times(hidden, down_weight))).astype(LOW)
    gate_back, input_back, rate_w_grad, inlet_w_grad, small = backward_mix(
        lengths, d_mixed, gate_pre, input_pre, conv, rate, inlet, state, conv_weight, rate_w, inlet_w, extra
    )
    first_input = sum_rows(times_transposed(gate_back, branch_gate) + times_transposed(input_back, branch_input))
    branch_gate_grad = transposed_times(gate_back, first_rows)
    branch_input_grad = transposed_times(input_back, first_rows)
    part, first_gain_grad = norm_back(own_input, first_scale, first_gain, first_input)
    input_grad = middle_grad + part

    gains = lax.psum(jnp.stack([first_gain_grad, second_gain_grad]), ("dp", "mp"))
    mlp = sum_buckets(jnp.concatenate([down_grad.reshape(-1, features), gate_grad.reshape(-1, features), up_grad.reshape(-1, features)]))
    square = jnp.stack([pick_blocks(rate_w_grad, heads), pick_blocks(inlet_w_grad, heads)])
    flat = jnp.concatenate([square.reshape(-1), small.reshape(-1)])
    flat = jnp.pad(flat, (0, -flat.shape[0] % (16 * features))).reshape(-1, features)
    rec = sum_buckets(jnp.concatenate([block_grad, branch_gate_grad, branch_input_grad, flat]))
    hidden_count = down_weight.shape[0]
    down_grad = mlp[:hidden_count]
    gate_grad = mlp[hidden_count : 2 * hidden_count].reshape(features, -1)
    up_grad = mlp[2 * hidden_count :].reshape(features, -1)
    flat = rec[3 * width :].reshape(-1)
    square = flat[: square.size].reshape(square.shape)
    small = flat[square.size : square.size + small.size].reshape(small.shape)
    return (
        output,
        input_grad,
        gains[0],
        rec[width : 2 * width].T,
        rec[2 * width : 3 * width].T,
        small[4 : 4 + taps_count],
        small[0],
        square[0],
        small[1],
        square[1],
        small[2],
        small[3],
        rec[:width],
        gains[1],
        gate_grad,
        up_grad,
        down_grad,
    )


def solution(mesh):
    rows = P(("dp", "mp"), None)
    out_columns = P(None, "mp")
    out_rows = P("mp", None)
    blocks = P("mp", None, None)
    vector = P("mp")
    in_specs = (
        rows, P("dp", None), P(), out_columns, out_columns, out_columns, vector, blocks, vector, blocks,
        vector, vector, out_rows, P(), out_columns, out_columns, out_rows, rows,
    )
    out_specs = (
        rows, rows, P(), out_columns, out_columns, out_columns, vector, blocks, vector, blocks,
        vector, vector, out_rows, P(), out_columns, out_columns, out_rows,
    )
    return jax.shard_map(local, mesh=mesh, in_specs=in_specs, out_specs=out_specs, check_vma=False)
```

time: 1900 us -> 708 us (0.37)
  local copies, waits for them, and re-layouts: 826 us -> 65.6 us
  waiting for transfers between devices: 748 us -> 461 us
  other arithmetic: 156 us -> 23.6 us
  Pallas kernels: 0 us -> 22.9 us
    pad x73 -> x0, local copies, waits for them, and re-layouts: 420 us -> none  [gated_recurrence(): return lax.associative_scan(combine_steps, (carry, drive), axis=0)[1]]
    slice x70 -> x7, local copies, waits for them, and re-layouts: 365 us -> 15.8 us  [the longest x1 9.31 us: local(): down_grad = mlp[:hidden_count]]
    psum x1, waiting for transfers between devices: 472 us -> 252 us  [sum_buckets(): return lax.psum(values.astype(LOW), 'dp').astype(WIDE)]
    reduce_scatter x4, waiting for transfers between devices: 138 us -> 78.6 us  [sum_rows(): lax.psum_scatter(values.astype(LOW), 'mp', scatter_dimension=0, tiled=True)]
    mul x21 -> x1, other arithmetic: 41.9 us -> 0.69 us  [local(): slope = DECAY_SCALE * jax.nn.sigmoid(decay_param)]
    add_any x18 -> x0, other arithmetic: 28.8 us -> none  [the longest x8 18.3 us: combine_steps(): return (early[0] * late[0], late[0] * early[1] + late[1])]
    reshape x4 -> x9, local copies, waits for them, and re-layouts: 2.74 us -> 28.6 us  [the longest x1 7.82 us: local(): gate_grad = mlp[hidden_count:2 * hidden_count].reshape(features, -1)]
    add x21 -> x1, other arithmetic: 28.5 us -> 2.72 us  [local(): input_grad = middle_grad + part]
  transfers between devices with their start and end apart: 9 -> 9, of which waited for: 7 -> 7; matrix products, arithmetic and copies ran while one was open for 3% -> 10% of each run, Pallas kernels for 0% -> 0%
where the time goes in v1:
time: 708 us; the launch traced here: 702 us
  waiting for transfers between devices  461 us (65%)
  matrix products  71.8 us (10%)
  local copies, waits for them, and re-layouts  65.6 us (9%)
  blocking collectives  41.4 us (6%)
  other arithmetic  23.6 us (3%)
  Pallas kernels  22.9 us (3%)
  between operations  14.7 us (2%)
    psum x1, waiting for transfers between devices, sum_buckets(): return lax.psum(values.astype(LOW), 'dp').astype(WIDE)  252 us
    all_gather x4, waiting for transfers between devices, all_rows(): return lax.all_gather(values, 'mp', axis=0, tiled=True)  129 us
    reduce_scatter x4, waiting for transfers between devices, sum_rows(): lax.psum_scatter(values.astype(LOW), 'mp', scatter_dimension=0, tiled=True)  78.6 us
    psum x1, blocking collectives, local(): lax.psum(jnp.stack([first_gain_grad, second_gain_grad]), ('dp', 'mp'))  41.4 us
    dot_general x6, matrix products, times(): return jnp.dot(left, right, preferred_element_type=WIDE)  26.7 us
    dot_general x6, matrix products, times_transposed(): lax.dot_general(left, right, (((1,), (1,)), ((), ())), preferred_element_...  24.4 us
    pallas_call x2, Pallas kernels, run_kernel(): pl.pallas_call(body, in_specs=[pl.BlockSpec(memory_space=pltpu.SMEM)] + [...  22.9 us
    dot_general x6, matrix products, transposed_times(): lax.dot_general(left, right, (((0,), (0,)), ((), ())), preferred_element_...  20.7 us
  transfers between devices with their start and end apart: 9, of which 7 were waited for; matrix products, arithmetic and copies ran while one was open for 10% of the time, Pallas kernels for 0%

profile of v1, /device:TPU:0, one launch (start us, length us, event | category | flops | bytes accessed | tf_op | source)
XLA Modules:
  0.0 701.8 jit_solution(9933894860621636231)
XLA Ops:
  7.3 1.3 fusion.17
  9.1 1.9 fusion.14
  11.1 1.2 stack.63
  12.4 1.2 stack.64
  13.6 1.2 stack.65
  16.7 0.9 slice_bitcast_fusion.7
  17.6 0.9 bitcast_dynamic-update-slice_fusion
  18.5 1.1 copy.36
  19.6 1.2 reshape.272.inlet_w_ref
  20.8 1.1 copy.35
  21.9 1.9 reshape.269.rate_w_ref
  24.6 27.6 %all-gather.5.cloned.1.call-done = bf16[768,2048]{1,0:T(8,128)(2,1)} async-done(((bf16[96,2048]{1,0:T(8,128)(2,1)}), bf16[768,2048]{1,0:T(8,128)(2,1)}) %all-gather.5.cloned.1.call-update) | async-done | bytes 3145744 | tf_op jit(solution)/shard_map/all_gather | solution.py:283
  52.2 5.2 fusion.29.input_ref
  57.5 1.8 fusion.28.gate_ref
  59.3 9.9 %shard_map.305 = (bf16[768,320]{1,0:T(8,128)(2,1)S(1)}, bf16[768,320]{1,0:T(8,128)(2,1)S(1)}, f32[768,320]{1,0:T(8,128)S(1)}, f32[768,320]{1,0:T(8,128)S(1)}, f32[776,320]{1,0:T(8,128)}) custom-call(s32[1,3]{1,0:T(1,128)S(1)} %copy-done.19, f32[768,320]{1,0:T(8,128)S(1)} %fusion.28.gate_ref, f32[768,320]{1,0:T(8,128)} %fusion.29.input_ref, ...), custom_call_target="tpu_custom_call" | custom-call | flops 329318400 | bytes 6389760 | tf_op jit(solution)/shard_map/pallas_call | solution.py:214
  69.3 1.0 copy-done.2
  70.3 1.0 copy-done.6
  71.3 1.1 copy-done.7
  72.4 0.8 copy-done.8
  73.2 0.8 copy-done.20
  74.0 3.5 convolution_convert_fusion.4
  77.6 39.3 %reduce-scatter.5.cloned.1.call-done = bf16[96,2048]{1,0:T(8,128)(2,1)} async-done(((bf16[768,2048]{1,0:T(8,128)(2,1)}), bf16[96,2048]{1,0:T(8,128)(2,1)}) %reduce-scatter.5.cloned.1.call-update) | async-done | bytes 393232 | tf_op jit(solution)/shard_map/reduce_scatter | solution.py:279
  116.9 1.3 multiply_reduce_fusion
  118.3 2.0 multiply_convert_fusion.3
  121.1 36.6 %all-gather.7.cloned.1.call-done = bf16[768,2048]{1,0:T(8,128)(2,1)} async-done(((bf16[96,2048]{1,0:T(8,128)(2,1)}), bf16[768,2048]{1,0:T(8,128)(2,1)}) %all-gather.7.cloned.1.call-update) | async-done | bytes 3145744 | tf_op jit(solution)/shard_map/all_gather | solution.py:283
  157.8 7.0 fusion.31
  164.8 4.0 fusion.30
  168.8 27.7 %all-gather.9.cloned.1.call-done = bf16[768,2048]{1,0:T(8,128)(2,1)} async-done(((bf16[96,2048]{1,0:T(8,128)(2,1)}), bf16[768,2048]{1,0:T(8,128)(2,1)}) %all-gather.9.cloned.1.call-update) | async-done | bytes 3145744 | tf_op jit(solution)/shard_map/all_gather | solution.py:283
  196.4 8.4 %multiply_convert_fusion = (bf16[768,768]{1,0:T(8,128)(2,1)S(1)}, bf16[768,768]{1,0:T(8,128)(2,1)S(1)}, bf16[768,768]{1,0:T(8,128)(2,1)}) fusion(f32[768,768]{1,0:T(8,128)} %fusion.30, f32[768,768]{1,0:T(8,128)} %fusion.31, bf16[768,2048]{1,0:T(8,128)(2,1)} %all-gather.9.cloned.1.call-done, bf16[768,2048]{1,0:T(8,128)(2,1)S(1)} %copy-done), kind=kOutput, calls=%fused_computation.14 | convolution fusion | flops 2429485056 | bytes 14548992 | tf_op jit(solution)/shard_map/dot_general | solution.py:23
  204.8 2.6 fusion.32
  207.6 4.0 add_convert_fusion.1
  211.6 39.3 %reduce-scatter.9.cloned.1.call-done = bf16[96,2048]{1,0:T(8,128)(2,1)} async-done(((bf16[768,2048]{1,0:T(8,128)(2,1)}), bf16[96,2048]{1,0:T(8,128)(2,1)}) %reduce-scatter.9.cloned.1.call-update) | async-done | bytes 393232 | tf_op jit(solution)/shard_map/reduce_scatter | solution.py:279
  250.9 1.7 fusion.13
  252.6 2.5 fusion.23
  255.3 37.3 %all-gather.11.cloned.1.call-done = bf16[768,2048]{1,0:T(8,128)(2,1)} async-done(((bf16[96,2048]{1,0:T(8,128)(2,1)}), bf16[768,2048]{1,0:T(8,128)(2,1)}) %all-gather.11.cloned.1.call-update) | async-done | bytes 3145744 | tf_op jit(solution)/shard_map/all_gather | solution.py:283
  292.6 4.2 fusion.33.grad_ref
  296.9 13.0 %shard_map.306 = (bf16[768,320]{1,0:T(8,128)(2,1)S(1)}, bf16[768,320]{1,0:T(8,128)(2,1)S(1)}, f32[320,320]{1,0:T(8,128)S(1)}, f32[320,320]{1,0:T(8,128)S(1)}, f32[8,320]{1,0:T(8,128)S(1)}) custom-call(s32[1,3]{1,0:T(1,128)S(1)} %copy-done.19, f32[768,320]{1,0:T(8,128)S(1)} %fusion.33.grad_ref, f32[768,320]{1,0:T(8,128)S(1)} %copy-done.3, ...), custom_call_target="tpu_custom_call" | custom-call | flops 666009600 | bytes 7372800 | tf_op jit(solution)/shard_map/pallas_call | solution.py:214
  310.0 1.8 fusion.34
  312.0 3.5 add_convert_fusion
  315.5 5.2 convolution_convert_fusion.3
  320.8 4.9 convolution_convert_fusion.1
  325.7 4.9 reshape.277
  330.6 4.9 convolution_convert_fusion
  335.6 4.4 reshape.278
  340.0 5.1 convolution_convert_fusion.2
  345.1 4.5 pad_maximum_fusion
  350.9 3.3 convolution_convert_fusion.7
  354.2 1.2 convolution_convert_fusion.6
  355.5 1.2 convolution_convert_fusion.5
  356.7 2.3 pad_maximum_fusion.1
  359.0 0.9 copy-done.22
  360.0 1.4 fusion.16
  361.4 41.4 %psum.21 = f32[2,2048]{1,0:T(2,128)S(1)} all-reduce(f32[2,2048]{1,0:T(2,128)S(1)} %pad_maximum_fusion.3), channel_id=1, replica_groups=mesh['dp'=4,'mp'=8] {'dp','mp'}, use_global_device_ids=true, to_apply=%region_10.11 | all-reduce | flops 4096 | bytes 32768 | tf_op jit(solution)/shard_map/psum | solution.py:359
  403.4 2.7 fusion.9
  406.2 252.5 %all-reduce.6.cloned.1.call-done = (bf16[1024,2048]{1,0:T(8,128)(2,1)}, bf16[2304,2048]{1,0:T(8,128)(2,1)}) async-done(((bf16[1024,2048]{1,0:T(8,128)(2,1)}, bf16[2304,2048]{1,0:T(8,128)(2,1)}), (bf16[1024,2048]{1,0:T(8,128)(2,1)}, bf16[2304,2048]{1,0:T(8,128)(2,1)})) %all-reduce.6.cloned.1.call-update) | async-done | bytes 13631504 | tf_op jit(solution)/shard_map/psum | solution.py:287
  658.6 1.2 fusion.25
  659.8 3.3 slice.244
  663.1 1.1 convert_element_type.78
  664.3 2.7 slice_bitcast_fusion
  667.7 0.9 squeeze.10
  668.7 0.9 squeeze.9
  670.3 9.3 %fusion.24 = (f32[768,2048]{1,0:T(8,128)}, f32[768,2048]{1,0:T(8,128)}, f32[768,2048]{1,0:T(8,128)}) fusion(bf16[2304,2048]{1,0:T(8,128)(2,1)} %get-tuple-element.90), kind=kLoop, calls=%fused_computation.72 | loop fusion | bytes 37748736 | tf_op jit(solution)/shard_map/slice | solution.py:366
  679.6 7.7 %reshape.280 = f32[2048,768]{1,0:T(8,128)} reshape(f32[768,2048]{1,0:T(8,128)} %get-tuple-element.92) | data formatting | bytes 12582912 | tf_op jit(solution)/shard_map/reshape | solution.py:368
  687.3 7.8 %reshape.279 = f32[2048,768]{1,0:T(8,128)} reshape(f32[768,2048]{1,0:T(8,128)} %get-tuple-element.93) | data formatting | bytes 12582912 | tf_op jit(solution)/shard_map/reshape | solution.py:367
  (136 shorter events, 8.3 us)
Async XLA Ops:
  7.2 189.2 %copy-start = (bf16[768,2048]{1,0:T(8,128)(2,1)S(1)}, bf16[768,2048]{1,0:T(8,128)(2,1)}, u32[]{:S(2)}) copy-start(bf16[768,2048]{1,0:T(8,128)(2,1)} %param.42) | copy-start | bytes 9437188
  7.2 13.6 %copy-start.32 = (bf16[2,160,160]{2,1,0:T(8,128)(2,1)S(1)}, bf16[2,160,160]{2,1,0:T(8,128)(2,1)}, u32[]{:S(2)}) copy-start(bf16[2,160,160]{2,1,0:T(8,128)(2,1)} %param.33) | copy-start | bytes 307204
  7.2 45.0 %all-gather.5.cloned.1.call-start = ((), (), s32[]{:S(2)}) async-start(), calls=%async_computation.4 | async-start | bytes 3538944 | tf_op jit(solution)/shard_map/all_gather | solution.py:283
  8.6 0.5 copy-start.35
  11.1 105.8 %reduce-scatter.5.cloned.1.call-start = ((), (), s32[]{:S(2)}) async-start(), calls=%async_computation.5 | async-start | bytes 3538944 | tf_op jit(solution)/shard_map/reduce_scatter | solution.py:279
  52.2 5.2 copy-start.29
  52.2 5.2 copy-start.40
  57.4 1.9 copy-start.4
  57.5 1.9 copy-start.18
  57.5 1.9 copy-start.19
  57.5 16.6 %copy-start.43 = (bf16[320,2048]{1,0:T(8,128)(2,1)S(1)}, bf16[320,2048]{1,0:T(8,128)(2,1)}, u32[]{:S(2)}) copy-start(bf16[320,2048]{1,0:T(8,128)(2,1)} %param.38) | copy-start | bytes 3932164
  69.2 1.0 copy-start.2
  70.3 1.0 copy-start.6
  71.3 1.1 copy-start.7
  72.4 0.8 copy-start.8
  73.2 0.8 copy-start.20
  77.5 40.8 %copy-start.33 = (f32[2048]{0:T(1024)S(1)}, f32[2048]{0:T(1024)}, u32[]{:S(2)}) copy-start(f32[2048]{0:T(1024)} %param.39) | copy-start | bytes 24580
  77.5 80.2 %all-gather.7.cloned.1.call-start = ((), (), s32[]{:S(2)}) async-start(), calls=%async_computation.6 | async-start | bytes 3538944 | tf_op jit(solution)/shard_map/all_gather | solution.py:283
  120.3 76.1 %all-gather.9.cloned.1.call-start = ((), (), s32[]{:S(2)}) async-start(), calls=%async_computation.8 | async-start | bytes 3538944 | tf_op jit(solution)/shard_map/all_gather | solution.py:283
  120.9 130.0 %reduce-scatter.9.cloned.1.call-start = ((), (), s32[]{:S(2)}) async-start(), calls=%async_computation.9 | async-start | bytes 3538944 | tf_op jit(solution)/shard_map/reduce_scatter | solution.py:279
  157.8 7.0 copy-start.37
  157.8 7.0 copy-start.42
  196.4 8.4 %copy-start.38 = (bf16[2048,768]{1,0:T(8,128)(2,1)S(1)}, bf16[2048,768]{1,0:T(8,128)(2,1)}, u32[]{:S(2)}) copy-start(bf16[2048,768]{1,0:T(8,128)(2,1)} %param.40) | copy-start | bytes 9437188
  204.8 2.7 copy-start.44
  204.8 2.7 copy-start.45
  204.8 2.7 copy-start.39
  211.6 81.0 %all-gather.11.cloned.1.call-start = ((), (), s32[]{:S(2)}) async-start(), calls=%async_computation.10 | async-start | bytes 3538944 | tf_op jit(solution)/shard_map/all_gather | solution.py:283
  255.1 104.0 %reduce-scatter.11.cloned.1.call-start = ((), (), s32[]{:S(2)}) async-start(), calls=%async_computation.11 | async-start | bytes 3538944 | tf_op jit(solution)/shard_map/reduce_scatter | solution.py:279
  292.6 4.2 copy-start.3
  292.6 4.2 copy-start.5
  292.6 4.2 copy-start.9
  296.9 13.1 %copy-start.30 = (bf16[2048,320]{0,1:T(8,128)(2,1)S(1)}, bf16[2048,320]{0,1:T(8,128)(2,1)}, u32[]{:S(2)}) copy-start(bf16[2048,320]{0,1:T(8,128)(2,1)} %param.29) | copy-start | bytes 3932164
  309.9 1.9 copy-start.12
  309.9 1.9 copy-start.14
  309.9 1.9 copy-start.16
  309.9 1.9 copy-start.10
  309.9 2.1 copy-start.31
  315.5 87.9 %reduce-scatter.7.cloned.1.call-start = ((), (), s32[]{:S(2)}) async-start(), calls=%async_computation.7 | async-start | bytes 3538944 | tf_op jit(solution)/shard_map/reduce_scatter | solution.py:279
  320.8 337.8 %all-reduce.6.cloned.1.call-start = ((), (), s32[]{:S(2)}) async-start(), calls=%async_computation.12 | async-start | bytes 27262976 | tf_op jit(solution)/shard_map/psum | solution.py:287
  340.0 5.1 copy-start.24
  340.0 5.1 copy-start.25
  345.1 4.6 copy-start.17
  345.1 4.7 copy-start.15
  349.7 1.2 copy-start.21
  350.9 3.3 copy-start.13
  350.9 3.3 copy-start.41
  354.2 1.2 copy-start.11
  358.9 1.0 copy-start.22
  359.0 1.0 copy-start.34
  359.0 1.0 copy-start.36
  359.0 44.5 %copy-start.26 = (bf16[96,2048]{1,0:T(8,128)(2,1)S(1)}, bf16[96,2048]{1,0:T(8,128)(2,1)}, u32[]{:S(2)}) copy-start(bf16[96,2048]{1,0:T(8,128)(2,1)} %reduce-scatter.5.cloned.1.call-done) | copy-start | bytes 1179652
  359.0 44.5 %copy-start.27 = (bf16[96,2048]{1,0:T(8,128)(2,1)S(1)}, bf16[96,2048]{1,0:T(8,128)(2,1)}, u32[]{:S(2)}) copy-start(bf16[96,2048]{1,0:T(8,128)(2,1)} %param.43) | copy-start | bytes 1179652
  359.0 44.5 %copy-start.28 = (bf16[96,2048]{1,0:T(8,128)(2,1)S(1)}, bf16[96,2048]{1,0:T(8,128)(2,1)}, u32[]{:S(2)}) copy-start(bf16[96,2048]{1,0:T(8,128)(2,1)} %reduce-scatter.9.cloned.1.call-done) | copy-start | bytes 1179652
  658.6 4.5 copy-start.23
  687.3 7.8 %copy-start.1 = (bf16[768,2048]{1,0:T(8,128)(2,1)S(1)}, bf16[768,2048]{1,0:T(8,128)(2,1)}, u32[]{:S(2)}) copy-start(bf16[768,2048]{1,0:T(8,128)(2,1)} %param.42) | copy-start | bytes 9437188
Sparse Core Ops, SparseCore 0:
  11.2 40.9 all-gather.4
  77.6 39.2 reduce-scatter.4
  120.4 37.2 all-gather.6
  159.3 37.1 all-gather.8
  211.7 39.1 reduce-scatter.8
  255.2 37.3 all-gather.10
  315.6 39.2 reduce-scatter.10
  357.7 40.4 reduce-scatter.6
  402.4 256.1 all-reduce.5

commit v2 on v1

--- a/solution.py
+++ b/solution.py
@@ -1,3 +1,5 @@
+import itertools
+
 import jax
 import jax.numpy as jnp
 from jax import lax
@@ -13,6 +15,9 @@
 SUB = 8
 LOW = jnp.bfloat16
 WIDE = jnp.float32
+NO_COST = pl.CostEstimate(flops=0, bytes_accessed=0, transcendentals=0)
+ROWS = 256
+COLUMNS = 512
 
 
 def times(left, right):
@@ -46,8 +51,7 @@
 def norm_back(values, scale, gain, grad):
     unit = values * scale
     lifted = gain * grad
-    back = scale * (lifted - unit * jnp.mean(lifted * unit, axis=-1, keepdims=True))
-    return back, jnp.sum(grad * unit, axis=0)
+    return scale * (lifted - unit * jnp.mean(lifted * unit, axis=-1, keepdims=True))
 
 
 def one_minus_exp(y):
@@ -75,12 +79,12 @@
 
 
 def forward_kernel(
-    lengths_ref, gate_ref, input_ref, taps_ref, rate_w_ref, inlet_w_ref, extra_ref,
+    lengths_ref, both_ref, taps_ref, rate_w_ref, inlet_w_ref, extra_ref,
     mixed_ref, conv_ref, rate_ref, inlet_ref, state_ref, padded_ref,
 ):
-    count, width = input_ref.shape
+    count, width = mixed_ref.shape
     padded_ref[pl.ds(0, SUB), :] = jnp.zeros((SUB, width), WIDE)
-    padded_ref[pl.ds(SUB, count), :] = input_ref[...]
+    padded_ref[pl.ds(SUB, count), :] = both_ref[:, width:]
     state_ref[pl.ds(0, SUB), :] = jnp.zeros((SUB, width), WIDE)
     taps = taps_ref[...]
     bias, rate_b, inlet_b, soft = (extra_ref[k : k + 1, :] for k in range(4))
@@ -114,21 +118,30 @@
             tiles.append(tile)
         state = jnp.concatenate(tiles, axis=0)
         state_ref[pl.ds(base + SUB, CHUNK), :] = state
-        mixed_ref[pl.ds(base, CHUNK), :] = (state * gelu(gate_ref[pl.ds(base, CHUNK), :])).astype(LOW)
+        mixed_ref[pl.ds(base, CHUNK), :] = (state * gelu(both_ref[pl.ds(base, CHUNK), :width])).astype(LOW)
         return before
 
     lax.fori_loop(0, count // CHUNK, step, jnp.zeros((1, width), WIDE))
 
 
 def backward_kernel(
-    lengths_ref, grad_ref, gate_ref, input_ref, conv_ref, rate_ref, inlet_ref, state_ref,
+    heads, lengths_ref, middle_ref, block_ref, first_ref, branches_ref, mixed_ref,
+    both_ref, conv_ref, rate_ref, inlet_ref, state_ref,
     taps_ref, rate_w_ref, inlet_w_ref, extra_ref,
-    gate_back_ref, input_back_ref, rate_w_grad_ref, inlet_w_grad_ref, small_ref,
-    padded_ref, rate_low_ref, inlet_low_ref,
+    partial_ref, block_grad_ref, branch_grad_ref, gain_ref,
+    grad_ref, back_ref, padded_ref, rate_low_ref, inlet_low_ref, stacked_ref,
 ):
-    count, width = input_ref.shape
+    count, width = grad_ref.shape
+    features = middle_ref.shape[1]
+
+    def spread_rows(turn, _):
+        here = pl.ds(pl.multiple_of(turn * ROWS, ROWS), ROWS)
+        grad_ref[here, :] = times_transposed(middle_ref[here, :], block_ref[...])
+        return _
+
+    lax.fori_loop(0, count // ROWS, spread_rows, 0)
     padded_ref[pl.ds(0, SUB), :] = jnp.zeros((SUB, width), WIDE)
-    padded_ref[pl.ds(SUB, count), :] = input_ref[...]
+    padded_ref[pl.ds(SUB, count), :] = both_ref[:, width:]
     taps = taps_ref[...]
     soft = extra_ref[3:4, :]
     slope = extra_ref[4:5, :]
@@ -147,11 +160,11 @@
         pos = wide_pos[:CHUNK]
         fresh = pos == 0
         grad = grad_ref[here, :]
-        value, bend = gelu_pair(gate_ref[here, :])
+        value, bend = gelu_pair(both_ref[here, :width])
         window = state_ref[pl.ds(base, CHUNK + SUB), :]
         state = window[SUB:]
         earlier = window[SUB - 1 : SUB - 1 + CHUNK]
-        gate_back_ref[here, :] = (grad * state * bend).astype(LOW)
+        back_ref[here, :width] = (grad * state * bend).astype(LOW)
         rate = rate_ref[here, :]
         inlet = inlet_ref[here, :]
         conv = conv_ref[here, :]
@@ -194,71 +207,109 @@
             kept = jnp.where(wide_pos >= k, ahead, 0.0)
             back = back + taps[k : k + 1] * kept[k : k + CHUNK]
             new.append(column(kept[:CHUNK] * source[SUB - k : SUB - k + CHUNK]))
-        input_back_ref[here, :] = back.astype(LOW)
+        back_ref[here, width:] = back.astype(LOW)
         return after, late, spread[:SUB], tuple(x + y for x, y in zip(sums, new))
 
     start = tuple(zero for _ in range(4 + taps.shape[0]))
     sums = lax.fori_loop(0, steps, step, (zero, zero, jnp.zeros((SUB, width), WIDE), start))[3]
     rows = list(sums)
     rows[3] = -slope * rows[3]
-    small_ref[...] = jnp.concatenate(rows, axis=0)
-    rate_w_grad_ref[...] = transposed_times(conv_ref[...], rate_low_ref[...])
-    inlet_w_grad_ref[...] = transposed_times(conv_ref[...], inlet_low_ref[...])
+    def spread_columns(turn, _):
+        here = pl.ds(pl.multiple_of(turn * COLUMNS, COLUMNS), COLUMNS)
+        block_grad_ref[:width, here] = transposed_times(mixed_ref[...], middle_ref[:, here]).astype(LOW)
+        branch_grad = transposed_times(back_ref[...], first_ref[:, here])
+        branch_grad_ref[:, here] = branch_grad.astype(LOW)
+        gain_ref[:, here] = column(branch_grad * branches_ref[:, here].astype(WIDE))
+        partial_ref[:, here] = times(back_ref[...], branches_ref[:, here]).astype(LOW)
+        return _
+
+    lax.fori_loop(0, features // COLUMNS, spread_columns, 0)
+    size = width // heads
+    strips, depth = strip_shape(features, heads, size, len(rows))
+    stacked_ref[...] = jnp.zeros_like(stacked_ref)
+    block = 0
+    for low_ref in (rate_low_ref, inlet_low_ref):
+        full = transposed_times(conv_ref[...], low_ref[...])
+        for h in range(heads):
+            part = slice(h * size, (h + 1) * size)
+            stacked_ref[pl.ds(block * size, size), :] = full[part, part]
+            block += 1
+    small = jnp.concatenate(rows, axis=0)
+    for h in range(heads):
+        stacked_ref[pl.ds(block * size + h * SUB, len(rows)), :] = small[:, h * size : (h + 1) * size]
+    block_grad_ref[pl.ds(width, depth), :] = jnp.zeros((depth, features), LOW)
+    for k in range(strips):
+        block_grad_ref[pl.ds(width, depth), k * size : (k + 1) * size] = stacked_ref[pl.ds(k * depth, depth), :].astype(LOW)
+
+
+def strip_shape(features, heads, size, small):
+    strips = features // size
+    rows = 2 * heads * size + heads * SUB
+    return strips, -(-rows // (strips * 2 * SUB)) * 2 * SUB
+
+
+def unpack_strips(packed, heads, size, small):
+    strips, depth = strip_shape(packed.shape[1], heads, size, small)
+    stacked = jnp.concatenate([packed[:, k * size : (k + 1) * size] for k in range(strips)])
+    square = stacked[: 2 * heads * size].reshape(2, heads, size, size)
+    parts = [stacked[2 * heads * size + h * SUB :][:small] for h in range(heads)]
+    return square, jnp.concatenate(parts, axis=1)
 
 
 def in_vmem():
     return pl.BlockSpec(memory_space=pltpu.VMEM)
 
 
-def run_kernel(body, outs, scratch, operands, cost):
+def run_kernel(body, outs, scratch, operands, room):
     return pl.pallas_call(
         body,
         in_specs=[pl.BlockSpec(memory_space=pltpu.SMEM)] + [in_vmem()] * (len(operands) - 1),
         out_specs=[in_vmem()] * len(outs),
         out_shape=outs,
         scratch_shapes=scratch,
-        compiler_params=pltpu.CompilerParams(vmem_limit_bytes=48 * 1024 * 1024),
-        cost_estimate=cost,
+        compiler_params=pltpu.CompilerParams(vmem_limit_bytes=room * 1024 * 1024),
+        cost_estimate=NO_COST,
     )(*operands)
 
 
-def forward_mix(lengths, gate_pre, input_pre, taps, rate_w, inlet_w, extra):
-    count, width = input_pre.shape
+def forward_mix(lengths, both, taps, rate_w, inlet_w, extra):
+    count, width = both.shape[0], both.shape[1] // 2
     wide = jax.ShapeDtypeStruct((count, width), WIDE)
     low = jax.ShapeDtypeStruct((count, width), LOW)
     state = jax.ShapeDtypeStruct((count + SUB, width), WIDE)
-    cost = pl.CostEstimate(
-        flops=60 * count * width + 4 * count * width * width,
-        bytes_accessed=26 * count * width,
-        transcendentals=5 * count * width,
-    )
     return run_kernel(
         forward_kernel,
         [low, low, wide, wide, state],
         [pltpu.VMEM((count + SUB, width), WIDE)],
-        (lengths, gate_pre, input_pre, taps, rate_w, inlet_w, extra),
-        cost,
+        (lengths, both, taps, rate_w, inlet_w, extra),
+        20,
     )
 
 
-def backward_mix(lengths, grad, gate_pre, input_pre, conv, rate, inlet, state, taps, rate_w, inlet_w, extra):
-    count, width = input_pre.shape
-    low = jax.ShapeDtypeStruct((count, width), LOW)
-    square = jax.ShapeDtypeStruct((width, width), WIDE)
-    small = jax.ShapeDtypeStruct((4 + taps.shape[0], width), WIDE)
-    cost = pl.CostEstimate(
-        flops=150 * count * width + 8 * count * width * width,
-        bytes_accessed=30 * count * width,
-        transcendentals=5 * count * width,
-    )
-    padded = pltpu.VMEM((count + SUB, width), WIDE)
+def backward_mix(heads, lengths, middle, block, first, branches, mixed, both, conv, *others):
+    count, width = mixed.shape
+    features = middle.shape[1]
     narrow = pltpu.VMEM((count, width), LOW)
+    size = width // heads
+    strips, depth = strip_shape(features, heads, size, SUB)
     return run_kernel(
-        backward_kernel,
-        [low, low, square, square, small],
-        [padded, narrow, narrow],
-        (lengths, grad, gate_pre, input_pre, conv, rate, inlet, state, taps, rate_w, inlet_w, extra),
-        cost,
+        lambda *refs: backward_kernel(heads, *refs),
+        [
+            jax.ShapeDtypeStruct((count, features), LOW),
+            jax.ShapeDtypeStruct((width + depth, features), LOW),
+            jax.ShapeDtypeStruct((2 * width, features), LOW),
+            jax.ShapeDtypeStruct((1, features), WIDE),
+        ],
+        [
+            pltpu.VMEM((count, width), WIDE),
+            pltpu.VMEM((count, 2 * width), LOW),
+            pltpu.VMEM((count + SUB, width), WIDE),
+            narrow,
+            narrow,
+            pltpu.VMEM((strips * depth, size), WIDE),
+        ],
+        (lengths, middle, block, first, branches, mixed, both, conv) + others,
+        44,
     )
 
 
@@ -270,11 +321,6 @@
     return full.reshape(heads * size, heads * size)
 
 
-def pick_blocks(full, heads):
-    size = full.shape[0] // heads
-    return jnp.stack([full[h * size : (h + 1) * size, h * size : (h + 1) * size] for h in range(heads)])
-
-
 def sum_rows(values):
     return lax.psum_scatter(values.astype(LOW), "mp", scatter_dimension=0, tiled=True).astype(WIDE)
 
@@ -283,8 +329,146 @@
     return lax.all_gather(values, "mp", axis=0, tiled=True)
 
 
-def sum_buckets(values):
-    return lax.psum(values.astype(LOW), "dp").astype(WIDE)
+def place_kernel(pieces, kept, splits, where_ref, *refs):
+    out_refs = refs[pieces + kept :]
+    for k in range(pieces):
+
+        @pl.when(pl.program_id(0) == k)
+        def _():
+            start = 0
+            for out_ref, rows in zip(out_refs, splits):
+                out_ref[...] = refs[k][pl.ds(start, rows), :].astype(out_ref.dtype)
+                start += rows
+
+
+def place(pieces, spots, total, axis, splits, kind, onto=()):
+    count = len(pieces)
+    rows, columns = pieces[0].shape
+    splits = splits or (rows,)
+    outs = [
+        jax.ShapeDtypeStruct((r * total, columns) if axis == 0 else (r, columns * total), kind) for r in splits
+    ]
+    spot = (lambda k, at: (at[k], 0)) if axis == 0 else (lambda k, at: (0, at[k]))
+    room = rows * columns * (2 * 2 * count + 4 * 2) + 4 * 1024 * 1024
+    return pl.pallas_call(
+        lambda *refs: place_kernel(count, len(onto), splits, *refs),
+        grid_spec=pltpu.PrefetchScalarGridSpec(
+            num_scalar_prefetch=1,
+            grid=(count,),
+            in_specs=[pl.BlockSpec((rows, columns), lambda k, at: (0, 0))] * count
+            + [pl.BlockSpec(memory_space=pl.ANY)] * len(onto),
+            out_specs=[pl.BlockSpec((r, columns), spot) for r in splits],
+        ),
+        out_shape=outs,
+        input_output_aliases={1 + count + k: k for k in range(len(onto))},
+        compiler_params=pltpu.CompilerParams(vmem_limit_bytes=room),
+        cost_estimate=NO_COST,
+    )(jnp.stack(spots).astype(jnp.int32), *pieces, *onto)
+
+
+def halves(values, axis):
+    size = values.shape[axis] // 2
+    return lax.slice_in_dim(values, 0, size, axis=axis), lax.slice_in_dim(values, size, 2 * size, axis=axis)
+
+
+def dp_bits():
+    return lax.axis_size("dp").bit_length() - 1
+
+
+def swap(values, bit):
+    count = lax.axis_size("dp")
+    return lax.ppermute(values, "dp", [(i, i ^ (1 << bit)) for i in range(count)])
+
+
+def order_of(turn):
+    bits = dp_bits()
+    return [(turn + k) % bits for k in range(bits)]
+
+
+def split_for(values, axis, bit):
+    first, second = halves(values, axis)
+    upper = ((lax.axis_index("dp") >> bit) & 1) == 1
+    return jnp.where(upper, first, second), jnp.where(upper, second, first)
+
+
+def join(kept, got):
+    return (kept.astype(WIDE) + got.astype(WIDE)).astype(LOW)
+
+
+class Part:
+    def __init__(self, values, axis, turn):
+        self.axis, self.order = axis, order_of(turn)
+        self.step = 0
+        self.load(values)
+
+    def load(self, values):
+        if self.step < len(self.order):
+            self.send, self.kept = split_for(values, self.axis, self.order[self.step])
+        else:
+            self.pieces = {0: values}
+
+    def reduce(self):
+        return swap(self.send, self.order[self.step])
+
+    def land(self, got):
+        self.step += 1
+        self.load(join(self.kept, got))
+
+    def forwards(self, level):
+        made = []
+        for chosen in itertools.combinations(reversed(self.order), level):
+            made.append((sum(1 << bit for bit in chosen[:-1]), chosen[-1]))
+        return made
+
+    def spot(self, mask):
+        owner = lax.axis_index("dp") ^ mask
+        bits = len(self.order)
+        return sum(((owner >> self.order[k]) & 1) << (bits - 1 - k) for k in range(bits))
+
+
+def start_gather(parts, level):
+    return [(part, mask ^ (1 << bit), swap(part.pieces[mask], bit)) for part in parts for mask, bit in part.forwards(level)]
+
+
+def exchange(reducing=(), gathered=(), extras=()):
+    gots = [part.reduce() for part in reducing]
+    made = lax.optimization_barrier((*gots, *[piece for _, _, piece in gathered], *extras))
+    for part, got in zip(reducing, made):
+        part.land(got)
+    for (part, mask, _), piece in zip(gathered, made[len(gots) :]):
+        part.pieces[mask] = piece
+    return made[len(gots) + len(gathered) :]
+
+
+def reduce_fully(parts):
+    while parts[0].step < len(parts[0].order):
+        exchange(parts)
+
+
+def gather_fully(parts, level):
+    for more in range(level, dp_bits() + 1):
+        exchange(gathered=start_gather(parts, more))
+
+
+def finish(parts, axis, splits=None, masks=None, onto=()):
+    count = 1 << dp_bits()
+    chosen = [(turn, mask) for turn, part in enumerate(parts) for mask in part.pieces if masks is None or mask in masks]
+    spots = [parts[turn].spot(mask) + turn * count for turn, mask in chosen]
+    blocks = [parts[turn].pieces[mask] for turn, mask in chosen]
+    return place(blocks, spots, len(parts) * count, axis, splits, WIDE, onto)
+
+
+def column_parts(values):
+    return [Part(half, 1, turn) for turn, half in enumerate(halves(values, 1))]
+
+
+def shifts_of(values, axis, shifts):
+    count = lax.axis_size(axis)
+    return [lax.ppermute(values, axis, [(i, (i + shift) % count) for i in range(count)]) for shift in shifts]
+
+
+def tie(values, *others):
+    return lax.optimization_barrier((values,) + others)[0]
 
 
 def local(
@@ -315,66 +499,97 @@
     own_grad = out_grad.astype(WIDE)
     first_scale = norm_scale(own_input)
     first_rows = all_rows((own_input * first_scale * first_gain).astype(LOW))
-    grad_rows = all_rows(out_grad)
     soft = DECAY_SCALE * jax.nn.softplus(decay_param)
     slope = DECAY_SCALE * jax.nn.sigmoid(decay_param)
     extra = jnp.stack([conv_bias, rate_bias, inlet_bias, soft, slope])
     rate_w = spread_blocks(rate_weight)
     inlet_w = spread_blocks(inlet_weight)
-
-    gate_pre = times(first_rows, branch_gate)
-    input_pre = times(first_rows, branch_input)
-    mixed, conv, rate, inlet, state = forward_mix(
-        lengths, gate_pre, input_pre, conv_weight, rate_w, inlet_w, extra
-    )
-    own_middle = own_input + sum_rows(times(mixed, block_out))
+    branches = jnp.concatenate([branch_gate.T, branch_input.T])
+
+    first_rows = tie(first_rows, rate_w, inlet_w, extra, branches)
+    both = times_transposed(first_rows, branches)
+    grad_rows = all_rows(tie(out_grad, first_rows))
+    mixed, conv, rate, inlet, state = forward_mix(lengths, both, conv_weight, rate_w, inlet_w, extra)
+    block_partial = tie(times(mixed, block_out), grad_rows)
+    own_middle = own_input + sum_rows(block_partial)
     second_scale = norm_scale(own_middle)
     second_rows = all_rows((own_middle * second_scale * second_gain).astype(LOW))
     d_hidden = times_transposed(grad_rows, down_weight)
+    second_rows, d_hidden = lax.optimization_barrier((second_rows, d_hidden))
     gate_act = times(second_rows, gate_weight)
     up_act = times(second_rows, up_weight)
     value, bend = gelu_pair(gate_act)
     hidden = (value * up_act).astype(LOW)
     gate_low = (d_hidden * up_act * bend).astype(LOW)
     up_low = (d_hidden * value).astype(LOW)
-    second_input = sum_rows(times_transposed(gate_low, gate_weight) + times_transposed(up_low, up_weight))
-    down_grad = transposed_times(hidden, grad_rows)
-    gate_grad = transposed_times(second_rows, gate_low)
-    up_grad = transposed_times(second_rows, up_low)
-    part, second_gain_grad = norm_back(own_middle, second_scale, second_gain, second_input)
-    middle_grad = own_grad + part
+
+    down_parts = column_parts(transposed_times(hidden, grad_rows).astype(LOW))
+    late_gate = tie(gate_low, *[part.send for part in down_parts])
+    second_input = sum_rows(times_transposed(late_gate, gate_weight) + times_transposed(up_low, up_weight))
+    gate_part = Part(transposed_times(second_rows, gate_low).astype(LOW), 0, 0)
+    up_part = Part(transposed_times(second_rows, up_low).astype(LOW), 0, 1)
+    wide_parts = [gate_part, up_part]
+    mlp = down_parts + wide_parts
+
+    exchange(down_parts)
+    (second_input,) = exchange(down_parts + wide_parts, extras=(second_input,))
+    middle_grad = own_grad + norm_back(own_middle, second_scale, second_gain, second_input)
+    second_gain_grad = jnp.sum(second_input * own_middle * second_scale, axis=0)
     middle_rows = all_rows(middle_grad.astype(LOW))
-    d_mixed = times_transposed(middle_rows, block_out)
-    block_grad = transposed_times(mixed, middle_rows)
-    output = (own_middle + sum_rows(times(hidden, down_weight))).astype(LOW)
-    gate_back, input_back, rate_w_grad, inlet_w_grad, small = backward_mix(
-        lengths, d_mixed, gate_pre, input_pre, conv, rate, inlet, state, conv_weight, rate_w, inlet_w, extra
+
+    reduce_fully(down_parts)
+    out_partial = times(tie(hidden, second_input), down_weight)
+    middle_rows, out_partial = exchange(wide_parts, start_gather(down_parts, 1), (middle_rows, out_partial))
+    out_sum = sum_rows(out_partial)
+
+    reduce_fully(wide_parts)
+    made = backward_mix(
+        heads, lengths, middle_rows, block_out, first_rows, branches, mixed,
+        both, conv, rate, inlet, state, conv_weight, rate_w, inlet_w, extra,
     )
-    first_input = sum_rows(times_transposed(gate_back, branch_gate) + times_transposed(input_back, branch_input))
-    branch_gate_grad = transposed_times(gate_back, first_rows)
-    branch_input_grad = transposed_times(input_back, first_rows)
-    part, first_gain_grad = norm_back(own_input, first_scale, first_gain, first_input)
-    input_grad = middle_grad + part
-
-    gains = lax.psum(jnp.stack([first_gain_grad, second_gain_grad]), ("dp", "mp"))
-    mlp = sum_buckets(jnp.concatenate([down_grad.reshape(-1, features), gate_grad.reshape(-1, features), up_grad.reshape(-1, features)]))
-    square = jnp.stack([pick_blocks(rate_w_grad, heads), pick_blocks(inlet_w_grad, heads)])
-    flat = jnp.concatenate([square.reshape(-1), small.reshape(-1)])
-    flat = jnp.pad(flat, (0, -flat.shape[0] % (16 * features))).reshape(-1, features)
-    rec = sum_buckets(jnp.concatenate([block_grad, branch_gate_grad, branch_input_grad, flat]))
-    hidden_count = down_weight.shape[0]
-    down_grad = mlp[:hidden_count]
-    gate_grad = mlp[hidden_count : 2 * hidden_count].reshape(features, -1)
-    up_grad = mlp[2 * hidden_count :].reshape(features, -1)
-    flat = rec[3 * width :].reshape(-1)
-    square = flat[: square.size].reshape(square.shape)
-    small = flat[square.size : square.size + small.size].reshape(small.shape)
+    first_partial, block_grad, branch_grad, gain = exchange(gathered=start_gather(wide_parts, 1), extras=made)
+    first_input = sum_rows(tie(first_partial, out_sum))
+    output = (own_middle + out_sum).astype(LOW)
+    gains = jnp.concatenate([gain / first_gain, second_gain_grad[None]])
+
+    branch_parts = column_parts(branch_grad)
+    block_parts = column_parts(block_grad)
+    late = branch_parts + block_parts
+    wide_rest = start_gather(wide_parts, 2)
+    cores = lax.axis_size("mp")
+    (other,) = exchange(late, extras=[lax.ppermute(gains, "mp", [(i, i ^ 1) for i in range(cores)])])
+    gains = gains + other
+    others = shifts_of(gains, "mp", range(2, cores, 2))
+    down_rest = start_gather(down_parts, 2)
+    first_input, output, *others = exchange(late, wide_rest + down_rest, (first_input, output, *others))
+    gather_fully(mlp, 3)
+    reduce_fully(late)
+    gains = gains + sum(others)
+    others = shifts_of(gains, "dp", range(1, lax.axis_size("dp")))
+    input_grad = middle_grad + norm_back(own_input, first_scale, first_gain, first_input)
+    (gate_grad,) = finish([gate_part], 0)
+    (up_grad,) = finish([up_part], 0)
+    (down_grad,) = finish(down_parts, 1)
+    made = exchange(gathered=start_gather(late, 1), extras=(gate_grad, up_grad, down_grad, input_grad, *others))
+    gate_grad, up_grad, down_grad, input_grad = made[:4]
+    gains = gains + sum(made[4:])
+    own = [0] + [1 << bit for bit in range(dp_bits())]
+    depth = block_grad.shape[0] - width
+    halfway = finish(branch_parts, 1, (width, width), own)
+    block_halfway = finish(block_parts, 1, (width, depth), own)
+    made = exchange(gathered=start_gather(late, 2), extras=(gains, *halfway, *block_halfway))
+    gather_fully(late, 3)
+    gains = made[0]
+    rest = [mask for mask in branch_parts[0].pieces if mask not in own]
+    branch_gate_grad, branch_input_grad = finish(branch_parts, 1, (width, width), rest, made[1:3])
+    block_grad, packed = finish(block_parts, 1, (width, depth), rest, made[3:5])
+    square, small = unpack_strips(packed, heads, width // heads, 4 + taps_count)
     return (
         output,
         input_grad,
         gains[0],
-        rec[width : 2 * width].T,
-        rec[2 * width : 3 * width].T,
+        branch_gate_grad.T,
+        branch_input_grad.T,
         small[4 : 4 + taps_count],
         small[0],
         square[0],
@@ -382,7 +597,7 @@
         square[1],
         small[2],
         small[3],
-        rec[:width],
+        block_grad,
         gains[1],
         gate_grad,
         up_grad,

time: 708 us -> 471 us (0.67)
  waiting for transfers between devices: 461 us -> 207 us
  starting transfers between devices: 0.75 us -> 48.9 us
  blocking collectives: 41.4 us -> 0 us
  other arithmetic: 23.6 us -> 58.9 us
  Pallas kernels: 22.9 us -> 56.9 us
  local copies, waits for them, and re-layouts: 65.6 us -> 31.7 us
  matrix products: 71.8 us -> 45.7 us
    psum x1 -> x0, waiting for transfers between devices: 252 us -> none  [sum_buckets(): return lax.psum(values.astype(LOW), 'dp').astype(WIDE)]
    ppermute x0 -> x47, waiting for transfers between devices: none -> 82.2 us  [the longest x40 80.9 us: swap(): return lax.ppermute(values, 'dp', [(i, i ^ 1 << bit) for i in range(count)])]
    all_gather x4, waiting for transfers between devices: 129 us -> 69.6 us  [all_rows(): return lax.all_gather(values, 'mp', axis=0, tiled=True)]
    ppermute x0 -> x47, starting transfers between devices: none -> 47.7 us  [the longest x40 39.5 us: swap(): return lax.ppermute(values, 'dp', [(i, i ^ 1 << bit) for i in range(count)])]
    psum x1 -> x0, blocking collectives: 41.4 us -> none  [local(): lax.psum(jnp.stack([first_gain_grad, second_gain_grad]), ('dp', 'mp'))]
    reshape x7 -> x0, local copies, waits for them, and re-layouts: 25.5 us -> none  [the longest x1 7.82 us: local(): gate_grad = mlp[hidden_count:2 * hidden_count].reshape(features, -1)]
    reduce_scatter x4, waiting for transfers between devices: 78.6 us -> 54.6 us  [sum_rows(): lax.psum_scatter(values.astype(LOW), 'mp', scatter_dimension=0, tiled=True)]
    convert_element_type x1 -> x16, other arithmetic: 1.06 us -> 23.9 us  [the longest x13 19.8 us: join(): return (kept.astype(WIDE) + got.astype(WIDE)).astype(LOW)]
  transfers between devices with their start and end apart: 9 -> 55, of which waited for: 7 -> 18; matrix products, arithmetic and copies ran while one was open for 10% -> 19% of each run, Pallas kernels for 0% -> 12%
where the time goes in v2:
time: 471 us; the launch traced here: 464 us
  waiting for transfers between devices  207 us (44%)
  other arithmetic  58.9 us (13%)
  Pallas kernels  56.9 us (12%)
  starting transfers between devices  48.9 us (10%)
  matrix products  45.7 us (10%)
  local copies, waits for them, and re-layouts  31.7 us (7%)
  between operations  15.7 us (3%)
    ppermute x40, waiting for transfers between devices, swap(): return lax.ppermute(values, 'dp', [(i, i ^ 1 << bit) for i in range(count)])  80.9 us
    all_gather x4, waiting for transfers between devices, all_rows(): return lax.all_gather(values, 'mp', axis=0, tiled=True)  69.6 us
    reduce_scatter x4, waiting for transfers between devices, sum_rows(): lax.psum_scatter(values.astype(LOW), 'mp', scatter_dimension=0, tiled=True)  54.6 us
    ppermute x40, starting transfers between devices, swap(): return lax.ppermute(values, 'dp', [(i, i ^ 1 << bit) for i in range(count)])  39.5 us
    pallas_call x2, Pallas kernels, run_kernel(): pl.pallas_call(body, in_specs=[pl.BlockSpec(memory_space=pltpu.SMEM)] + [...  34.2 us
    pallas_call x7, Pallas kernels, place(): pl.pallas_call(lambda *refs: place_kernel(count, len(onto), splits, *refs...  22.7 us
    convert_element_type x13, other arithmetic, join(): return (kept.astype(WIDE) + got.astype(WIDE)).astype(LOW)  19.8 us
    dot_general x4, matrix products, times_transposed(): lax.dot_general(left, right, (((1,), (1,)), ((), ())), preferred_element_...  18.9 us
  transfers between devices with their start and end apart: 55, of which 18 were waited for; matrix products, arithmetic and copies ran while one was open for 19% of the time, Pallas kernels for 12%

profile of v2, /device:TPU:0, one launch (start us, length us, event | category | flops | bytes accessed | tf_op | source)
XLA Modules:
  0.0 464.4 jit_solution(8188550375480369827)
XLA Ops:
  9.2 1.9 fusion.4
  22.0 1.9 reshape.229.inlet_w_ref.refs_13_
  24.6 3.5 pad_maximum_fusion.refs_4_
  28.2 24.1 %all-gather.5.cloned.1.call-done.refs_3_ = bf16[768,2048]{1,0:T(8,128)(2,1)} async-done(((bf16[96,2048]{1,0:T(8,128)(2,1)}), bf16[768,2048]{1,0:T(8,128)(2,1)}) %all-gather.5.cloned.1.call-update) | async-done | bytes 3145744 | tf_op jit(solution)/shard_map/all_gather | solution.py:329
  52.4 5.3 %fusion.21.both_ref.refs_6_ = f32[768,640]{1,0:T(8,128)S(1)} fusion(bf16[768,2048]{1,0:T(8,128)(2,1)} %all-gather.5.cloned.1.call-done.refs_3_, bf16[320,2048]{1,0:T(8,128)(2,1)} %bitcast.54, bf16[320,2048]{1,0:T(8,128)(2,1)} %bitcast.56), kind=kOutput, calls=%fused_computation.107 | convolution fusion | flops 2018508800 | bytes 7733248 | tf_op jit(solution)/shard_map/dot_general | solution.py:28
  57.8 8.5 %shard_map.305 = (bf16[768,320]{1,0:T(8,128)(2,1)S(1)}, bf16[768,320]{1,0:T(8,128)(2,1)S(1)}, f32[768,320]{1,0:T(8,128)S(1)}, f32[768,320]{1,0:T(8,128)S(1)}, f32[776,320]{1,0:T(8,128)S(1)}) custom-call(s32[1,3]{1,0:T(1,128)S(1)} %copy-done.45, f32[768,640]{1,0:T(8,128)S(1)} %fusion.21.both_ref.refs_6_, f32[4,320]{1,0:T(4,128)S(1)} %copy-done.44, ...), custom_call_target="tpu_custom_call" | custom-call | tf_op jit(solution)/shard_map/pallas_call | solution.py:264
  71.4 3.5 fusion.24
  75.7 15.4 %all-gather.7.cloned.1.call-done = bf16[768,2048]{1,0:T(8,128)(2,1)} async-done(((bf16[96,2048]{1,0:T(8,128)(2,1)}), bf16[768,2048]{1,0:T(8,128)(2,1)}) %all-gather.7.cloned.1.call-update) | async-done | bytes 3145744 | tf_op jit(solution)/shard_map/all_gather | solution.py:329
  91.2 42.0 %reduce-scatter.5.cloned.1.call-done = bf16[96,2048]{1,0:T(8,128)(2,1)} async-done(((bf16[768,2048]{1,0:T(8,128)(2,1)}), bf16[96,2048]{1,0:T(8,128)(2,1)}) %reduce-scatter.5.cloned.1.call-update) | async-done | bytes 393232 | tf_op jit(solution)/shard_map/reduce_scatter | solution.py:325
  134.6 2.0 multiply_convert_fusion.3
  137.2 6.9 %fusion.25 = f32[768,768]{1,0:T(8,128)} fusion(bf16[768,2048]{1,0:T(8,128)(2,1)} %all-gather.7.cloned.1.call-done, bf16[768,2048]{1,0:T(8,128)(2,1)} %param.42), kind=kOutput, calls=%fused_computation.111 | convolution fusion | flops 2415919104 | bytes 8650752 | tf_op jit(solution)/shard_map/dot_general | solution.py:28
  144.1 30.1 %all-gather.9.cloned.1.call-done = bf16[768,2048]{1,0:T(8,128)(2,1)} async-done(((bf16[96,2048]{1,0:T(8,128)(2,1)}), bf16[768,2048]{1,0:T(8,128)(2,1)}) %all-gather.9.cloned.1.call-update) | async-done | bytes 3145744 | tf_op jit(solution)/shard_map/all_gather | solution.py:329
  174.2 5.6 %fusion.26 = f32[768,768]{1,0:T(8,128)S(1)} fusion(bf16[768,2048]{1,0:T(8,128)(2,1)} %all-gather.9.cloned.1.call-done, bf16[2048,768]{1,0:T(8,128)(2,1)} %param.41), kind=kOutput, calls=%fused_computation.112 | convolution fusion | flops 2415919104 | bytes 8650752 | tf_op jit(solution)/shard_map/dot_general | solution.py:24
  179.8 3.9 multiply_convert_fusion
  183.7 2.9 convolution_convert_fusion.1
  186.6 1.4 broadcast_select_fusion.3
  188.8 2.6 fusion.27
  191.5 4.0 add_convert_fusion
  195.8 1.5 collective-permute-start
  197.3 1.5 collective-permute-start.1
  198.8 4.2 convolution_convert_fusion
  203.0 2.9 convolution_convert_fusion.2
  205.9 1.5 broadcast_select_fusion
  210.6 5.8 %collective-permute-done = bf16[768,512]{1,0:T(8,128)(2,1)S(1)} collective-permute-done((bf16[768,512]{1,0:T(8,128)(2,1)}, bf16[768,512]{1,0:T(8,128)(2,1)S(1)}, u32[]{:S(2)}, u32[]{:S(2)}) %collective-permute-start) | collective-permute-done | bytes 786464 | tf_op jit(solution)/shard_map/ppermute | solution.py:380
  216.4 1.5 collective-permute-done.1
  220.8 1.5 collective-permute-start.2
  222.3 12.6 %reduce-scatter.7.cloned.1.call-done = bf16[96,2048]{1,0:T(8,128)(2,1)} async-done(((bf16[768,2048]{1,0:T(8,128)(2,1)}), bf16[96,2048]{1,0:T(8,128)(2,1)}) %reduce-scatter.7.cloned.1.call-update) | async-done | bytes 393232 | tf_op jit(solution)/shard_map/reduce_scatter | solution.py:325
  236.0 22.0 %collective-permute-done.3 = bf16[768,256]{1,0:T(8,128)(2,1)} collective-permute-done((bf16[768,256]{1,0:T(8,128)(2,1)}, bf16[768,256]{1,0:T(8,128)(2,1)}, u32[]{:S(2)}, u32[]{:S(2)}) %collective-permute-start.3) | collective-permute-done | bytes 393248 | tf_op jit(solution)/shard_map/ppermute | solution.py:380
  263.4 1.5 collective-permute-start.11
  264.9 3.3 add_convert_fusion.1
  269.6 1.4 collective-permute-start.7
  271.0 2.2 add_convert_fusion.2
  277.2 3.9 fusion.28
  281.1 19.3 %collective-permute-done.8.refs_2_ = bf16[768,256]{1,0:T(8,128)(2,1)S(1)} collective-permute-done((bf16[768,256]{1,0:T(8,128)(2,1)S(1)}, bf16[768,256]{1,0:T(8,128)(2,1)S(1)}, u32[]{:S(2)}, u32[]{:S(2)}) %collective-permute-start.8) | collective-permute-done | bytes 393248 | tf_op jit(solution)/shard_map/ppermute | solution.py:380
  300.8 2.0 add_convert_fusion.3.refs_1_
  304.4 2.1 add_convert_fusion.4.refs_1_
  312.4 25.8 %shard_map.306 = (bf16[768,2048]{1,0:T(8,128)(2,1)}, bf16[384,2048]{1,0:T(8,128)(2,1)S(1)}, bf16[640,2048]{1,0:T(8,128)(2,1)}, f32[1,2048]{1,0:T(1,128)S(1)}) custom-call(s32[1,3]{1,0:T(1,128)S(1)} %copy-done.45, bf16[768,2048]{1,0:T(8,128)(2,1)} %all-gather.11.cloned.1.call-done.refs_1_, bf16[320,2048]{1,0:T(8,128)(2,1)S(1)} %copy-done.11, ...), custom_call_target="tpu_custom_call" | custom-call | tf_op jit(solution)/shard_map/pallas_call | solution.py:264
  341.6 3.0 broadcast_select_fusion.6
  348.1 1.5 collective-permute-start.19
  354.0 17.0 %collective-permute-done.18 = bf16[384,512]{1,0:T(8,128)(2,1)} collective-permute-done((bf16[384,512]{1,0:T(8,128)(2,1)}, bf16[384,512]{1,0:T(8,128)(2,1)}, u32[]{:S(2)}, u32[]{:S(2)}) %collective-permute-start.18) | collective-permute-done | bytes 393248 | tf_op jit(solution)/shard_map/ppermute | solution.py:380
  375.3 1.4 add_convert_fusion.10
  376.8 2.1 add_convert_fusion.7
  383.8 1.6 collective-permute-start.31
  386.1 1.3 collective-permute-start.24
  388.8 7.4 %collective-permute-done.25.refs_4_ = bf16[512,768]{1,0:T(8,128)(2,1)S(1)} collective-permute-done((bf16[512,768]{1,0:T(8,128)(2,1)}, bf16[512,768]{1,0:T(8,128)(2,1)S(1)}, u32[]{:S(2)}, u32[]{:S(2)}) %collective-permute-start.25) | collective-permute-done | bytes 786464 | tf_op jit(solution)/shard_map/ppermute | solution.py:380
  397.6 1.9 add_convert_fusion.9
  400.8 2.3 collective-permute-done.22
  406.0 1.7 collective-permute-start.41
  407.7 2.1 collective-permute-start.42
  415.6 1.5 collective-permute-start.36
  417.1 1.9 collective-permute-start.37
  419.7 1.5 collective-permute-start.32
  421.2 2.3 collective-permute-done.36.refs_2_
  423.5 2.0 collective-permute-start.33
  425.5 1.4 fusion.8
  426.9 4.8 %shard_map.308 = f32[2048,768]{1,0:T(8,128)} custom-call(s32[4]{0:T(128)S(1)} %pad_add_fusion.1.refs_0_, bf16[512,768]{1,0:T(8,128)(2,1)S(1)} %add_convert_fusion.3.refs_1_, bf16[512,768]{1,0:T(8,128)(2,1)S(1)} %copy-done.19, bf16[512,768]{1,0:T(8,128)(2,1)S(1)} %copy-done.21, bf16[512,768]{1,0:T(8,128)(2,1)} %collective-permute-done.26.refs_4_), custom_call_target="tpu_custom_call" | custom-call | tf_op jit(solution)/shard_map/pallas_call | solution.py:353
  431.8 3.6 shard_map.307
  435.5 4.6 shard_map.309
  440.3 1.5 collective-permute-start.44
  441.7 1.9 collective-permute-start.45
  444.3 3.0 shard_map.311
  447.3 3.5 shard_map.310
  450.8 1.4 shard_map.313
  454.8 1.7 shard_map.312
  (356 shorter events, 86.7 us)
Async XLA Ops:
  7.2 172.6 %copy-start = (bf16[2048,768]{1,0:T(8,128)(2,1)S(1)}, bf16[2048,768]{1,0:T(8,128)(2,1)}, u32[]{:S(2)}) copy-start(bf16[2048,768]{1,0:T(8,128)(2,1)} %param.40) | copy-start | bytes 9437188
  7.2 45.0 %all-gather.5.cloned.1.call-start = ((), (), s32[]{:S(2)}) async-start(), calls=%async_computation.4 | async-start | bytes 3538944 | tf_op jit(solution)/shard_map/all_gather | solution.py:329
  11.1 80.0 %all-gather.7.cloned.1.call-start = ((), (), s32[]{:S(2)}) async-start(), calls=%async_computation.5 | async-start | bytes 3538944 | tf_op jit(solution)/shard_map/all_gather | solution.py:329
  52.3 80.9 %reduce-scatter.5.cloned.1.call-start = ((), (), s32[]{:S(2)}) async-start(), calls=%async_computation.6 | async-start | bytes 3538944 | tf_op jit(solution)/shard_map/reduce_scatter | solution.py:325
  75.7 58.9 %copy-start.74 = (f32[2048]{0:T(1024)S(1)}, f32[2048]{0:T(1024)}, u32[]{:S(2)}) copy-start(f32[2048]{0:T(1024)} %param.39) | copy-start | bytes 24580
  91.1 83.1 %all-gather.9.cloned.1.call-start = ((), (), s32[]{:S(2)}) async-start(), calls=%async_computation.7 | async-start | bytes 3538944 | tf_op jit(solution)/shard_map/all_gather | solution.py:329
  134.6 125.4 %copy-start.84 = (f32[96]{0:T(128)}, f32[96]{0:T(128)S(1)}, u32[]{:S(2)}) copy-start(f32[96]{0:T(128)S(1)} %add_rsqrt_fusion) | copy-start | bytes 1156
  136.6 98.3 %reduce-scatter.7.cloned.1.call-start = ((), (), s32[]{:S(2)}) async-start(), calls=%async_computation.8 | async-start | bytes 3538944 | tf_op jit(solution)/shard_map/reduce_scatter | solution.py:325
  195.5 105.0 %all-gather.11.cloned.1.call-start = ((), (), s32[]{:S(2)}) async-start(), calls=%async_computation.9 | async-start | bytes 3538944 | tf_op jit(solution)/shard_map/all_gather | solution.py:329
  195.8 20.6 %collective-permute-start = (bf16[768,512]{1,0:T(8,128)(2,1)}, bf16[768,512]{1,0:T(8,128)(2,1)S(1)}, u32[]{:S(2)}, u32[]{:S(2)}) collective-permute-start(bf16[768,512]{1,0:T(8,128)(2,1)} %get-tuple-element.257), channel_id=1, source_target_pairs={{0,8},{8,0},{16,24},{24,16},{1,9},{9,1},{17,25},{25,17},{2,10},{10... | collective-permute-start | bytes 2359304 | tf_op jit(solution)/shard_map/ppermute | solution.py:380
  197.3 20.6 %collective-permute-start.1 = (bf16[768,512]{1,0:T(8,128)(2,1)}, bf16[768,512]{1,0:T(8,128)(2,1)S(1)}, u32[]{:S(2)}, u32[]{:S(2)}) collective-permute-start(bf16[768,512]{1,0:T(8,128)(2,1)} %get-tuple-element.256), channel_id=1, source_target_pairs={{0,16},{8,24},{16,0},{24,8},{1,17},{9,25},{17,1},{25,9},{2,18},{10... | collective-permute-start | bytes 2359304 | tf_op jit(solution)/shard_map/ppermute | solution.py:380
  207.5 51.6 %collective-permute-start.5 = (bf16[1024,768]{1,0:T(8,128)(2,1)}, bf16[1024,768]{1,0:T(8,128)(2,1)}, u32[]{:S(2)}, u32[]{:S(2)}) collective-permute-start(bf16[1024,768]{1,0:T(8,128)(2,1)} %broadcast_select_fusion), channel_id=1, source_target_pairs={{0,16},{8,24},{16,0},{24,8},{1,17},{9,25},{17,1},{25,9},{2,18},{10... | collective-permute-start | bytes 4718600 | tf_op jit(solution)/shard_map/ppermute | solution.py:380
  209.4 49.6 %collective-permute-start.4 = (bf16[1024,768]{1,0:T(8,128)(2,1)}, bf16[1024,768]{1,0:T(8,128)(2,1)}, u32[]{:S(2)}, u32[]{:S(2)}) collective-permute-start(bf16[1024,768]{1,0:T(8,128)(2,1)} %broadcast_select_fusion.1), channel_id=1, source_target_pairs={{0,8},{8,0},{16,24},{24,16},{1,9},{9,1},{17,25},{25,17},{2,10},{10... | collective-permute-start | bytes 4718600 | tf_op jit(solution)/shard_map/ppermute | solution.py:380
  218.6 40.4 %copy-start.47 = (bf16[96,2048]{1,0:T(8,128)(2,1)S(1)}, bf16[96,2048]{1,0:T(8,128)(2,1)}, u32[]{:S(2)}) copy-start(bf16[96,2048]{1,0:T(8,128)(2,1)} %param.26) | copy-start | bytes 1179652
  218.6 40.4 %copy-start.52 = (bf16[96,2048]{1,0:T(8,128)(2,1)S(1)}, bf16[96,2048]{1,0:T(8,128)(2,1)}, u32[]{:S(2)}) copy-start(bf16[96,2048]{1,0:T(8,128)(2,1)} %reduce-scatter.5.cloned.1.call-done) | copy-start | bytes 1179652
  218.7 41.8 %copy-start.67 = (bf16[96,2048]{1,0:T(8,128)(2,1)S(1)}, bf16[96,2048]{1,0:T(8,128)(2,1)}, u32[]{:S(2)}) copy-start(bf16[96,2048]{1,0:T(8,128)(2,1)} %param.43) | copy-start | bytes 1179652
  219.5 38.5 %collective-permute-start.3 = (bf16[768,256]{1,0:T(8,128)(2,1)}, bf16[768,256]{1,0:T(8,128)(2,1)}, u32[]{:S(2)}, u32[]{:S(2)}) collective-permute-start(bf16[768,256]{1,0:T(8,128)(2,1)} %broadcast_select_fusion.10), channel_id=1, source_target_pairs={{0,8},{8,0},{16,24},{24,16},{1,9},{9,1},{17,25},{25,17},{2,10},{10... | collective-permute-start | bytes 1179656 | tf_op jit(solution)/shard_map/ppermute | solution.py:380
  220.8 38.2 %collective-permute-start.2 = (bf16[768,256]{1,0:T(8,128)(2,1)}, bf16[768,256]{1,0:T(8,128)(2,1)S(1)}, u32[]{:S(2)}, u32[]{:S(2)}) collective-permute-start(bf16[768,256]{1,0:T(8,128)(2,1)} %broadcast_select_fusion.11), channel_id=1, source_target_pairs={{0,16},{8,24},{16,0},{24,8},{1,17},{9,25},{17,1},{25,9},{2,18},{10... | collective-permute-start | bytes 1179656 | tf_op jit(solution)/shard_map/ppermute | solution.py:380
  235.9 25.7 %copy-start.60 = (f32[96,2048]{1,0:T(8,128)}, f32[96,2048]{1,0:T(8,128)S(1)}, u32[]{:S(2)}) copy-start(f32[96,2048]{1,0:T(8,128)S(1)} %convert_element_type.220) | copy-start | bytes 2359300
  261.6 136.0 %reduce-scatter.9.cloned.1.call-start = ((), (), s32[]{:S(2)}) async-start(), calls=%async_computation.10 | async-start | bytes 3538944 | tf_op jit(solution)/shard_map/reduce_scatter | solution.py:325
  262.8 13.7 %collective-permute-start.10 = (bf16[768,256]{1,0:T(8,128)(2,1)S(1)}, bf16[768,256]{1,0:T(8,128)(2,1)S(1)}, u32[]{:S(2)}, u32[]{:S(2)}) collective-permute-start(bf16[768,256]{1,0:T(8,128)(2,1)S(1)} %add_convert_fusion.12.refs_5_), channel_id=1, source_target_pairs={{0,8},{8,0},{16,24},{24,16},{1,9},{9,1},{17,25},{25,17},{2,10},{10... | collective-permute-start | bytes 1179656 | tf_op jit(solution)/shard_map/ppermute | solution.py:380
  263.4 17.7 %collective-permute-start.11 = (bf16[768,256]{1,0:T(8,128)(2,1)S(1)}, bf16[768,256]{1,0:T(8,128)(2,1)S(1)}, u32[]{:S(2)}, u32[]{:S(2)}) collective-permute-start(bf16[768,256]{1,0:T(8,128)(2,1)S(1)} %add_convert_fusion.12.refs_5_), channel_id=1, source_target_pairs={{0,16},{8,24},{16,0},{24,8},{1,17},{9,25},{17,1},{25,9},{2,18},{10... | collective-permute-start | bytes 1179656 | tf_op jit(solution)/shard_map/ppermute | solution.py:380
  269.6 30.8 %collective-permute-start.7 = (bf16[512,768]{1,0:T(8,128)(2,1)}, bf16[512,768]{1,0:T(8,128)(2,1)}, u32[]{:S(2)}, u32[]{:S(2)}) collective-permute-start(bf16[512,768]{1,0:T(8,128)(2,1)} %broadcast_select_fusion.2), channel_id=1, source_target_pairs={{0,8},{8,0},{16,24},{24,16},{1,9},{9,1},{17,25},{25,17},{2,10},{10... | collective-permute-start | bytes 2359304 | tf_op jit(solution)/shard_map/ppermute | solution.py:380
  274.3 26.2 %collective-permute-start.6 = (bf16[512,768]{1,0:T(8,128)(2,1)}, bf16[512,768]{1,0:T(8,128)(2,1)}, u32[]{:S(2)}, u32[]{:S(2)}) collective-permute-start(bf16[512,768]{1,0:T(8,128)(2,1)} %broadcast_select_fusion.5), channel_id=1, source_target_pairs={{0,16},{8,24},{16,0},{24,8},{1,17},{9,25},{17,1},{25,9},{2,18},{10... | collective-permute-start | bytes 2359304 | tf_op jit(solution)/shard_map/ppermute | solution.py:380
  275.5 24.9 %collective-permute-start.8 = (bf16[768,256]{1,0:T(8,128)(2,1)S(1)}, bf16[768,256]{1,0:T(8,128)(2,1)S(1)}, u32[]{:S(2)}, u32[]{:S(2)}) collective-permute-start(bf16[768,256]{1,0:T(8,128)(2,1)S(1)} %add_convert_fusion.13.refs_1_), channel_id=1, source_target_pairs={{0,16},{8,24},{16,0},{24,8},{1,17},{9,25},{17,1},{25,9},{2,18},{10... | collective-permute-start | bytes 1179656 | tf_op jit(solution)/shard_map/ppermute | solution.py:380
  276.5 23.9 %collective-permute-start.9 = (bf16[768,256]{1,0:T(8,128)(2,1)S(1)}, bf16[768,256]{1,0:T(8,128)(2,1)S(1)}, u32[]{:S(2)}, u32[]{:S(2)}) collective-permute-start(bf16[768,256]{1,0:T(8,128)(2,1)S(1)} %add_convert_fusion.13.refs_1_), channel_id=1, source_target_pairs={{0,8},{8,0},{16,24},{24,16},{1,9},{9,1},{17,25},{25,17},{2,10},{10... | collective-permute-start | bytes 1179656 | tf_op jit(solution)/shard_map/ppermute | solution.py:380
  300.5 99.0 %reduce-scatter.11.cloned.1.call-start = ((), (), s32[]{:S(2)}) async-start(), calls=%async_computation.11 | async-start | bytes 3538944 | tf_op jit(solution)/shard_map/reduce_scatter | solution.py:325
  302.9 35.3 %collective-permute-start.14 = (bf16[512,768]{1,0:T(8,128)(2,1)S(1)}, bf16[512,768]{1,0:T(8,128)(2,1)S(1)}, u32[]{:S(2)}, u32[]{:S(2)}) collective-permute-start(bf16[512,768]{1,0:T(8,128)(2,1)S(1)} %add_convert_fusion.3.refs_1_), channel_id=1, source_target_pairs={{0,8},{8,0},{16,24},{24,16},{1,9},{9,1},{17,25},{25,17},{2,10},{10... | collective-permute-start | bytes 2359304 | tf_op jit(solution)/shard_map/ppermute | solution.py:380
  303.7 34.5 %collective-permute-start.15 = (bf16[512,768]{1,0:T(8,128)(2,1)S(1)}, bf16[512,768]{1,0:T(8,128)(2,1)S(1)}, u32[]{:S(2)}, u32[]{:S(2)}) collective-permute-start(bf16[512,768]{1,0:T(8,128)(2,1)S(1)} %add_convert_fusion.3.refs_1_), channel_id=1, source_target_pairs={{0,16},{8,24},{16,0},{24,8},{1,17},{9,25},{17,1},{25,9},{2,18},{10... | collective-permute-start | bytes 2359304 | tf_op jit(solution)/shard_map/ppermute | solution.py:380
  306.6 32.6 %collective-permute-start.12 = (bf16[512,768]{1,0:T(8,128)(2,1)S(1)}, bf16[512,768]{1,0:T(8,128)(2,1)S(1)}, u32[]{:S(2)}, u32[]{:S(2)}) collective-permute-start(bf16[512,768]{1,0:T(8,128)(2,1)S(1)} %add_convert_fusion.4.refs_1_), channel_id=1, source_target_pairs={{0,16},{8,24},{16,0},{24,8},{1,17},{9,25},{17,1},{25,9},{2,18},{10... | collective-permute-start | bytes 2359304 | tf_op jit(solution)/shard_map/ppermute | solution.py:380
  307.7 31.5 %collective-permute-start.13 = (bf16[512,768]{1,0:T(8,128)(2,1)S(1)}, bf16[512,768]{1,0:T(8,128)(2,1)S(1)}, u32[]{:S(2)}, u32[]{:S(2)}) collective-permute-start(bf16[512,768]{1,0:T(8,128)(2,1)S(1)} %add_convert_fusion.4.refs_1_), channel_id=1, source_target_pairs={{0,8},{8,0},{16,24},{24,16},{1,9},{9,1},{17,25},{25,17},{2,10},{10... | collective-permute-start | bytes 2359304 | tf_op jit(solution)/shard_map/ppermute | solution.py:380
  341.6 29.4 %copy-start.33 = (bf16[768,256]{1,0:T(8,128)(2,1)S(1)}, bf16[768,256]{1,0:T(8,128)(2,1)}, u32[]{:S(2)}) copy-start(bf16[768,256]{1,0:T(8,128)(2,1)} %copy-done.32) | copy-start | bytes 1179652
  344.5 28.1 %collective-permute-start.16 = (bf16[640,512]{1,0:T(8,128)(2,1)}, bf16[640,512]{1,0:T(8,128)(2,1)}, u32[]{:S(2)}, u32[]{:S(2)}) collective-permute-start(bf16[640,512]{1,0:T(8,128)(2,1)} %get-tuple-element.261), channel_id=1, source_target_pairs={{0,8},{8,0},{16,24},{24,16},{1,9},{9,1},{17,25},{25,17},{2,10},{10... | collective-permute-start | bytes 1966088 | tf_op jit(solution)/shard_map/ppermute | solution.py:380
  345.3 28.5 %collective-permute-start.17 = (bf16[640,512]{1,0:T(8,128)(2,1)}, bf16[640,512]{1,0:T(8,128)(2,1)}, u32[]{:S(2)}, u32[]{:S(2)}) collective-permute-start(bf16[640,512]{1,0:T(8,128)(2,1)} %get-tuple-element.260), channel_id=1, source_target_pairs={{0,16},{8,24},{16,0},{24,8},{1,17},{9,25},{17,1},{25,9},{2,18},{10... | collective-permute-start | bytes 1966088 | tf_op jit(solution)/shard_map/ppermute | solution.py:380
  347.2 23.8 %collective-permute-start.18 = (bf16[384,512]{1,0:T(8,128)(2,1)}, bf16[384,512]{1,0:T(8,128)(2,1)}, u32[]{:S(2)}, u32[]{:S(2)}) collective-permute-start(bf16[384,512]{1,0:T(8,128)(2,1)} %get-tuple-element.265), channel_id=1, source_target_pairs={{0,8},{8,0},{16,24},{24,16},{1,9},{9,1},{17,25},{25,17},{2,10},{10... | collective-permute-start | bytes 1179656 | tf_op jit(solution)/shard_map/ppermute | solution.py:380
  348.1 23.4 %collective-permute-start.19 = (bf16[384,512]{1,0:T(8,128)(2,1)}, bf16[384,512]{1,0:T(8,128)(2,1)}, u32[]{:S(2)}, u32[]{:S(2)}) collective-permute-start(bf16[384,512]{1,0:T(8,128)(2,1)} %get-tuple-element.264), channel_id=1, source_target_pairs={{0,16},{8,24},{16,0},{24,8},{1,17},{9,25},{17,1},{25,9},{2,18},{10... | collective-permute-start | bytes 1179656 | tf_op jit(solution)/shard_map/ppermute | solution.py:380
  351.7 1.5 collective-permute-start.20
  351.9 24.8 %copy-start.62 = (bf16[640,2048]{1,0:T(8,128)(2,1)S(1)}, bf16[640,2048]{1,0:T(8,128)(2,1)}, u32[]{:S(2)}) copy-start(bf16[640,2048]{1,0:T(8,128)(2,1)} %get-tuple-element.181) | copy-start | bytes 7864324
  353.2 28.0 %collective-permute-start.27 = (bf16[768,256]{1,0:T(8,128)(2,1)}, bf16[768,256]{1,0:T(8,128)(2,1)S(1)}, u32[]{:S(2)}, u32[]{:S(2)}) collective-permute-start(bf16[768,256]{1,0:T(8,128)(2,1)} %copy-done.36), channel_id=1, source_target_pairs={{0,8},{8,0},{16,24},{24,16},{1,9},{9,1},{17,25},{25,17},{2,10},{10... | collective-permute-start | bytes 1179656 | tf_op jit(solution)/shard_map/ppermute | solution.py:380
  371.0 12.1 %collective-permute-start.28 = (bf16[768,256]{1,0:T(8,128)(2,1)S(1)}, bf16[768,256]{1,0:T(8,128)(2,1)S(1)}, u32[]{:S(2)}, u32[]{:S(2)}) collective-permute-start(bf16[768,256]{1,0:T(8,128)(2,1)S(1)} %copy-done.33), channel_id=1, source_target_pairs={{0,16},{8,24},{16,0},{24,8},{1,17},{9,25},{17,1},{25,9},{2,18},{10... | collective-permute-start | bytes 1179656 | tf_op jit(solution)/shard_map/ppermute | solution.py:380
  371.5 24.6 %collective-permute-start.25 = (bf16[512,768]{1,0:T(8,128)(2,1)}, bf16[512,768]{1,0:T(8,128)(2,1)S(1)}, u32[]{:S(2)}, u32[]{:S(2)}) collective-permute-start(bf16[512,768]{1,0:T(8,128)(2,1)} %copy-done.22), channel_id=1, source_target_pairs={{0,8},{8,0},{16,24},{24,16},{1,9},{9,1},{17,25},{25,17},{2,10},{10... | collective-permute-start | bytes 2359304 | tf_op jit(solution)/shard_map/ppermute | solution.py:380
  372.6 28.0 %collective-permute-start.26 = (bf16[512,768]{1,0:T(8,128)(2,1)}, bf16[512,768]{1,0:T(8,128)(2,1)}, u32[]{:S(2)}, u32[]{:S(2)}) collective-permute-start(bf16[512,768]{1,0:T(8,128)(2,1)} %copy-done.18), channel_id=1, source_target_pairs={{0,16},{8,24},{16,0},{24,8},{1,17},{9,25},{17,1},{25,9},{2,18},{10... | collective-permute-start | bytes 2359304 | tf_op jit(solution)/shard_map/ppermute | solution.py:380
  374.5 11.6 %collective-permute-start.29 = (f32[2,2048]{1,0:T(2,128)S(1)}, f32[2,2048]{1,0:T(2,128)S(1)}, u32[]{:S(2)}, u32[]{:S(2)}) collective-permute-start(f32[2,2048]{1,0:T(2,128)S(1)} %fusion.19), channel_id=1, source_target_pairs={{0,2},{1,3},{2,4},{3,5},{4,6},{5,7},{6,0},{7,1},{8,10},{9,11},{10,... | collective-permute-start | bytes 49160 | tf_op jit(solution)/shard_map/ppermute | solution.py:467
  381.2 6.3 %collective-permute-start.30 = (f32[2,2048]{1,0:T(2,128)S(1)}, f32[2,2048]{1,0:T(2,128)S(1)}, u32[]{:S(2)}, u32[]{:S(2)}) collective-permute-start(f32[2,2048]{1,0:T(2,128)S(1)} %fusion.19), channel_id=1, source_target_pairs={{0,4},{1,5},{2,6},{3,7},{4,0},{5,1},{6,2},{7,3},{8,12},{9,13},{10,... | collective-permute-start | bytes 49160 | tf_op jit(solution)/shard_map/ppermute | solution.py:467
  383.8 4.2 collective-permute-start.31
  386.1 14.6 %collective-permute-start.24 = (bf16[384,256]{1,0:T(8,128)(2,1)}, bf16[384,256]{1,0:T(8,128)(2,1)}, u32[]{:S(2)}, u32[]{:S(2)}) collective-permute-start(bf16[384,256]{1,0:T(8,128)(2,1)} %broadcast_select_fusion.14), channel_id=1, source_target_pairs={{0,8},{8,0},{16,24},{24,16},{1,9},{9,1},{17,25},{25,17},{2,10},{10... | collective-permute-start | bytes 589832 | tf_op jit(solution)/shard_map/ppermute | solution.py:380
  387.4 13.4 %collective-permute-start.23 = (bf16[384,256]{1,0:T(8,128)(2,1)}, bf16[384,256]{1,0:T(8,128)(2,1)}, u32[]{:S(2)}, u32[]{:S(2)}) collective-permute-start(bf16[384,256]{1,0:T(8,128)(2,1)} %broadcast_select_fusion.15), channel_id=1, source_target_pairs={{0,16},{8,24},{16,0},{24,8},{1,17},{9,25},{17,1},{25,9},{2,18},{10... | collective-permute-start | bytes 589832 | tf_op jit(solution)/shard_map/ppermute | solution.py:380
  388.0 15.2 %collective-permute-start.22 = (bf16[640,256]{1,0:T(8,128)(2,1)}, bf16[640,256]{1,0:T(8,128)(2,1)}, u32[]{:S(2)}, u32[]{:S(2)}) collective-permute-start(bf16[640,256]{1,0:T(8,128)(2,1)} %broadcast_select_fusion.12), channel_id=1, source_target_pairs={{0,8},{8,0},{16,24},{24,16},{1,9},{9,1},{17,25},{25,17},{2,10},{10... | collective-permute-start | bytes 983048 | tf_op jit(solution)/shard_map/ppermute | solution.py:380
  397.0 7.4 %collective-permute-start.21 = (bf16[640,256]{1,0:T(8,128)(2,1)}, bf16[640,256]{1,0:T(8,128)(2,1)}, u32[]{:S(2)}, u32[]{:S(2)}) collective-permute-start(bf16[640,256]{1,0:T(8,128)(2,1)} %broadcast_select_fusion.13), channel_id=1, source_target_pairs={{0,16},{8,24},{16,0},{24,8},{1,17},{9,25},{17,1},{25,9},{2,18},{10... | collective-permute-start | bytes 983048 | tf_op jit(solution)/shard_map/ppermute | solution.py:380
  405.2 10.4 %collective-permute-start.40 = (f32[2,2048]{1,0:T(2,128)S(1)}, f32[2,2048]{1,0:T(2,128)S(1)}, u32[]{:S(2)}, u32[]{:S(2)}) collective-permute-start(f32[2,2048]{1,0:T(2,128)S(1)} %add_add_fusion.1), channel_id=1, source_target_pairs={{0,8},{8,16},{16,24},{24,0},{1,9},{9,17},{17,25},{25,1},{2,10},{10... | collective-permute-start | bytes 49160 | tf_op jit(solution)/shard_map/ppermute | solution.py:467
  406.0 11.1 %collective-permute-start.41 = (f32[2,2048]{1,0:T(2,128)S(1)}, f32[2,2048]{1,0:T(2,128)S(1)}, u32[]{:S(2)}, u32[]{:S(2)}) collective-permute-start(f32[2,2048]{1,0:T(2,128)S(1)} %add_add_fusion.1), channel_id=1, source_target_pairs={{0,16},{8,24},{16,0},{24,8},{1,17},{9,25},{17,1},{25,9},{2,18},{10... | collective-permute-start | bytes 49160 | tf_op jit(solution)/shard_map/ppermute | solution.py:467
  407.7 11.3 %collective-permute-start.42 = (f32[2,2048]{1,0:T(2,128)S(1)}, f32[2,2048]{1,0:T(2,128)S(1)}, u32[]{:S(2)}, u32[]{:S(2)}) collective-permute-start(f32[2,2048]{1,0:T(2,128)S(1)} %add_add_fusion.1), channel_id=1, source_target_pairs={{0,24},{8,0},{16,8},{24,16},{1,25},{9,1},{17,9},{25,17},{2,26},{10... | collective-permute-start | bytes 49160 | tf_op jit(solution)/shard_map/ppermute | solution.py:467
  411.1 8.1 %collective-permute-start.38 = (bf16[384,256]{1,0:T(8,128)(2,1)S(1)}, bf16[384,256]{1,0:T(8,128)(2,1)S(1)}, u32[]{:S(2)}, u32[]{:S(2)}) collective-permute-start(bf16[384,256]{1,0:T(8,128)(2,1)S(1)} %add_convert_fusion.16.refs_4_), channel_id=1, source_target_pairs={{0,8},{8,0},{16,24},{24,16},{1,9},{9,1},{17,25},{25,17},{2,10},{10... | collective-permute-start | bytes 589832 | tf_op jit(solution)/shard_map/ppermute | solution.py:380
  411.2 8.5 %collective-permute-start.39 = (bf16[384,256]{1,0:T(8,128)(2,1)S(1)}, bf16[384,256]{1,0:T(8,128)(2,1)S(1)}, u32[]{:S(2)}, u32[]{:S(2)}) collective-permute-start(bf16[384,256]{1,0:T(8,128)(2,1)S(1)} %add_convert_fusion.16.refs_4_), channel_id=1, source_target_pairs={{0,16},{8,24},{16,0},{24,8},{1,17},{9,25},{17,1},{25,9},{2,18},{10... | collective-permute-start | bytes 589832 | tf_op jit(solution)/shard_map/ppermute | solution.py:380
  415.6 7.9 %collective-permute-start.36 = (bf16[384,256]{1,0:T(8,128)(2,1)S(1)}, bf16[384,256]{1,0:T(8,128)(2,1)S(1)}, u32[]{:S(2)}, u32[]{:S(2)}) collective-permute-start(bf16[384,256]{1,0:T(8,128)(2,1)S(1)} %add_convert_fusion.17.refs_1_), channel_id=1, source_target_pairs={{0,16},{8,24},{16,0},{24,8},{1,17},{9,25},{17,1},{25,9},{2,18},{10... | collective-permute-start | bytes 589832 | tf_op jit(solution)/shard_map/ppermute | solution.py:380
  417.1 23.0 %collective-permute-start.37 = (bf16[384,256]{1,0:T(8,128)(2,1)S(1)}, bf16[384,256]{1,0:T(8,128)(2,1)S(1)}, u32[]{:S(2)}, u32[]{:S(2)}) collective-permute-start(bf16[384,256]{1,0:T(8,128)(2,1)S(1)} %add_convert_fusion.17.refs_1_), channel_id=1, source_target_pairs={{0,8},{8,0},{16,24},{24,16},{1,9},{9,1},{17,25},{25,17},{2,10},{10... | collective-permute-start | bytes 589832 | tf_op jit(solution)/shard_map/ppermute | solution.py:380
  419.0 21.1 %collective-permute-start.34 = (bf16[640,256]{1,0:T(8,128)(2,1)S(1)}, bf16[640,256]{1,0:T(8,128)(2,1)S(1)}, u32[]{:S(2)}, u32[]{:S(2)}) collective-permute-start(bf16[640,256]{1,0:T(8,128)(2,1)S(1)} %add_convert_fusion.14.refs_4_), channel_id=1, source_target_pairs={{0,8},{8,0},{16,24},{24,16},{1,9},{9,1},{17,25},{25,17},{2,10},{10... | collective-permute-start | bytes 983048 | tf_op jit(solution)/shard_map/ppermute | solution.py:380
  419.1 21.0 %collective-permute-start.35 = (bf16[640,256]{1,0:T(8,128)(2,1)S(1)}, bf16[640,256]{1,0:T(8,128)(2,1)S(1)}, u32[]{:S(2)}, u32[]{:S(2)}) collective-permute-start(bf16[640,256]{1,0:T(8,128)(2,1)S(1)} %add_convert_fusion.14.refs_4_), channel_id=1, source_target_pairs={{0,16},{8,24},{16,0},{24,8},{1,17},{9,25},{17,1},{25,9},{2,18},{10... | collective-permute-start | bytes 983048 | tf_op jit(solution)/shard_map/ppermute | solution.py:380
  419.7 20.4 %collective-permute-start.32 = (bf16[640,256]{1,0:T(8,128)(2,1)S(1)}, bf16[640,256]{1,0:T(8,128)(2,1)S(1)}, u32[]{:S(2)}, u32[]{:S(2)}) collective-permute-start(bf16[640,256]{1,0:T(8,128)(2,1)S(1)} %add_convert_fusion.15.refs_1_), channel_id=1, source_target_pairs={{0,16},{8,24},{16,0},{24,8},{1,17},{9,25},{17,1},{25,9},{2,18},{10... | collective-permute-start | bytes 983048 | tf_op jit(solution)/shard_map/ppermute | solution.py:380
  423.5 16.7 %collective-permute-start.33 = (bf16[640,256]{1,0:T(8,128)(2,1)S(1)}, bf16[640,256]{1,0:T(8,128)(2,1)S(1)}, u32[]{:S(2)}, u32[]{:S(2)}) collective-permute-start(bf16[640,256]{1,0:T(8,128)(2,1)S(1)} %add_convert_fusion.15.refs_1_), channel_id=1, source_target_pairs={{0,8},{8,0},{16,24},{24,16},{1,9},{9,1},{17,25},{25,17},{2,10},{10... | collective-permute-start | bytes 983048 | tf_op jit(solution)/shard_map/ppermute | solution.py:380
  440.2 10.6 %collective-permute-start.43 = (bf16[640,256]{1,0:T(8,128)(2,1)S(1)}, bf16[640,256]{1,0:T(8,128)(2,1)S(1)}, u32[]{:S(2)}, u32[]{:S(2)}) collective-permute-start(bf16[640,256]{1,0:T(8,128)(2,1)S(1)} %collective-permute-done.32.refs_2_), channel_id=1, source_target_pairs={{0,8},{8,0},{16,24},{24,16},{1,9},{9,1},{17,25},{25,17},{2,10},{10... | collective-permute-start | bytes 983048 | tf_op jit(solution)/shard_map/ppermute | solution.py:380
  440.3 10.5 %collective-permute-start.44 = (bf16[640,256]{1,0:T(8,128)(2,1)S(1)}, bf16[640,256]{1,0:T(8,128)(2,1)S(1)}, u32[]{:S(2)}, u32[]{:S(2)}) collective-permute-start(bf16[640,256]{1,0:T(8,128)(2,1)S(1)} %collective-permute-done.34.refs_5_), channel_id=1, source_target_pairs={{0,16},{8,24},{16,0},{24,8},{1,17},{9,25},{17,1},{25,9},{2,18},{10... | collective-permute-start | bytes 983048 | tf_op jit(solution)/shard_map/ppermute | solution.py:380
  441.7 9.0 %collective-permute-start.45 = (bf16[384,256]{1,0:T(8,128)(2,1)S(1)}, bf16[384,256]{1,0:T(8,128)(2,1)S(1)}, u32[]{:S(2)}, u32[]{:S(2)}) collective-permute-start(bf16[384,256]{1,0:T(8,128)(2,1)S(1)} %collective-permute-done.36.refs_2_), channel_id=1, source_target_pairs={{0,8},{8,0},{16,24},{24,16},{1,9},{9,1},{17,25},{25,17},{2,10},{10... | collective-permute-start | bytes 589832 | tf_op jit(solution)/shard_map/ppermute | solution.py:380
  443.6 7.1 %collective-permute-start.46 = (bf16[384,256]{1,0:T(8,128)(2,1)S(1)}, bf16[384,256]{1,0:T(8,128)(2,1)S(1)}, u32[]{:S(2)}, u32[]{:S(2)}) collective-permute-start(bf16[384,256]{1,0:T(8,128)(2,1)S(1)} %collective-permute-done.38.refs_5_), channel_id=1, source_target_pairs={{0,16},{8,24},{16,0},{24,8},{1,17},{9,25},{17,1},{25,9},{2,18},{10... | collective-permute-start | bytes 589832 | tf_op jit(solution)/shard_map/ppermute | solution.py:380
  (93 other events, 617.5 us)
Sparse Core Ops, SparseCore 0:
  11.2 40.9 all-gather.4
  53.9 37.1 all-gather.6
  94.0 39.1 reduce-scatter.4
  136.7 37.4 all-gather.8
  195.6 39.2 reduce-scatter.6
  261.7 36.2 all-gather.10
  300.9 39.1 reduce-scatter.8
  343.0 40.2 reduce-scatter.10

commit v3 on v2

--- a/solution.py
+++ b/solution.py
@@ -17,7 +17,10 @@
 WIDE = jnp.float32
 NO_COST = pl.CostEstimate(flops=0, bytes_accessed=0, transcendentals=0)
 ROWS = 256
-COLUMNS = 512
+SPARE = 16
+ROOM = 60
+TILE = 512
+LOAD = 192
 
 
 def times(left, right):
@@ -61,12 +64,12 @@
     return jnp.where(y < 0.5, y * series, 1.0 - jnp.exp(-y))
 
 
-def row_positions(lengths_ref, base, rows, width):
+def row_positions(scalars_ref, base, rows, width):
     places = base + lax.broadcasted_iota(jnp.int32, (rows, width), 0)
     first = jnp.zeros_like(places)
     start = jnp.int32(0)
-    for at in range(lengths_ref.shape[1] - 1):
-        start = start + lengths_ref[0, at]
+    for at in range(4, scalars_ref.shape[1] - 1):
+        start = start + scalars_ref[0, at]
         first = jnp.where(places >= start, start, first)
     return places - first
 
@@ -78,11 +81,33 @@
     return carry, scale
 
 
-def forward_kernel(
-    lengths_ref, both_ref, taps_ref, rate_w_ref, inlet_w_ref, extra_ref,
-    mixed_ref, conv_ref, rate_ref, inlet_ref, state_ref, padded_ref,
-):
+def forward_kernel(scalars_ref, *refs):
+    sources, (taps_ref, rate_w_ref, inlet_w_ref, extra_ref), refs = refs[:3], refs[3:7], refs[7:]
+    out_refs, refs = refs[:7], refs[7:]
+    first_ref, branches_ref, block_ref = refs[:3]
+    partial_ref, mixed_ref, conv_ref, rate_ref, inlet_ref, state_ref, both_ref = refs[3:10]
+    padded_ref, in_sems, out_sems = refs[10:]
     count, width = mixed_ref.shape
+    features = first_ref.shape[1]
+    pieces = count // LOAD
+    arrivals = [
+        pltpu.make_async_copy(sources[1], branches_ref, in_sems.at[pieces]),
+        *[
+            pltpu.make_async_copy(sources[0].at[pl.ds(k * LOAD, LOAD), :], first_ref.at[pl.ds(k * LOAD, LOAD), :], in_sems.at[k])
+            for k in range(pieces)
+        ],
+        pltpu.make_async_copy(sources[2], block_ref, in_sems.at[pieces + 1]),
+    ]
+    for arrival in arrivals:
+        arrival.start()
+    arrivals[0].wait()
+    for k in range(pieces):
+        arrivals[1 + k].wait()
+        here = pl.ds(k * LOAD, LOAD)
+        both_ref[here, :] = times_transposed(first_ref[here, :], branches_ref[...])
+    departures = [pltpu.make_async_copy(both_ref, out_refs[6], out_sems.at[0])]
+    departures[0].start()
+
     padded_ref[pl.ds(0, SUB), :] = jnp.zeros((SUB, width), WIDE)
     padded_ref[pl.ds(SUB, count), :] = both_ref[:, width:]
     state_ref[pl.ds(0, SUB), :] = jnp.zeros((SUB, width), WIDE)
@@ -90,22 +115,36 @@
     bias, rate_b, inlet_b, soft = (extra_ref[k : k + 1, :] for k in range(4))
     lanes = lax.broadcasted_iota(jnp.int32, (CHUNK, width), 0) % SUB
 
-    def step(at, before):
+    def convolve(at, _):
         base = pl.multiple_of(at * CHUNK, SUB)
-        pos = row_positions(lengths_ref, base, CHUNK, width)
+        pos = row_positions(scalars_ref, base, CHUNK, width)
         window = padded_ref[pl.ds(base, CHUNK + SUB), :]
         total = bias + taps[0:1] * window[SUB:]
         for k in range(1, taps.shape[0]):
             moved = window[SUB - k : SUB - k + CHUNK]
             total = total + jnp.where(pos >= k, taps[k : k + 1] * moved, 0.0)
-        low = total.astype(LOW)
-        conv_ref[pl.ds(base, CHUNK), :] = low
-        rate = jax.nn.sigmoid(times(low, rate_w_ref[...]) + rate_b)
-        inlet = jax.nn.sigmoid(times(low, inlet_w_ref[...]) + inlet_b)
-        rate_ref[pl.ds(base, CHUNK), :] = rate
-        inlet_ref[pl.ds(base, CHUNK), :] = inlet
-        a, scale = gates(rate, inlet, soft, pos == 0)
-        b = scale * inlet * low.astype(WIDE)
+        conv_ref[pl.ds(base, CHUNK), :] = total.astype(LOW)
+        return _
+
+    lax.fori_loop(0, count // CHUNK, convolve, 0)
+
+    def open_gates(at, _):
+        here = pl.ds(pl.multiple_of(at * ROWS, ROWS), ROWS)
+        rate_ref[here, :] = jax.nn.sigmoid(times(conv_ref[here, :], rate_w_ref[...]) + rate_b)
+        inlet_ref[here, :] = jax.nn.sigmoid(times(conv_ref[here, :], inlet_w_ref[...]) + inlet_b)
+        return _
+
+    lax.fori_loop(0, count // ROWS, open_gates, 0)
+    for k, (ref, out_ref) in enumerate(((conv_ref, out_refs[2]), (rate_ref, out_refs[3]), (inlet_ref, out_refs[4]))):
+        departures.append(pltpu.make_async_copy(ref, out_ref, out_sems.at[1 + k]))
+        departures[-1].start()
+
+    def step(at, before):
+        base = pl.multiple_of(at * CHUNK, SUB)
+        here = pl.ds(base, CHUNK)
+        pos = row_positions(scalars_ref, base, CHUNK, width)
+        a, scale = gates(rate_ref[here, :], inlet_ref[here, :], soft, pos == 0)
+        b = scale * inlet_ref[here, :] * conv_ref[here, :].astype(WIDE)
         for k in (1, 2, 4):
             inside = lanes >= k
             b = b + jnp.where(inside, a * pltpu.roll(b, k, 0), 0.0)
@@ -118,19 +157,35 @@
             tiles.append(tile)
         state = jnp.concatenate(tiles, axis=0)
         state_ref[pl.ds(base + SUB, CHUNK), :] = state
-        mixed_ref[pl.ds(base, CHUNK), :] = (state * gelu(both_ref[pl.ds(base, CHUNK), :width])).astype(LOW)
+        mixed_ref[here, :] = (state * gelu(both_ref[here, :width])).astype(LOW)
         return before
 
     lax.fori_loop(0, count // CHUNK, step, jnp.zeros((1, width), WIDE))
-
-
-def backward_kernel(
-    heads, lengths_ref, middle_ref, block_ref, first_ref, branches_ref, mixed_ref,
-    both_ref, conv_ref, rate_ref, inlet_ref, state_ref,
-    taps_ref, rate_w_ref, inlet_w_ref, extra_ref,
-    partial_ref, block_grad_ref, branch_grad_ref, gain_ref,
-    grad_ref, back_ref, padded_ref, rate_low_ref, inlet_low_ref, stacked_ref,
-):
+    for k, (ref, out_ref) in enumerate(((mixed_ref, out_refs[1]), (state_ref, out_refs[5]))):
+        departures.append(pltpu.make_async_copy(ref, out_ref, out_sems.at[4 + k]))
+        departures[-1].start()
+    arrivals[-1].wait()
+    for k in range(features // TILE):
+        here = pl.ds(k * TILE, TILE)
+        partial_ref[:, here] = times(mixed_ref[...], block_ref[:, here]).astype(LOW)
+        departures.append(pltpu.make_async_copy(partial_ref.at[:, here], out_refs[0].at[:, here], out_sems.at[6 + k]))
+        departures[-1].start()
+    for departure in departures:
+        departure.wait()
+
+
+def backward_kernel(heads, owners, scalars_ref, *refs):
+    sources, small_refs, refs = refs[:10], refs[10:16], refs[16:]
+    partial_out_ref, quarter_out_refs, held, refs = refs[0], refs[1:5], refs[5:15], refs[15:]
+    grad_ref, back_ref, padded_ref, rate_low_ref, inlet_low_ref, stacked_ref, strips_ref = refs[:7]
+    partials_ref, quarters_ref, in_sems, out_sems = refs[7:]
+    taps_ref, rate_w_ref, inlet_w_ref, extra_ref, first_gain_ref, second_grad_ref = small_refs
+    middle_ref, block_ref, both_ref, conv_ref, rate_ref, inlet_ref, state_ref, mixed_ref, first_ref, branches_ref = held
+    arrivals = [pltpu.make_async_copy(*pair, in_sems.at[k]) for k, pair in enumerate(zip(sources, held))]
+    for arrival in arrivals:
+        arrival.start()
+    for arrival in arrivals[:2]:
+        arrival.wait()
     count, width = grad_ref.shape
     features = middle_ref.shape[1]
 
@@ -140,6 +195,8 @@
         return _
 
     lax.fori_loop(0, count // ROWS, spread_rows, 0)
+    for arrival in arrivals[2:7]:
+        arrival.wait()
     padded_ref[pl.ds(0, SUB), :] = jnp.zeros((SUB, width), WIDE)
     padded_ref[pl.ds(SUB, count), :] = both_ref[:, width:]
     taps = taps_ref[...]
@@ -156,7 +213,7 @@
         after, late, beyond, sums = held
         base = pl.multiple_of((steps - 1 - turn) * CHUNK, SUB)
         here = pl.ds(base, CHUNK)
-        wide_pos = row_positions(lengths_ref, base, CHUNK + SUB, width)
+        wide_pos = row_positions(scalars_ref, base, CHUNK + SUB, width)
         pos = wide_pos[:CHUNK]
         fresh = pos == 0
         grad = grad_ref[here, :]
@@ -214,16 +271,6 @@
     sums = lax.fori_loop(0, steps, step, (zero, zero, jnp.zeros((SUB, width), WIDE), start))[3]
     rows = list(sums)
     rows[3] = -slope * rows[3]
-    def spread_columns(turn, _):
-        here = pl.ds(pl.multiple_of(turn * COLUMNS, COLUMNS), COLUMNS)
-        block_grad_ref[:width, here] = transposed_times(mixed_ref[...], middle_ref[:, here]).astype(LOW)
-        branch_grad = transposed_times(back_ref[...], first_ref[:, here])
-        branch_grad_ref[:, here] = branch_grad.astype(LOW)
-        gain_ref[:, here] = column(branch_grad * branches_ref[:, here].astype(WIDE))
-        partial_ref[:, here] = times(back_ref[...], branches_ref[:, here]).astype(LOW)
-        return _
-
-    lax.fori_loop(0, features // COLUMNS, spread_columns, 0)
     size = width // heads
     strips, depth = strip_shape(features, heads, size, len(rows))
     stacked_ref[...] = jnp.zeros_like(stacked_ref)
@@ -237,9 +284,47 @@
     small = jnp.concatenate(rows, axis=0)
     for h in range(heads):
         stacked_ref[pl.ds(block * size + h * SUB, len(rows)), :] = small[:, h * size : (h + 1) * size]
-    block_grad_ref[pl.ds(width, depth), :] = jnp.zeros((depth, features), LOW)
+    strips_ref[...] = jnp.zeros_like(strips_ref)
     for k in range(strips):
-        block_grad_ref[pl.ds(width, depth), k * size : (k + 1) * size] = stacked_ref[pl.ds(k * depth, depth), :].astype(LOW)
+        strips_ref[:, k * size : (k + 1) * size] = stacked_ref[pl.ds(k * depth, depth), :].astype(LOW)
+
+    for arrival in arrivals[7:]:
+        arrival.wait()
+    share = count // owners
+    quarter = features // 4
+    departures = []
+    for slot in range(4):
+        if slot >= 2:
+            for departure in departures[slot - 2]:
+                departure.wait()
+        partial_ref, quarter_ref = partials_ref.at[slot % 2], quarters_ref.at[slot % 2]
+        here = pl.ds(pl.multiple_of(scalars_ref[0, slot] * quarter, quarter), quarter)
+        branch_grad = transposed_times(back_ref[...], first_ref[:, here])
+        quarter_ref[: 2 * width, :] = branch_grad.astype(LOW)
+        quarter_ref[2 * width : 3 * width, :] = transposed_times(mixed_ref[...], middle_ref[:, here]).astype(LOW)
+        quarter_ref[3 * width :, :] = strips_ref[:, here]
+        gain = column(branch_grad * branches_ref[:, here].astype(WIDE)) / first_gain_ref[:, here]
+        tops = []
+        for value in (gain, second_grad_ref[:, here]):
+            top = value.astype(LOW).astype(WIDE)
+            tops += [top, value - top]
+        tops = jnp.concatenate(tops + [jnp.zeros((SPARE - len(tops), quarter), WIDE)], axis=0).astype(LOW)
+        partial = times(back_ref[...], branches_ref[:, here]).astype(LOW)
+        for k in range(owners):
+            base = k * (share + SPARE)
+            partial_ref[base : base + share, :] = partial[k * share : (k + 1) * share]
+            partial_ref[base + share : base + share + SPARE, :] = tops
+        departures.append(
+            [
+                pltpu.make_async_copy(quarter_ref, quarter_out_refs[slot], out_sems.at[2 * slot]),
+                pltpu.make_async_copy(partial_ref, partial_out_ref.at[:, here], out_sems.at[2 * slot + 1]),
+            ]
+        )
+        for departure in departures[slot]:
+            departure.start()
+    for slot in (2, 3):
+        for departure in departures[slot]:
+            departure.wait()
 
 
 def strip_shape(features, heads, size, small):
@@ -248,12 +333,29 @@
     return strips, -(-rows // (strips * 2 * SUB)) * 2 * SUB
 
 
-def unpack_strips(packed, heads, size, small):
-    strips, depth = strip_shape(packed.shape[1], heads, size, small)
-    stacked = jnp.concatenate([packed[:, k * size : (k + 1) * size] for k in range(strips)])
-    square = stacked[: 2 * heads * size].reshape(2, heads, size, size)
-    parts = [stacked[2 * heads * size + h * SUB :][:small] for h in range(heads)]
-    return square, jnp.concatenate(parts, axis=1)
+def unpack_kernel(heads, strips, packed_ref, square_ref, small_ref, stacked_ref):
+    depth, size = packed_ref.shape[0], square_ref.shape[-1]
+    for k in range(strips):
+        stacked_ref[pl.ds(k * depth, depth), :] = packed_ref[:, k * size : (k + 1) * size]
+    for k in range(2 * heads):
+        square_ref[k] = stacked_ref[pl.ds(k * size, size), :]
+    small_ref[...] = jnp.concatenate(
+        [stacked_ref[pl.ds(2 * heads * size + h * SUB, SUB), :] for h in range(heads)], axis=1
+    )
+
+
+def unpack_strips(packed, heads, size):
+    strips, depth = strip_shape(packed.shape[1], heads, size, SUB)
+    return pl.pallas_call(
+        lambda *refs: unpack_kernel(heads, strips, *refs),
+        out_shape=[
+            jax.ShapeDtypeStruct((2 * heads, size, size), WIDE),
+            jax.ShapeDtypeStruct((SUB, heads * size), WIDE),
+        ],
+        scratch_shapes=[pltpu.VMEM((strips * depth, size), WIDE)],
+        compiler_params=pltpu.CompilerParams(vmem_limit_bytes=16 * 1024 * 1024),
+        cost_estimate=NO_COST,
+    )(packed)
 
 
 def in_vmem():
@@ -272,44 +374,196 @@
     )(*operands)
 
 
-def forward_mix(lengths, both, taps, rate_w, inlet_w, extra):
-    count, width = both.shape[0], both.shape[1] // 2
-    wide = jax.ShapeDtypeStruct((count, width), WIDE)
-    low = jax.ShapeDtypeStruct((count, width), LOW)
-    state = jax.ShapeDtypeStruct((count + SUB, width), WIDE)
-    return run_kernel(
+def forward_mix(scalars, first, branches, block, taps, rate_w, inlet_w, extra):
+    count, features = first.shape
+    width = block.shape[0]
+    made = [
+        ((count, features), LOW),
+        ((count, width), LOW),
+        ((count, width), LOW),
+        ((count, width), WIDE),
+        ((count, width), WIDE),
+        ((count + SUB, width), WIDE),
+        ((count, 2 * width), WIDE),
+    ]
+    anywhere = pl.BlockSpec(memory_space=pl.ANY)
+    return pl.pallas_call(
         forward_kernel,
-        [low, low, wide, wide, state],
-        [pltpu.VMEM((count + SUB, width), WIDE)],
-        (lengths, both, taps, rate_w, inlet_w, extra),
-        20,
-    )
-
-
-def backward_mix(heads, lengths, middle, block, first, branches, mixed, both, conv, *others):
-    count, width = mixed.shape
-    features = middle.shape[1]
-    narrow = pltpu.VMEM((count, width), LOW)
+        in_specs=[pl.BlockSpec(memory_space=pltpu.SMEM)] + [anywhere] * 3 + [in_vmem()] * 4,
+        out_specs=[anywhere] * len(made),
+        out_shape=[jax.ShapeDtypeStruct(*one) for one in made],
+        scratch_shapes=[pltpu.VMEM(array.shape, array.dtype) for array in (first, branches, block)]
+        + [pltpu.VMEM(*one) for one in made]
+        + [
+            pltpu.VMEM((count + SUB, width), WIDE),
+            pltpu.SemaphoreType.DMA((count // LOAD + 2,)),
+            pltpu.SemaphoreType.DMA((6 + features // TILE,)),
+        ],
+        compiler_params=pltpu.CompilerParams(vmem_limit_bytes=ROOM * 1024 * 1024),
+        cost_estimate=NO_COST,
+    )(scalars, first, branches, block, taps, rate_w, inlet_w, extra)
+
+
+def backward_mix(heads, owners, scalars, large, small):
+    middle, block = large[:2]
+    count, features = middle.shape
+    width = block.shape[0]
     size = width // heads
     strips, depth = strip_shape(features, heads, size, SUB)
-    return run_kernel(
-        lambda *refs: backward_kernel(heads, *refs),
-        [
-            jax.ShapeDtypeStruct((count, features), LOW),
-            jax.ShapeDtypeStruct((width + depth, features), LOW),
-            jax.ShapeDtypeStruct((2 * width, features), LOW),
-            jax.ShapeDtypeStruct((1, features), WIDE),
-        ],
-        [
+    rows, lines = count + owners * SPARE, 3 * width + depth
+    narrow = pltpu.VMEM((count, width), LOW)
+    anywhere = pl.BlockSpec(memory_space=pl.ANY)
+    return pl.pallas_call(
+        lambda *refs: backward_kernel(heads, owners, *refs),
+        in_specs=[pl.BlockSpec(memory_space=pltpu.SMEM)] + [anywhere] * len(large) + [in_vmem()] * len(small),
+        out_specs=[anywhere] * 5,
+        out_shape=[jax.ShapeDtypeStruct((rows, features), LOW)] + [jax.ShapeDtypeStruct((lines, features // 4), LOW)] * 4,
+        scratch_shapes=[pltpu.VMEM(array.shape, array.dtype) for array in large]
+        + [
             pltpu.VMEM((count, width), WIDE),
             pltpu.VMEM((count, 2 * width), LOW),
             pltpu.VMEM((count + SUB, width), WIDE),
             narrow,
             narrow,
             pltpu.VMEM((strips * depth, size), WIDE),
+            pltpu.VMEM((depth, features), LOW),
+            pltpu.VMEM((2, rows, features // 4), LOW),
+            pltpu.VMEM((2, lines, features // 4), LOW),
+            pltpu.SemaphoreType.DMA((len(large),)),
+            pltpu.SemaphoreType.DMA((8,)),
         ],
-        (lengths, middle, block, first, branches, mixed, both, conv) + others,
-        44,
+        compiler_params=pltpu.CompilerParams(vmem_limit_bytes=ROOM * 1024 * 1024),
+        cost_estimate=NO_COST,
+    )(scalars, *large, *small)
+
+
+def call_blocks(body, grid, spots, inputs, outputs, operands, room):
+    return pl.pallas_call(
+        body,
+        grid_spec=pltpu.PrefetchScalarGridSpec(
+            num_scalar_prefetch=1,
+            grid=(grid,),
+            in_specs=[pl.BlockSpec(shape, index) for shape, index in inputs],
+            out_specs=[pl.BlockSpec(shape, index) for _, shape, index in outputs],
+        ),
+        out_shape=[made for made, _, _ in outputs],
+        compiler_params=pltpu.CompilerParams(vmem_limit_bytes=room * 1024 * 1024),
+        cost_estimate=NO_COST,
+    )(spots, *operands)
+
+
+def whole(_, at):
+    return (0, 0)
+
+
+def across(k, at):
+    return (0, k)
+
+
+def down(k, at):
+    return (k, 0)
+
+
+def across_spot(k, at):
+    return (0, at[k])
+
+
+def down_spot(k, at):
+    return (at[k], 0)
+
+
+def second_kernel(_, gate_low_ref, up_low_ref, gate_w_ref, up_w_ref, out_ref):
+    total = times_transposed(gate_low_ref[...], gate_w_ref[...]) + times_transposed(up_low_ref[...], up_w_ref[...])
+    out_ref[...] = total.astype(LOW)
+
+
+def second_partial(gate_low, up_low, gate_weight, up_weight):
+    count, units = gate_low.shape
+    features = gate_weight.shape[0]
+    return call_blocks(
+        second_kernel,
+        features // TILE,
+        jnp.zeros((1,), jnp.int32),
+        [((count, units), whole)] * 2 + [((TILE, units), down)] * 2,
+        [(jax.ShapeDtypeStruct((count, features), LOW), (count, TILE), across)],
+        (gate_low, up_low, gate_weight, up_weight),
+        ROOM,
+    )[0]
+
+
+def gradient_kernel(_, left_ref, right_ref, out_ref):
+    out_ref[...] = transposed_times(left_ref[...], right_ref[...]).astype(LOW)
+
+
+def gradient_half(left, right, which):
+    count, features = left.shape
+    units = right.shape[1]
+    block = features // 4
+    spots = jnp.stack([2 * which, 2 * which + 1]).astype(jnp.int32)
+    return call_blocks(
+        gradient_kernel,
+        2,
+        spots,
+        [((count, block), across_spot), ((count, units), whole)],
+        [(jax.ShapeDtypeStruct((2 * block, units), LOW), (block, units), down)],
+        (left, right),
+        ROOM,
+    )[0]
+
+
+def norm_kernel(_, start_ref, added_ref, gain_ref, *out_refs):
+    values = start_ref[...].astype(WIDE)
+    if len(out_refs) == 2:
+        values = values + added_ref[...].astype(WIDE)
+        out_refs[1][...] = values
+    out_refs[0][...] = (values * norm_scale(values) * gain_ref[...]).astype(LOW)
+
+
+def normed(start, gain, added=None):
+    rows, features = start.shape
+    block = (rows // 2, features)
+    outs = [(jax.ShapeDtypeStruct((rows, features), kind), block, down) for kind in (LOW, WIDE)]
+    return call_blocks(
+        norm_kernel,
+        2,
+        jnp.zeros((1,), jnp.int32),
+        [(block, down), (block, down), ((1, features), whole)],
+        outs if added is not None else outs[:1],
+        (start, start if added is None else added, gain[None]),
+        16,
+    )
+
+
+def norm_back_kernel(_, start_ref, grad_ref, added_ref, gain_ref, low_ref, total_ref, gain_grad_ref):
+    values, grad = start_ref[...], grad_ref[...].astype(WIDE)
+    scale = norm_scale(values)
+    total = added_ref[...].astype(WIDE) + norm_back(values, scale, gain_ref[...], grad)
+    total_ref[...] = total
+    low_ref[...] = total.astype(LOW)
+    part = jnp.sum(grad * values * scale, axis=0, keepdims=True)
+
+    @pl.when(pl.program_id(0) == 0)
+    def _():
+        gain_grad_ref[...] = part
+
+    @pl.when(pl.program_id(0) > 0)
+    def _():
+        gain_grad_ref[...] += part
+
+
+def normed_back(start, grad, added, gain):
+    rows, features = start.shape
+    block = (rows // 2, features)
+    line = (1, features)
+    return call_blocks(
+        norm_back_kernel,
+        2,
+        jnp.zeros((1,), jnp.int32),
+        [(block, down)] * 3 + [(line, whole)],
+        [(jax.ShapeDtypeStruct((rows, features), kind), block, down) for kind in (LOW, WIDE)]
+        + [(jax.ShapeDtypeStruct(line, WIDE), line, whole)],
+        (start, grad, added, gain[None]),
+        16,
     )
 
 
@@ -322,7 +576,7 @@
 
 
 def sum_rows(values):
-    return lax.psum_scatter(values.astype(LOW), "mp", scatter_dimension=0, tiled=True).astype(WIDE)
+    return lax.psum_scatter(values.astype(LOW), "mp", scatter_dimension=0, tiled=True)
 
 
 def all_rows(values):
@@ -349,7 +603,7 @@
         jax.ShapeDtypeStruct((r * total, columns) if axis == 0 else (r, columns * total), kind) for r in splits
     ]
     spot = (lambda k, at: (at[k], 0)) if axis == 0 else (lambda k, at: (0, at[k]))
-    room = rows * columns * (2 * 2 * count + 4 * 2) + 4 * 1024 * 1024
+    room = rows * columns * (2 * 2 * count + 4 * 2) + 3 * 1024 * 1024
     return pl.pallas_call(
         lambda *refs: place_kernel(count, len(onto), splits, *refs),
         grid_spec=pltpu.PrefetchScalarGridSpec(
@@ -366,53 +620,56 @@
     )(jnp.stack(spots).astype(jnp.int32), *pieces, *onto)
 
 
+def dp_bits():
+    return lax.axis_size("dp").bit_length() - 1
+
+
+def swap(values, bit):
+    count = lax.axis_size("dp")
+    return lax.ppermute(values, "dp", [(i, i ^ (1 << bit)) for i in range(count)])
+
+
+def order_of(turn):
+    bits = dp_bits()
+    return [(turn + k) % bits for k in range(bits)]
+
+
+def upper_of(bit):
+    return (lax.axis_index("dp") >> bit) & 1
+
+
+def quarter_spots():
+    left, right = (upper_of(order_of(turn)[0]) for turn in range(2))
+    return jnp.stack([1 - left, left, 3 - right, 2 + right]).astype(jnp.int32)
+
+
 def halves(values, axis):
     size = values.shape[axis] // 2
     return lax.slice_in_dim(values, 0, size, axis=axis), lax.slice_in_dim(values, size, 2 * size, axis=axis)
 
 
-def dp_bits():
-    return lax.axis_size("dp").bit_length() - 1
-
-
-def swap(values, bit):
-    count = lax.axis_size("dp")
-    return lax.ppermute(values, "dp", [(i, i ^ (1 << bit)) for i in range(count)])
-
-
-def order_of(turn):
-    bits = dp_bits()
-    return [(turn + k) % bits for k in range(bits)]
-
-
 def split_for(values, axis, bit):
     first, second = halves(values, axis)
-    upper = ((lax.axis_index("dp") >> bit) & 1) == 1
+    upper = upper_of(bit) == 1
     return jnp.where(upper, first, second), jnp.where(upper, second, first)
 
 
-def join(kept, got):
-    return (kept.astype(WIDE) + got.astype(WIDE)).astype(LOW)
-
-
 class Part:
-    def __init__(self, values, axis, turn):
+    def __init__(self, send, kept, axis, turn):
+        self.send, self.kept = send, kept
         self.axis, self.order = axis, order_of(turn)
         self.step = 0
-        self.load(values)
-
-    def load(self, values):
-        if self.step < len(self.order):
-            self.send, self.kept = split_for(values, self.axis, self.order[self.step])
-        else:
-            self.pieces = {0: values}
 
     def reduce(self):
         return swap(self.send, self.order[self.step])
 
     def land(self, got):
         self.step += 1
-        self.load(join(self.kept, got))
+        total = (self.kept.astype(WIDE) + got.astype(WIDE)).astype(LOW)
+        if self.step < len(self.order):
+            self.send, self.kept = split_for(total, self.axis, self.order[self.step])
+        else:
+            self.pieces = {0: total}
 
     def forwards(self, level):
         made = []
@@ -432,12 +689,14 @@
 
 def exchange(reducing=(), gathered=(), extras=()):
     gots = [part.reduce() for part in reducing]
-    made = lax.optimization_barrier((*gots, *[piece for _, _, piece in gathered], *extras))
-    for part, got in zip(reducing, made):
+    kepts = [part.kept for part in reducing]
+    made = lax.optimization_barrier((*gots, *[piece for _, _, piece in gathered], *extras, *kepts))
+    for part, got, kept in zip(reducing, made, made[len(made) - len(kepts) :]):
+        part.kept = kept
         part.land(got)
     for (part, mask, _), piece in zip(gathered, made[len(gots) :]):
         part.pieces[mask] = piece
-    return made[len(gots) + len(gathered) :]
+    return made[len(gots) + len(gathered) : len(made) - len(kepts)]
 
 
 def reduce_fully(parts):
@@ -458,13 +717,17 @@
     return place(blocks, spots, len(parts) * count, axis, splits, WIDE, onto)
 
 
-def column_parts(values):
-    return [Part(half, 1, turn) for turn, half in enumerate(halves(values, 1))]
-
-
-def shifts_of(values, axis, shifts):
-    count = lax.axis_size(axis)
-    return [lax.ppermute(values, axis, [(i, (i + shift) % count) for i in range(count)]) for shift in shifts]
+def column_parts(quarters):
+    return [Part(quarters[2 * turn], quarters[2 * turn + 1], 1, turn) for turn in range(2)]
+
+
+def next_chip(values, step):
+    count = lax.axis_size("mp")
+    return lax.ppermute(values, "mp", [(i, (i + 2 * step) % count) for i in range(count)])
+
+
+def other_core(values):
+    return lax.ppermute(values, "mp", [(i, i ^ 1) for i in range(lax.axis_size("mp"))])
 
 
 def tie(values, *others):
@@ -495,10 +758,10 @@
     width = decay_param.shape[0]
     features = tokens.shape[1]
     taps_count = conv_weight.shape[0]
+    own_count = tokens.shape[0]
     own_input = tokens.astype(WIDE)
     own_grad = out_grad.astype(WIDE)
-    first_scale = norm_scale(own_input)
-    first_rows = all_rows((own_input * first_scale * first_gain).astype(LOW))
+    first_rows = all_rows(normed(tokens, first_gain)[0])
     soft = DECAY_SCALE * jax.nn.softplus(decay_param)
     slope = DECAY_SCALE * jax.nn.sigmoid(decay_param)
     extra = jnp.stack([conv_bias, rate_bias, inlet_bias, soft, slope])
@@ -507,13 +770,39 @@
     branches = jnp.concatenate([branch_gate.T, branch_input.T])
 
     first_rows = tie(first_rows, rate_w, inlet_w, extra, branches)
-    both = times_transposed(first_rows, branches)
-    grad_rows = all_rows(tie(out_grad, first_rows))
-    mixed, conv, rate, inlet, state = forward_mix(lengths, both, conv_weight, rate_w, inlet_w, extra)
-    block_partial = tie(times(mixed, block_out), grad_rows)
-    own_middle = own_input + sum_rows(block_partial)
-    second_scale = norm_scale(own_middle)
-    second_rows = all_rows((own_middle * second_scale * second_gain).astype(LOW))
+    spots = quarter_spots()
+    scalars = jnp.concatenate([spots, lengths[0]])[None]
+    block_partial, mixed, conv, rate, inlet, state, both = forward_mix(
+        scalars, first_rows, branches, block_out, conv_weight, rate_w, inlet_w, extra
+    )
+    chips = lax.axis_size("mp") // 2
+    onward, backward = {0: tie(out_grad, first_rows)}, {}
+    onward[1], backward[1] = next_chip(onward[0], 1), next_chip(onward[0], -1)
+    block_partial, onward[1], backward[1] = lax.optimization_barrier((block_partial, onward[1], backward[1]))
+
+    block_sum = sum_rows(block_partial)
+    for hop in range(2, chips // 2 + 1):
+        onward[hop] = next_chip(onward[hop - 1], 1)
+        if 2 * hop < chips:
+            backward[hop] = next_chip(backward[hop - 1], -1)
+    shards = {hop: piece for hop, piece in onward.items()} | {-hop: piece for hop, piece in backward.items()}
+    near_hops = [hop for hop in shards if abs(hop) < 2]
+    far_hops = [hop for hop in shards if abs(hop) >= 2]
+    made = lax.optimization_barrier(
+        (block_sum, *[shards[hop] for hop in far_hops], *[other_core(shards[hop]) for hop in near_hops])
+    )
+    block_sum = made[0]
+    shards |= dict(zip(far_hops, made[1:]))
+    others = dict(zip(near_hops, made[1 + len(far_hops) :])) | {hop: other_core(shards[hop]) for hop in far_hops}
+    own_second, own_middle = normed(tokens, second_gain, block_sum)
+    second_rows = all_rows(own_second)
+    me = lax.axis_index("mp")
+    blocks, places = [], []
+    for hop in shards:
+        base = 2 * ((me // 2 + chips - hop) % chips)
+        blocks += [shards[hop], others[hop]]
+        places += [base + me % 2, base + 1 - me % 2]
+    (grad_rows,) = place(blocks, places, 2 * chips, 0, None, LOW)
     d_hidden = times_transposed(grad_rows, down_weight)
     second_rows, d_hidden = lax.optimization_barrier((second_rows, d_hidden))
     gate_act = times(second_rows, gate_weight)
@@ -523,67 +812,77 @@
     gate_low = (d_hidden * up_act * bend).astype(LOW)
     up_low = (d_hidden * value).astype(LOW)
 
-    down_parts = column_parts(transposed_times(hidden, grad_rows).astype(LOW))
-    late_gate = tie(gate_low, *[part.send for part in down_parts])
-    second_input = sum_rows(times_transposed(late_gate, gate_weight) + times_transposed(up_low, up_weight))
-    gate_part = Part(transposed_times(second_rows, gate_low).astype(LOW), 0, 0)
-    up_part = Part(transposed_times(second_rows, up_low).astype(LOW), 0, 1)
-    wide_parts = [gate_part, up_part]
+    down_parts = []
+    for turn, half in enumerate(halves(transposed_times(hidden, grad_rows).astype(LOW), 1)):
+        down_parts.append(Part(*split_for(half, 1, order_of(turn)[0]), 1, turn))
+    late_rows = tie(second_rows, *[part.send for part in down_parts])
+    uppers = [upper_of(order_of(turn)[0]) for turn in range(2)]
+    gate_send = gradient_half(late_rows, gate_low, 1 - uppers[0])
+    up_send = gradient_half(tie(late_rows, gate_send), up_low, 1 - uppers[1])
+    partial = second_partial(tie(gate_low, gate_send, up_send), up_low, gate_weight, up_weight)
+    partial, gate_send, up_send = exchange(down_parts, extras=(partial, gate_send, up_send))
+
+    second_input = sum_rows(partial)
+    late_rows = tie(second_rows, partial)
+    wide_parts = [
+        Part(gate_send, gradient_half(late_rows, gate_low, uppers[0]), 0, 0),
+        Part(up_send, gradient_half(late_rows, up_low, uppers[1]), 0, 1),
+    ]
     mlp = down_parts + wide_parts
-
-    exchange(down_parts)
-    (second_input,) = exchange(down_parts + wide_parts, extras=(second_input,))
-    middle_grad = own_grad + norm_back(own_middle, second_scale, second_gain, second_input)
-    second_gain_grad = jnp.sum(second_input * own_middle * second_scale, axis=0)
-    middle_rows = all_rows(middle_grad.astype(LOW))
+    middle_low, middle_grad, second_gain_grad = normed_back(own_middle, second_input, out_grad, second_gain)
+    made = exchange(down_parts + wide_parts, extras=(middle_low, middle_grad, second_gain_grad))
+    middle_low, middle_grad, second_gain_grad = made
+    middle_rows = all_rows(middle_low)
 
     reduce_fully(down_parts)
-    out_partial = times(tie(hidden, second_input), down_weight)
+    out_partial = times(tie(hidden, middle_low), down_weight)
     middle_rows, out_partial = exchange(wide_parts, start_gather(down_parts, 1), (middle_rows, out_partial))
     out_sum = sum_rows(out_partial)
 
     reduce_fully(wide_parts)
+    owners = lax.axis_size("mp")
     made = backward_mix(
-        heads, lengths, middle_rows, block_out, first_rows, branches, mixed,
-        both, conv, rate, inlet, state, conv_weight, rate_w, inlet_w, extra,
+        heads,
+        owners,
+        scalars,
+        (middle_rows, block_out, both, conv, rate, inlet, state, mixed, first_rows, branches),
+        (conv_weight, rate_w, inlet_w, extra, first_gain[None], second_gain_grad),
     )
-    first_partial, block_grad, branch_grad, gain = exchange(gathered=start_gather(wide_parts, 1), extras=made)
+    first_partial, *quarters = exchange(gathered=start_gather(wide_parts, 1), extras=made)
     first_input = sum_rows(tie(first_partial, out_sum))
-    output = (own_middle + out_sum).astype(LOW)
-    gains = jnp.concatenate([gain / first_gain, second_gain_grad[None]])
-
-    branch_parts = column_parts(branch_grad)
-    block_parts = column_parts(block_grad)
-    late = branch_parts + block_parts
+    output = (own_middle + out_sum.astype(WIDE)).astype(LOW)
+
+    late = column_parts(quarters)
     wide_rest = start_gather(wide_parts, 2)
-    cores = lax.axis_size("mp")
-    (other,) = exchange(late, extras=[lax.ppermute(gains, "mp", [(i, i ^ 1) for i in range(cores)])])
-    gains = gains + other
-    others = shifts_of(gains, "mp", range(2, cores, 2))
+    exchange(late)
     down_rest = start_gather(down_parts, 2)
-    first_input, output, *others = exchange(late, wide_rest + down_rest, (first_input, output, *others))
+    first_input, output = exchange(late, wide_rest + down_rest, (first_input, output))
     gather_fully(mlp, 3)
     reduce_fully(late)
-    gains = gains + sum(others)
-    others = shifts_of(gains, "dp", range(1, lax.axis_size("dp")))
-    input_grad = middle_grad + norm_back(own_input, first_scale, first_gain, first_input)
-    (gate_grad,) = finish([gate_part], 0)
-    (up_grad,) = finish([up_part], 0)
+    first_input = first_input.astype(WIDE)
+    first_scale = norm_scale(own_input)
+    sums = first_input[own_count:]
+    gains = jnp.stack([sums[0] + sums[1], sums[2] + sums[3]])
+    input_grad = middle_grad + norm_back(own_input, first_scale, first_gain, first_input[:own_count])
+    (gate_grad,) = finish([wide_parts[0]], 0)
+    (up_grad,) = finish([wide_parts[1]], 0)
     (down_grad,) = finish(down_parts, 1)
-    made = exchange(gathered=start_gather(late, 1), extras=(gate_grad, up_grad, down_grad, input_grad, *others))
-    gate_grad, up_grad, down_grad, input_grad = made[:4]
-    gains = gains + sum(made[4:])
+    gate_grad, down_grad, input_grad, other = exchange(
+        gathered=start_gather(late, 1), extras=(gate_grad, down_grad, input_grad, swap(gains, 0))
+    )
+    gains = gains + other
     own = [0] + [1 << bit for bit in range(dp_bits())]
-    depth = block_grad.shape[0] - width
-    halfway = finish(branch_parts, 1, (width, width), own)
-    block_halfway = finish(block_parts, 1, (width, depth), own)
-    made = exchange(gathered=start_gather(late, 2), extras=(gains, *halfway, *block_halfway))
+    splits = (width, width, width, quarters[0].shape[0] - 3 * width)
+    halfway = finish(late, 1, splits, own)
+    made = exchange(gathered=start_gather(late, 2), extras=(swap(gains, 1), up_grad, *halfway))
     gather_fully(late, 3)
-    gains = made[0]
-    rest = [mask for mask in branch_parts[0].pieces if mask not in own]
-    branch_gate_grad, branch_input_grad = finish(branch_parts, 1, (width, width), rest, made[1:3])
-    block_grad, packed = finish(block_parts, 1, (width, depth), rest, made[3:5])
-    square, small = unpack_strips(packed, heads, width // heads, 4 + taps_count)
+    gains, up_grad = gains + made[0], made[1]
+    for bit in range(2, dp_bits()):
+        gains = gains + swap(gains, bit)
+    rest = [mask for mask in late[0].pieces if mask not in own]
+    branch_gate_grad, branch_input_grad, block_grad, packed = finish(late, 1, splits, rest, made[2:])
+    square, small = unpack_strips(packed, heads, width // heads)
+    square = square.reshape(2, heads, *square.shape[1:])
     return (
         output,
         input_grad,

time: 471 us -> 450 us (0.955)
  Pallas kernels: 56.9 us -> 101 us
  matrix products: 45.7 us -> 19.1 us
  waiting for transfers between devices: 207 us -> 181 us
  other arithmetic: 58.9 us -> 44.9 us
    pallas_call x2 -> x11, Pallas kernels: 34.2 us -> 73.1 us  [the longest x8 31 us: call_blocks(): pl.pallas_call(body, grid_spec=pltpu.PrefetchScalarGridSpec(num_scalar_pr...]
    reduce_scatter x4, waiting for transfers between devices: 54.6 us -> 32.2 us  [sum_rows(): lax.psum_scatter(values.astype(LOW), 'mp', scatter_dimension=0, tiled=True)]
    all_gather x4 -> x3, waiting for transfers between devices: 69.6 us -> 48.1 us  [all_rows(): return lax.all_gather(values, 'mp', axis=0, tiled=True)]
    ppermute x7, waiting for transfers between devices: 1.29 us -> 18.3 us  [the longest x3 15.7 us: next_chip(): lax.ppermute(values, 'mp', [(i, (i + 2 * step) % count) for i in range(co...]
    dot_general x4 -> x1, matrix products: 18.9 us -> 4.12 us  [times_transposed(): lax.dot_general(left, right, (((1,), (1,)), ((), ())), preferred_element_...]
    all_gather x4 -> x3, starting transfers between devices: 0.33 us -> 13.2 us  [all_rows(): return lax.all_gather(values, 'mp', axis=0, tiled=True)]
    dot_general x3 -> x1, matrix products: 9.96 us -> 2.87 us  [transposed_times(): lax.dot_general(left, right, (((0,), (0,)), ((), ())), preferred_element_...]
    ppermute x40 -> x32, starting transfers between devices: 39.5 us -> 33.1 us  [swap(): return lax.ppermute(values, 'dp', [(i, i ^ 1 << bit) for i in range(count)])]
  transfers between devices with their start and end apart: 55 -> 46, of which waited for: 18 -> 17; matrix products, arithmetic and copies ran while one was open for 19% -> 13% of each run, Pallas kernels for 12% -> 22%
where the time goes in v3:
time: 450 us; the launch traced here: 447 us
  waiting for transfers between devices  181 us (40%)
  Pallas kernels  101 us (22%)
  starting transfers between devices  50.2 us (11%)
  other arithmetic  44.9 us (10%)
  local copies, waits for them, and re-layouts  34.8 us (8%)
  matrix products  19.1 us (4%)
  between operations  14.9 us (3%)
    ppermute x32, waiting for transfers between devices, swap(): return lax.ppermute(values, 'dp', [(i, i ^ 1 << bit) for i in range(count)])  82.5 us
    all_gather x3, waiting for transfers between devices, all_rows(): return lax.all_gather(values, 'mp', axis=0, tiled=True)  48.1 us
    ppermute x32, starting transfers between devices, swap(): return lax.ppermute(values, 'dp', [(i, i ^ 1 << bit) for i in range(count)])  33.1 us
    reduce_scatter x4, waiting for transfers between devices, sum_rows(): lax.psum_scatter(values.astype(LOW), 'mp', scatter_dimension=0, tiled=True)  32.2 us
    pallas_call x8, Pallas kernels, call_blocks(): pl.pallas_call(body, grid_spec=pltpu.PrefetchScalarGridSpec(num_scalar_pr...  31 us
    pallas_call x6, Pallas kernels, place(): pl.pallas_call(lambda *refs: place_kernel(count, len(onto), splits, *refs...  28.3 us
    pallas_call x1, Pallas kernels, backward_mix(): pl.pallas_call(lambda *refs: backward_kernel(heads, owners, *refs), in_sp...  24.7 us
    convert_element_type x11, other arithmetic, land(): total = (self.kept.astype(WIDE) + got.astype(WIDE)).astype(LOW)  21.4 us
  transfers between devices with their start and end apart: 46, of which 17 were waited for; matrix products, arithmetic and copies ran while one was open for 13% of the time, Pallas kernels for 22%

profile of v3, /device:TPU:0, one launch (start us, length us, event | category | flops | bytes accessed | tf_op | source)
XLA Modules:
  0.0 446.6 jit_solution(14838907945593795348)
XLA Ops:
  15.8 1.9 reshape.216.refs_5_.refs_13_
  20.6 1.9 reshape.213.refs_4_.refs_12_
  23.1 3.5 pad_maximum_fusion.refs_1_.refs_10_
  26.7 24.6 %all-gather.4.cloned.1.call-done.refs_0_.refs_9_ = bf16[768,2048]{1,0:T(8,128)(2,1)} async-done(((bf16[96,2048]{1,0:T(8,128)(2,1)}), bf16[768,2048]{1,0:T(8,128)(2,1)}) %all-gather.4.cloned.1.call-update) | async-done | bytes 3145744 | tf_op jit(solution)/shard_map/all_gather | solution.py:583
  53.9 17.1 %shard_map.306 = (bf16[768,2048]{1,0:T(8,128)(2,1)}, bf16[768,320]{1,0:T(8,128)(2,1)}, bf16[768,320]{1,0:T(8,128)(2,1)}, f32[768,320]{1,0:T(8,128)}, f32[768,320...) custom-call(s32[1,7]{1,0:T(1,128)} %bitcast.70, bf16[768,2048]{1,0:T(8,128)(2,1)} %all-gather.4.cloned.1.call-done.refs_0_.refs_9_, ...), custom_call_target="tpu_custom_call" | custom-call | tf_op jit(solution)/shard_map/pallas_call | solution.py:390
  76.3 14.8 %collective-permute-done.2.refs_5_ = bf16[96,2048]{1,0:T(8,128)(2,1)} collective-permute-done((bf16[96,2048]{1,0:T(8,128)(2,1)}, bf16[96,2048]{1,0:T(8,128)(2,1)}, u32[]{:S(2)}, u32[]{:S(2)}) %collective-permute-start.2) | collective-permute-done | bytes 393248 | tf_op jit(solution)/shard_map/ppermute | solution.py:726
  91.1 25.6 %reduce-scatter.5.cloned.1.call-done.added_ref = bf16[96,2048]{1,0:T(8,128)(2,1)} async-done(((bf16[768,2048]{1,0:T(8,128)(2,1)}), bf16[96,2048]{1,0:T(8,128)(2,1)}) %reduce-scatter.5.cloned.1.call-update) | async-done | bytes 393232 | tf_op jit(solution)/shard_map/reduce_scatter | solution.py:579
  120.3 1.9 collective-permute-done.6.refs_6_
  125.1 2.8 shard_map.308
  127.9 1.7 copy-done.3
  129.6 4.1 fusion.12
  133.7 23.5 %all-gather.6.cloned.1.call-done.left_ref = bf16[768,2048]{1,0:T(8,128)(2,1)} async-done(((bf16[96,2048]{1,0:T(8,128)(2,1)}), bf16[768,2048]{1,0:T(8,128)(2,1)}) %all-gather.6.cloned.1.call-update) | async-done | bytes 3145744 | tf_op jit(solution)/shard_map/all_gather | solution.py:583
  157.2 5.6 %fusion.14 = f32[768,768]{1,0:T(8,128)S(1)} fusion(bf16[768,2048]{1,0:T(8,128)(2,1)} %all-gather.6.cloned.1.call-done.left_ref, bf16[2048,768]{1,0:T(8,128)(2,1)} %up_w_ref.1), kind=kOutput, calls=%fused_computation.75 | convolution fusion | flops 2415919104 | bytes 8650752 | tf_op jit(solution)/shard_map/dot_general | solution.py:27
  162.8 2.6 fusion.13
  165.4 2.8 multiply_convert_fusion
  168.3 2.9 convolution_convert_fusion
  171.2 1.8 broadcast_select_fusion.2
  172.9 1.5 collective-permute-start.7
  174.4 1.5 collective-permute-start.8
  177.1 4.8 %shard_map.309 = bf16[1024,768]{1,0:T(8,128)(2,1)} custom-call(s32[2]{0:T(128)} %pad_add_fusion._, bf16[768,2048]{1,0:T(8,128)(2,1)} %all-gather.6.cloned.1.call-done.left_ref, bf16[768,768]{1,0:T(8,128)(2,1)} %get-tuple-element.193.right_ref.gate_low_ref), custom_call_target="tpu_custom_call" | custom-call | tf_op jit(solution)/shard_map/pallas_call | solution.py:441
  181.8 4.8 %shard_map.310 = bf16[1024,768]{1,0:T(8,128)(2,1)} custom-call(s32[2]{0:T(128)} %pad_add_fusion.1._, bf16[768,2048]{1,0:T(8,128)(2,1)} %all-gather.6.cloned.1.call-done.left_ref, bf16[768,768]{1,0:T(8,128)(2,1)} %get-tuple-element.293.right_ref.up_low_ref), custom_call_target="tpu_custom_call" | custom-call | tf_op jit(solution)/shard_map/pallas_call | solution.py:441
  186.6 9.0 %shard_map.311 = bf16[768,2048]{1,0:T(8,128)(2,1)} custom-call(s32[1]{0:T(128)} %constant.193.clone.1._, bf16[768,768]{1,0:T(8,128)(2,1)} %get-tuple-element.193.right_ref.gate_low_ref, bf16[768,768]{1,0:T(8,128)(2,1)} %get-tuple-element.293.right_ref.up_low_ref, bf16[2048,768]{1,0:T(8,128)(2,1)} %gate_w_ref.1, bf16[2048,768]{1,0:T(8,128)(2,1)} %up_w_ref.1), custom_call_target="tpu_custom_call" | custom-call | tf_op jit(solution)/shard_map/pallas_call | solution.py:441
  195.6 13.1 %all-gather.8.cloned.1.call-start = ((), (), s32[]{:S(2)}) async-start(), calls=%async_computation.8 | async-start | bytes 3538944 | tf_op jit(solution)/shard_map/all_gather | solution.py:583
  209.9 2.3 add_convert_fusion.6
  213.2 1.5 collective-permute-start.10
  215.7 1.5 collective-permute-start.9
  218.3 4.8 %shard_map.314 = bf16[1024,768]{1,0:T(8,128)(2,1)} custom-call(s32[2]{0:T(128)} %pad_add_fusion.3._, bf16[768,2048]{1,0:T(8,128)(2,1)} %all-gather.6.cloned.1.call-done.left_ref, bf16[768,768]{1,0:T(8,128)(2,1)} %get-tuple-element.293.right_ref.up_low_ref), custom_call_target="tpu_custom_call" | custom-call | tf_op jit(solution)/shard_map/pallas_call | solution.py:441
  223.1 4.8 %shard_map.313 = bf16[1024,768]{1,0:T(8,128)(2,1)} custom-call(s32[2]{0:T(128)} %pad_add_fusion.2._, bf16[768,2048]{1,0:T(8,128)(2,1)} %all-gather.6.cloned.1.call-done.left_ref, bf16[768,768]{1,0:T(8,128)(2,1)} %get-tuple-element.193.right_ref.gate_low_ref), custom_call_target="tpu_custom_call" | custom-call | tf_op jit(solution)/shard_map/pallas_call | solution.py:441
  227.9 5.3 %reduce-scatter.7.cloned.1.call-done.grad_ref = bf16[96,2048]{1,0:T(8,128)(2,1)} async-done(((bf16[768,2048]{1,0:T(8,128)(2,1)}), bf16[96,2048]{1,0:T(8,128)(2,1)}) %reduce-scatter.7.cloned.1.call-update) | async-done | bytes 393232 | tf_op jit(solution)/shard_map/reduce_scatter | solution.py:579
  235.3 1.6 shard_map.312
  239.2 14.4 %collective-permute-done.10 = bf16[768,256]{1,0:T(8,128)(2,1)} collective-permute-done((bf16[768,256]{1,0:T(8,128)(2,1)}, bf16[768,256]{1,0:T(8,128)(2,1)}, u32[]{:S(2)}, u32[]{:S(2)}) %collective-permute-start.10) | collective-permute-done | bytes 393248 | tf_op jit(solution)/shard_map/ppermute | solution.py:629
  253.9 2.0 add_convert_fusion.11.refs_5_
  256.4 1.5 collective-permute-start.17
  257.9 2.4 add_convert_fusion.1
  261.6 1.5 collective-permute-start.13
  263.0 1.9 add_convert_fusion
  266.6 1.9 add_convert_fusion.12.refs_1_
  268.5 1.6 collective-permute-start.16
  271.6 4.0 fusion.15
  275.6 16.3 %collective-permute-done.16.refs_3_ = bf16[768,256]{1,0:T(8,128)(2,1)} collective-permute-done((bf16[768,256]{1,0:T(8,128)(2,1)}, bf16[768,256]{1,0:T(8,128)(2,1)}, u32[]{:S(2)}, u32[]{:S(2)}) %collective-permute-start.16) | collective-permute-done | bytes 393248 | tf_op jit(solution)/shard_map/ppermute | solution.py:629
  292.0 2.5 add_convert_fusion.4.refs_1_
  296.8 2.3 add_convert_fusion.5.refs_1_
  300.8 24.7 %shard_map.315 = (bf16[896,2048]{1,0:T(8,128)(2,1)}, bf16[1024,512]{1,0:T(8,128)(2,1)}, bf16[1024,512]{1,0:T(8,128)(2,1)}, bf16[1024,512]{1,0:T(8,128)(2,1)}, bf16[1024,512]{1,0:T(8,128)(2,1)}) custom-call(s32[1,7]{1,0:T(1,128)} %bitcast.71, bf16[768,2048]{1,0:T(8,128)(2,1)} %all-gather.8.cloned.1.call-done.refs_1_, bf16[320,2048]{1,0:T(8,128)(2,1)} %refs_2_.3, ...), custom_call_target="tpu_custom_call" | custom-call | tf_op jit(solution)/shard_map/pallas_call | solution.py:416
  325.5 5.4 %collective-permute-done.20.refs_3_ = bf16[512,768]{1,0:T(8,128)(2,1)} collective-permute-done((bf16[512,768]{1,0:T(8,128)(2,1)}, bf16[512,768]{1,0:T(8,128)(2,1)}, u32[]{:S(2)}, u32[]{:S(2)}) %collective-permute-start.20) | collective-permute-done | bytes 786464 | tf_op jit(solution)/shard_map/ppermute | solution.py:629
  332.2 1.5 collective-permute-start.23
  333.7 1.5 collective-permute-start.24
  337.1 1.5 collective-permute-start.27
  339.1 19.6 %collective-permute-done.23 = bf16[1024,512]{1,0:T(8,128)(2,1)} collective-permute-done((bf16[1024,512]{1,0:T(8,128)(2,1)}, bf16[1024,512]{1,0:T(8,128)(2,1)}, u32[]{:S(2)}, u32[]{:S(2)}) %collective-permute-start.23) | collective-permute-done | bytes 1048608 | tf_op jit(solution)/shard_map/ppermute | solution.py:629
  358.7 1.5 collective-permute-done.24
  360.2 1.9 add_convert_fusion.3
  363.1 1.5 collective-permute-start.25
  364.5 1.5 add_convert_fusion.2
  368.6 2.1 add_convert_fusion.10
  370.7 21.9 %collective-permute-done.30.refs_8_ = bf16[768,256]{1,0:T(8,128)(2,1)S(1)} collective-permute-done((bf16[768,256]{1,0:T(8,128)(2,1)}, bf16[768,256]{1,0:T(8,128)(2,1)S(1)}, u32[]{:S(2)}, u32[]{:S(2)}) %collective-permute-start.30) | collective-permute-done | bytes 393248 | tf_op jit(solution)/shard_map/ppermute | solution.py:629
  393.4 1.4 add_convert_fusion.8.refs_4_
  394.8 1.6 collective-permute-start.34
  398.3 1.6 collective-permute-start.32
  403.3 5.4 %shard_map.316 = f32[2048,768]{1,0:T(8,128)} custom-call(s32[4]{0:T(128)S(1)} %pad_add_fusion.4.refs_0_, bf16[512,768]{1,0:T(8,128)(2,1)} %add_convert_fusion.5.refs_1_, bf16[512,768]{1,0:T(8,128)(2,1)} %collective-permute-done.19.refs_2_, bf16[512,768]{1,0:T(8,128)(2,1)} %collective-permute-done.20.refs_3_, bf16[512,768]{1,0:T(8,128)(2,1)} %collective-permute-done.27.refs_4_), custom_call_target="tpu_custom_call" | custom-call | tf_op jit(solution)/shard_map/pallas_call | solution.py:607
  408.8 6.2 %shard_map.317 = f32[768,2048]{1,0:T(8,128)} custom-call(s32[8]{0:T(128)S(1)} %stack.201.refs_0_, bf16[768,256]{1,0:T(8,128)(2,1)} %add_convert_fusion.12.refs_1_, bf16[768,256]{1,0:T(8,128)(2,1)} %collective-permute-done.15.refs_2_, bf16[768,256]{1,0:T(8,128)(2,1)} %collective-permute-done.16.refs_3_, bf16[768,256]{1,0:T(8,128)(2,1)} %collective-permute-done.29.refs_4_, ...), custom_call_target="tpu_custom_call" | custom-call | tf_op jit(solution)/shard_map/pallas_call | solution.py:607
  415.0 3.1 collective-permute-done.35
  420.9 1.5 collective-permute-start.38
  422.6 5.5 %shard_map.318 = f32[2048,768]{1,0:T(8,128)} custom-call(s32[4]{0:T(128)S(1)} %pad_add_fusion.5.refs_0_, bf16[512,768]{1,0:T(8,128)(2,1)} %add_convert_fusion.4.refs_1_, bf16[512,768]{1,0:T(8,128)(2,1)} %collective-permute-done.21.refs_2_, bf16[512,768]{1,0:T(8,128)(2,1)} %collective-permute-done.22.refs_3_, bf16[512,768]{1,0:T(8,128)(2,1)} %collective-permute-done.28.refs_4_), custom_call_target="tpu_custom_call" | custom-call | tf_op jit(solution)/shard_map/pallas_call | solution.py:607
  428.1 5.2 %shard_map.319 = (f32[320,2048]{1,0:T(8,128)}, f32[320,2048]{1,0:T(8,128)}, f32[320,2048]{1,0:T(8,128)}, f32[64,2048]{1,0:T(8,128)S(1)}) custom-call(s32[6]{0:T(128)S(1)} %stack.208.refs_0_, bf16[1024,256]{1,0:T(8,128)(2,1)S(1)} %copy-done.10, bf16[1024,256]{1,0:T(8,128)(2,1)} %collective-permute-done.31.refs_2_, bf16[1024,256]{1,0:T(8,128)(2,1)S(1)} %copy-done.16, ...), custom_call_target="tpu_custom_call" | custom-call | tf_op jit(solution)/shard_map/pallas_call | solution.py:607
  433.4 3.2 shard_map.320
  (228 shorter events, 65.0 us)
Async XLA Ops:
  7.2 122.4 %copy-start = (bf16[768,2048]{1,0:T(8,128)(2,1)S(1)}, bf16[768,2048]{1,0:T(8,128)(2,1)}, u32[]{:S(2)}) copy-start(bf16[768,2048]{1,0:T(8,128)(2,1)} %param.42) | copy-start | bytes 9437188
  7.2 44.1 %all-gather.4.cloned.1.call-start = ((), (), s32[]{:S(2)}) async-start(), calls=%async_computation.4 | async-start | bytes 3538944 | tf_op jit(solution)/shard_map/all_gather | solution.py:583
  10.1 106.6 %reduce-scatter.5.cloned.1.call-start = ((), (), s32[]{:S(2)}) async-start(), calls=%async_computation.5 | async-start | bytes 3538944 | tf_op jit(solution)/shard_map/reduce_scatter | solution.py:579
  23.1 30.2 %copy-start.53 = (s32[1,3]{1,0:T(1,128)S(1)}, s32[1,3]{1,0:T(1,128)}, u32[]{:S(2)}) copy-start(s32[1,3]{1,0:T(1,128)} %param.27) | copy-start | bytes 40
  51.3 19.8 %collective-permute-start.1 = (bf16[96,2048]{1,0:T(8,128)(2,1)}, bf16[96,2048]{1,0:T(8,128)(2,1)}, u32[]{:S(2)}, u32[]{:S(2)}) collective-permute-start(bf16[96,2048]{1,0:T(8,128)(2,1)} %added_ref.3), channel_id=1, source_target_pairs={{0,6},{1,7},{2,0},{3,1},{4,2},{5,3},{6,4},{7,5},{8,14},{9,15},{10,... | collective-permute-start | bytes 1179656 | tf_op jit(solution)/shard_map/ppermute | solution.py:726
  52.6 19.4 %collective-permute-start = (bf16[96,2048]{1,0:T(8,128)(2,1)}, bf16[96,2048]{1,0:T(8,128)(2,1)}, u32[]{:S(2)}, u32[]{:S(2)}) collective-permute-start(bf16[96,2048]{1,0:T(8,128)(2,1)} %added_ref.3), channel_id=1, source_target_pairs={{0,2},{1,3},{2,4},{3,5},{4,6},{5,7},{6,0},{7,1},{8,10},{9,11},{10,... | collective-permute-start | bytes 1179656 | tf_op jit(solution)/shard_map/ppermute | solution.py:726
  71.0 45.7 %copy-start.2 = (bf16[96,2048]{1,0:T(8,128)(2,1)S(1)}, bf16[96,2048]{1,0:T(8,128)(2,1)}, u32[]{:S(2)}) copy-start(bf16[96,2048]{1,0:T(8,128)(2,1)} %start_ref.3) | copy-start | bytes 1179652
  71.0 45.7 %copy-start.33 = (f32[2048]{0:T(1024)S(1)}, f32[2048]{0:T(1024)}, u32[]{:S(2)}) copy-start(f32[2048]{0:T(1024)} %param.39) | copy-start | bytes 24580
  72.0 85.2 %all-gather.6.cloned.1.call-start = ((), (), s32[]{:S(2)}) async-start(), calls=%async_computation.6 | async-start | bytes 3538944 | tf_op jit(solution)/shard_map/all_gather | solution.py:583
  72.1 2.0 collective-permute-start.3
  72.1 2.7 collective-permute-start.5
  72.6 2.9 collective-permute-start.4
  72.7 18.4 %collective-permute-start.2 = (bf16[96,2048]{1,0:T(8,128)(2,1)}, bf16[96,2048]{1,0:T(8,128)(2,1)}, u32[]{:S(2)}, u32[]{:S(2)}) collective-permute-start(bf16[96,2048]{1,0:T(8,128)(2,1)} %collective-permute-done.refs_3_), channel_id=1, source_target_pairs={{0,2},{1,3},{2,4},{3,5},{4,6},{5,7},{6,0},{7,1},{8,10},{9,11},{10,... | collective-permute-start | bytes 1179656 | tf_op jit(solution)/shard_map/ppermute | solution.py:726
  119.7 113.5 %reduce-scatter.7.cloned.1.call-start = ((), (), s32[]{:S(2)}) async-start(), calls=%async_computation.7 | async-start | bytes 3538944 | tf_op jit(solution)/shard_map/reduce_scatter | solution.py:579
  120.0 2.1 collective-permute-start.6
  157.2 5.6 %copy-start.36 = (bf16[768,2048]{1,0:T(8,128)(2,1)S(1)}, bf16[768,2048]{1,0:T(8,128)(2,1)}, u32[]{:S(2)}) copy-start(bf16[768,2048]{1,0:T(8,128)(2,1)} %all-gather.6.cloned.1.call-done.left_ref) | copy-start | bytes 9437188
  157.2 5.6 %copy-start.38 = (bf16[2048,768]{1,0:T(8,128)(2,1)S(1)}, bf16[2048,768]{1,0:T(8,128)(2,1)}, u32[]{:S(2)}) copy-start(bf16[2048,768]{1,0:T(8,128)(2,1)} %gate_w_ref.1) | copy-start | bytes 9437188
  172.9 22.6 %collective-permute-start.7 = (bf16[768,512]{1,0:T(8,128)(2,1)}, bf16[768,512]{1,0:T(8,128)(2,1)}, u32[]{:S(2)}, u32[]{:S(2)}) collective-permute-start(bf16[768,512]{1,0:T(8,128)(2,1)} %get-tuple-element.297), channel_id=1, source_target_pairs={{0,8},{8,0},{16,24},{24,16},{1,9},{9,1},{17,25},{25,17},{2,10},{10... | collective-permute-start | bytes 2359304 | tf_op jit(solution)/shard_map/ppermute | solution.py:629
  174.4 21.2 %collective-permute-start.8 = (bf16[768,512]{1,0:T(8,128)(2,1)}, bf16[768,512]{1,0:T(8,128)(2,1)}, u32[]{:S(2)}, u32[]{:S(2)}) collective-permute-start(bf16[768,512]{1,0:T(8,128)(2,1)} %get-tuple-element.299), channel_id=1, source_target_pairs={{0,16},{8,24},{16,0},{24,8},{1,17},{9,25},{17,1},{25,9},{2,18},{10... | collective-permute-start | bytes 2359304 | tf_op jit(solution)/shard_map/ppermute | solution.py:629
  195.6 96.3 %all-gather.8.cloned.1.call-start = ((), (), s32[]{:S(2)}) async-start(), calls=%async_computation.8 | async-start | bytes 3538944 | tf_op jit(solution)/shard_map/all_gather | solution.py:583
  208.7 45.1 %collective-permute-start.11 = (bf16[1024,768]{1,0:T(8,128)(2,1)}, bf16[1024,768]{1,0:T(8,128)(2,1)}, u32[]{:S(2)}, u32[]{:S(2)}) collective-permute-start(bf16[1024,768]{1,0:T(8,128)(2,1)} %shard_map.309), channel_id=1, source_target_pairs={{0,8},{8,0},{16,24},{24,16},{1,9},{9,1},{17,25},{25,17},{2,10},{10... | collective-permute-start | bytes 4718600 | tf_op jit(solution)/shard_map/ppermute | solution.py:629
  209.4 44.4 %collective-permute-start.12 = (bf16[1024,768]{1,0:T(8,128)(2,1)}, bf16[1024,768]{1,0:T(8,128)(2,1)}, u32[]{:S(2)}, u32[]{:S(2)}) collective-permute-start(bf16[1024,768]{1,0:T(8,128)(2,1)} %shard_map.310), channel_id=1, source_target_pairs={{0,16},{8,24},{16,0},{24,8},{1,17},{9,25},{17,1},{25,9},{2,18},{10... | collective-permute-start | bytes 4718600 | tf_op jit(solution)/shard_map/ppermute | solution.py:629
  213.2 40.3 %collective-permute-start.10 = (bf16[768,256]{1,0:T(8,128)(2,1)}, bf16[768,256]{1,0:T(8,128)(2,1)}, u32[]{:S(2)}, u32[]{:S(2)}) collective-permute-start(bf16[768,256]{1,0:T(8,128)(2,1)} %get-tuple-element.311), channel_id=1, source_target_pairs={{0,8},{8,0},{16,24},{24,16},{1,9},{9,1},{17,25},{25,17},{2,10},{10... | collective-permute-start | bytes 1179656 | tf_op jit(solution)/shard_map/ppermute | solution.py:629
  215.7 38.1 %collective-permute-start.9 = (bf16[768,256]{1,0:T(8,128)(2,1)}, bf16[768,256]{1,0:T(8,128)(2,1)}, u32[]{:S(2)}, u32[]{:S(2)}) collective-permute-start(bf16[768,256]{1,0:T(8,128)(2,1)} %get-tuple-element.313), channel_id=1, source_target_pairs={{0,16},{8,24},{16,0},{24,8},{1,17},{9,25},{17,1},{25,9},{2,18},{10... | collective-permute-start | bytes 1179656 | tf_op jit(solution)/shard_map/ppermute | solution.py:629
  253.8 78.3 %reduce-scatter.9.cloned.1.call-start = ((), (), s32[]{:S(2)}) async-start(), calls=%async_computation.9 | async-start | bytes 3538944 | tf_op jit(solution)/shard_map/reduce_scatter | solution.py:579
  255.9 14.2 %collective-permute-start.18 = (bf16[768,256]{1,0:T(8,128)(2,1)}, bf16[768,256]{1,0:T(8,128)(2,1)S(1)}, u32[]{:S(2)}, u32[]{:S(2)}) collective-permute-start(bf16[768,256]{1,0:T(8,128)(2,1)} %add_convert_fusion.11.refs_5_), channel_id=1, source_target_pairs={{0,16},{8,24},{16,0},{24,8},{1,17},{9,25},{17,1},{25,9},{2,18},{10... | collective-permute-start | bytes 1179656 | tf_op jit(solution)/shard_map/ppermute | solution.py:629
  256.4 19.1 %collective-permute-start.17 = (bf16[768,256]{1,0:T(8,128)(2,1)}, bf16[768,256]{1,0:T(8,128)(2,1)}, u32[]{:S(2)}, u32[]{:S(2)}) collective-permute-start(bf16[768,256]{1,0:T(8,128)(2,1)} %add_convert_fusion.11.refs_5_), channel_id=1, source_target_pairs={{0,8},{8,0},{16,24},{24,16},{1,9},{9,1},{17,25},{25,17},{2,10},{10... | collective-permute-start | bytes 1179656 | tf_op jit(solution)/shard_map/ppermute | solution.py:629
  261.6 30.3 %collective-permute-start.13 = (bf16[512,768]{1,0:T(8,128)(2,1)}, bf16[512,768]{1,0:T(8,128)(2,1)}, u32[]{:S(2)}, u32[]{:S(2)}) collective-permute-start(bf16[512,768]{1,0:T(8,128)(2,1)} %get-tuple-element.303), channel_id=1, source_target_pairs={{0,16},{8,24},{16,0},{24,8},{1,17},{9,25},{17,1},{25,9},{2,18},{10... | collective-permute-start | bytes 2359304 | tf_op jit(solution)/shard_map/ppermute | solution.py:629
  264.9 6.7 %copy-start.43 = (bf16[768,768]{1,0:T(8,128)(2,1)S(1)}, bf16[768,768]{1,0:T(8,128)(2,1)}, u32[]{:S(2)}) copy-start(bf16[768,768]{1,0:T(8,128)(2,1)} %copy-done.42) | copy-start | bytes 3538948
  266.2 25.7 %collective-permute-start.14 = (bf16[512,768]{1,0:T(8,128)(2,1)}, bf16[512,768]{1,0:T(8,128)(2,1)}, u32[]{:S(2)}, u32[]{:S(2)}) collective-permute-start(bf16[512,768]{1,0:T(8,128)(2,1)} %get-tuple-element.301), channel_id=1, source_target_pairs={{0,8},{8,0},{16,24},{24,16},{1,9},{9,1},{17,25},{25,17},{2,10},{10... | collective-permute-start | bytes 2359304 | tf_op jit(solution)/shard_map/ppermute | solution.py:629
  268.5 23.4 %collective-permute-start.16 = (bf16[768,256]{1,0:T(8,128)(2,1)}, bf16[768,256]{1,0:T(8,128)(2,1)}, u32[]{:S(2)}, u32[]{:S(2)}) collective-permute-start(bf16[768,256]{1,0:T(8,128)(2,1)} %add_convert_fusion.12.refs_1_), channel_id=1, source_target_pairs={{0,8},{8,0},{16,24},{24,16},{1,9},{9,1},{17,25},{25,17},{2,10},{10... | collective-permute-start | bytes 1179656 | tf_op jit(solution)/shard_map/ppermute | solution.py:629
  270.9 21.0 %collective-permute-start.15 = (bf16[768,256]{1,0:T(8,128)(2,1)}, bf16[768,256]{1,0:T(8,128)(2,1)}, u32[]{:S(2)}, u32[]{:S(2)}) collective-permute-start(bf16[768,256]{1,0:T(8,128)(2,1)} %add_convert_fusion.12.refs_1_), channel_id=1, source_target_pairs={{0,16},{8,24},{16,0},{24,8},{1,17},{9,25},{17,1},{25,9},{2,18},{10... | collective-permute-start | bytes 1179656 | tf_op jit(solution)/shard_map/ppermute | solution.py:629
  291.9 101.4 %reduce-scatter.11.cloned.1.call-start = ((), (), s32[]{:S(2)}) async-start(), calls=%async_computation.10 | async-start | bytes 4128768 | tf_op jit(solution)/shard_map/reduce_scatter | solution.py:579
  294.5 30.9 %collective-permute-start.22 = (bf16[512,768]{1,0:T(8,128)(2,1)}, bf16[512,768]{1,0:T(8,128)(2,1)}, u32[]{:S(2)}, u32[]{:S(2)}) collective-permute-start(bf16[512,768]{1,0:T(8,128)(2,1)} %add_convert_fusion.4.refs_1_), channel_id=1, source_target_pairs={{0,16},{8,24},{16,0},{24,8},{1,17},{9,25},{17,1},{25,9},{2,18},{10... | collective-permute-start | bytes 2359304 | tf_op jit(solution)/shard_map/ppermute | solution.py:629
  295.8 29.6 %collective-permute-start.21 = (bf16[512,768]{1,0:T(8,128)(2,1)}, bf16[512,768]{1,0:T(8,128)(2,1)}, u32[]{:S(2)}, u32[]{:S(2)}) collective-permute-start(bf16[512,768]{1,0:T(8,128)(2,1)} %add_convert_fusion.4.refs_1_), channel_id=1, source_target_pairs={{0,8},{8,0},{16,24},{24,16},{1,9},{9,1},{17,25},{25,17},{2,10},{10... | collective-permute-start | bytes 2359304 | tf_op jit(solution)/shard_map/ppermute | solution.py:629
  299.2 31.7 %collective-permute-start.20 = (bf16[512,768]{1,0:T(8,128)(2,1)}, bf16[512,768]{1,0:T(8,128)(2,1)}, u32[]{:S(2)}, u32[]{:S(2)}) collective-permute-start(bf16[512,768]{1,0:T(8,128)(2,1)} %add_convert_fusion.5.refs_1_), channel_id=1, source_target_pairs={{0,8},{8,0},{16,24},{24,16},{1,9},{9,1},{17,25},{25,17},{2,10},{10... | collective-permute-start | bytes 2359304 | tf_op jit(solution)/shard_map/ppermute | solution.py:629
  300.1 30.8 %collective-permute-start.19 = (bf16[512,768]{1,0:T(8,128)(2,1)}, bf16[512,768]{1,0:T(8,128)(2,1)}, u32[]{:S(2)}, u32[]{:S(2)}) collective-permute-start(bf16[512,768]{1,0:T(8,128)(2,1)} %add_convert_fusion.5.refs_1_), channel_id=1, source_target_pairs={{0,16},{8,24},{16,0},{24,8},{1,17},{9,25},{17,1},{25,9},{2,18},{10... | collective-permute-start | bytes 2359304 | tf_op jit(solution)/shard_map/ppermute | solution.py:629
  332.2 26.5 %collective-permute-start.23 = (bf16[1024,512]{1,0:T(8,128)(2,1)}, bf16[1024,512]{1,0:T(8,128)(2,1)}, u32[]{:S(2)}, u32[]{:S(2)}) collective-permute-start(bf16[1024,512]{1,0:T(8,128)(2,1)} %get-tuple-element.233), channel_id=1, source_target_pairs={{0,8},{8,0},{16,24},{24,16},{1,9},{9,1},{17,25},{25,17},{2,10},{10... | collective-permute-start | bytes 3145736 | tf_op jit(solution)/shard_map/ppermute | solution.py:629
  333.7 26.4 %collective-permute-start.24 = (bf16[1024,512]{1,0:T(8,128)(2,1)}, bf16[1024,512]{1,0:T(8,128)(2,1)}, u32[]{:S(2)}, u32[]{:S(2)}) collective-permute-start(bf16[1024,512]{1,0:T(8,128)(2,1)} %get-tuple-element.234), channel_id=1, source_target_pairs={{0,16},{8,24},{16,0},{24,8},{1,17},{9,25},{17,1},{25,9},{2,18},{10... | collective-permute-start | bytes 3145736 | tf_op jit(solution)/shard_map/ppermute | solution.py:629
  336.5 28.0 %copy-start.44 = (bf16[1024,512]{1,0:T(8,128)(2,1)S(1)}, bf16[1024,512]{1,0:T(8,128)(2,1)}, u32[]{:S(2)}) copy-start(bf16[1024,512]{1,0:T(8,128)(2,1)} %get-tuple-element.239) | copy-start | bytes 3145732
  336.5 31.3 %collective-permute-start.29 = (bf16[768,256]{1,0:T(8,128)(2,1)}, bf16[768,256]{1,0:T(8,128)(2,1)}, u32[]{:S(2)}, u32[]{:S(2)}) collective-permute-start(bf16[768,256]{1,0:T(8,128)(2,1)} %collective-permute-done.15.refs_2_), channel_id=1, source_target_pairs={{0,8},{8,0},{16,24},{24,16},{1,9},{9,1},{17,25},{25,17},{2,10},{10... | collective-permute-start | bytes 1179656 | tf_op jit(solution)/shard_map/ppermute | solution.py:629
  337.1 56.3 %collective-permute-start.27 = (bf16[512,768]{1,0:T(8,128)(2,1)}, bf16[512,768]{1,0:T(8,128)(2,1)}, u32[]{:S(2)}, u32[]{:S(2)}) collective-permute-start(bf16[512,768]{1,0:T(8,128)(2,1)} %collective-permute-done.19.refs_2_), channel_id=1, source_target_pairs={{0,8},{8,0},{16,24},{24,16},{1,9},{9,1},{17,25},{25,17},{2,10},{10... | collective-permute-start | bytes 2359304 | tf_op jit(solution)/shard_map/ppermute | solution.py:629
  338.5 54.8 %collective-permute-start.28 = (bf16[512,768]{1,0:T(8,128)(2,1)}, bf16[512,768]{1,0:T(8,128)(2,1)}, u32[]{:S(2)}, u32[]{:S(2)}) collective-permute-start(bf16[512,768]{1,0:T(8,128)(2,1)} %collective-permute-done.21.refs_2_), channel_id=1, source_target_pairs={{0,16},{8,24},{16,0},{24,8},{1,17},{9,25},{17,1},{25,9},{2,18},{10... | collective-permute-start | bytes 2359304 | tf_op jit(solution)/shard_map/ppermute | solution.py:629
  363.1 30.3 %collective-permute-start.25 = (bf16[1024,256]{1,0:T(8,128)(2,1)}, bf16[1024,256]{1,0:T(8,128)(2,1)}, u32[]{:S(2)}, u32[]{:S(2)}) collective-permute-start(bf16[1024,256]{1,0:T(8,128)(2,1)} %get-tuple-element.307), channel_id=1, source_target_pairs={{0,16},{8,24},{16,0},{24,8},{1,17},{9,25},{17,1},{25,9},{2,18},{10... | collective-permute-start | bytes 1572872 | tf_op jit(solution)/shard_map/ppermute | solution.py:629
  367.1 26.2 %collective-permute-start.26 = (bf16[1024,256]{1,0:T(8,128)(2,1)}, bf16[1024,256]{1,0:T(8,128)(2,1)}, u32[]{:S(2)}, u32[]{:S(2)}) collective-permute-start(bf16[1024,256]{1,0:T(8,128)(2,1)} %get-tuple-element.305), channel_id=1, source_target_pairs={{0,8},{8,0},{16,24},{24,16},{1,9},{9,1},{17,25},{25,17},{2,10},{10... | collective-permute-start | bytes 1572872 | tf_op jit(solution)/shard_map/ppermute | solution.py:629
  367.8 24.8 %collective-permute-start.30 = (bf16[768,256]{1,0:T(8,128)(2,1)}, bf16[768,256]{1,0:T(8,128)(2,1)S(1)}, u32[]{:S(2)}, u32[]{:S(2)}) collective-permute-start(bf16[768,256]{1,0:T(8,128)(2,1)} %collective-permute-done.17.refs_6_), channel_id=1, source_target_pairs={{0,16},{8,24},{16,0},{24,8},{1,17},{9,25},{17,1},{25,9},{2,18},{10... | collective-permute-start | bytes 1179656 | tf_op jit(solution)/shard_map/ppermute | solution.py:629
  370.7 29.8 %copy-start.32 = (f32[2048]{0:T(1024)S(1)}, f32[2048]{0:T(1024)}, u32[]{:S(2)}) copy-start(f32[2048]{0:T(1024)} %param.28) | copy-start | bytes 24580
  393.4 7.0 %copy-start.45 = (bf16[112,2048]{1,0:T(8,128)(2,1)S(1)}, bf16[112,2048]{1,0:T(8,128)(2,1)}, u32[]{:S(2)}) copy-start(bf16[112,2048]{1,0:T(8,128)(2,1)} %reduce-scatter.11.cloned.1.call-done) | copy-start | bytes 1376260
  394.8 8.5 %copy-start.7 = (bf16[1024,256]{1,0:T(8,128)(2,1)}, bf16[1024,256]{1,0:T(8,128)(2,1)S(1)}, u32[]{:S(2)}) copy-start(bf16[1024,256]{1,0:T(8,128)(2,1)S(1)} %add_convert_fusion.8.refs_4_) | copy-start | bytes 1572868
  394.8 7.4 %copy-start.12 = (f32[96,2048]{1,0:T(8,128)S(1)}, f32[96,2048]{1,0:T(8,128)}, u32[]{:S(2)}) copy-start(f32[96,2048]{1,0:T(8,128)} %copy-done.11) | copy-start | bytes 2359300
  394.8 7.4 %copy-start.52 = (f32[96]{0:T(128)S(1)}, f32[96]{0:T(128)}, u32[]{:S(2)}) copy-start(f32[96]{0:T(128)} %add_rsqrt_fusion) | copy-start | bytes 1156
  394.8 23.3 %collective-permute-start.34 = (bf16[1024,256]{1,0:T(8,128)(2,1)S(1)}, bf16[1024,256]{1,0:T(8,128)(2,1)S(1)}, u32[]{:S(2)}, u32[]{:S(2)}) collective-permute-start(bf16[1024,256]{1,0:T(8,128)(2,1)S(1)} %add_convert_fusion.8.refs_4_), channel_id=1, source_target_pairs={{0,16},{8,24},{16,0},{24,8},{1,17},{9,25},{17,1},{25,9},{2,18},{10... | collective-permute-start | bytes 1572872 | tf_op jit(solution)/shard_map/ppermute | solution.py:629
  396.4 22.6 %collective-permute-start.33 = (bf16[1024,256]{1,0:T(8,128)(2,1)S(1)}, bf16[1024,256]{1,0:T(8,128)(2,1)}, u32[]{:S(2)}, u32[]{:S(2)}) collective-permute-start(bf16[1024,256]{1,0:T(8,128)(2,1)S(1)} %add_convert_fusion.8.refs_4_), channel_id=1, source_target_pairs={{0,8},{8,0},{16,24},{24,16},{1,9},{9,1},{17,25},{25,17},{2,10},{10... | collective-permute-start | bytes 1572872 | tf_op jit(solution)/shard_map/ppermute | solution.py:629
  398.3 20.7 %collective-permute-start.32 = (bf16[1024,256]{1,0:T(8,128)(2,1)S(1)}, bf16[1024,256]{1,0:T(8,128)(2,1)S(1)}, u32[]{:S(2)}, u32[]{:S(2)}) collective-permute-start(bf16[1024,256]{1,0:T(8,128)(2,1)S(1)} %add_convert_fusion.9.refs_1_), channel_id=1, source_target_pairs={{0,8},{8,0},{16,24},{24,16},{1,9},{9,1},{17,25},{25,17},{2,10},{10... | collective-permute-start | bytes 1572872 | tf_op jit(solution)/shard_map/ppermute | solution.py:629
  399.8 19.9 %collective-permute-start.31 = (bf16[1024,256]{1,0:T(8,128)(2,1)S(1)}, bf16[1024,256]{1,0:T(8,128)(2,1)}, u32[]{:S(2)}, u32[]{:S(2)}) collective-permute-start(bf16[1024,256]{1,0:T(8,128)(2,1)S(1)} %add_convert_fusion.9.refs_1_), channel_id=1, source_target_pairs={{0,16},{8,24},{16,0},{24,8},{1,17},{9,25},{17,1},{25,9},{2,18},{10... | collective-permute-start | bytes 1572872 | tf_op jit(solution)/shard_map/ppermute | solution.py:629
  400.5 20.4 %copy-start.46 = (f32[1,2048]{1,0:T(1,128)}, f32[1,2048]{1,0:T(1,128)S(1)}, u32[]{:S(2)}) copy-start(f32[1,2048]{1,0:T(1,128)S(1)} %get-tuple-element.308) | copy-start | bytes 24580
  400.5 20.4 %copy-start.48 = (f32[1,2048]{1,0:T(1,128)}, f32[1,2048]{1,0:T(1,128)S(1)}, u32[]{:S(2)}) copy-start(f32[1,2048]{1,0:T(1,128)S(1)} %get-tuple-element.309) | copy-start | bytes 24580
  401.5 16.7 %collective-permute-start.35 = (f32[2,2048]{1,0:T(2,128)S(1)}, f32[2,2048]{1,0:T(2,128)S(1)}, u32[]{:S(2)}, u32[]{:S(2)}) collective-permute-start(f32[2,2048]{1,0:T(2,128)S(1)} %pad_maximum_fusion.1), channel_id=1, source_target_pairs={{0,8},{8,0},{16,24},{24,16},{1,9},{9,1},{17,25},{25,17},{2,10},{10... | collective-permute-start | bytes 49160 | tf_op jit(solution)/shard_map/ppermute | solution.py:629
  419.7 13.6 %collective-permute-start.36 = (bf16[1024,256]{1,0:T(8,128)(2,1)}, bf16[1024,256]{1,0:T(8,128)(2,1)}, u32[]{:S(2)}, u32[]{:S(2)}) collective-permute-start(bf16[1024,256]{1,0:T(8,128)(2,1)} %collective-permute-done.31.refs_2_), channel_id=1, source_target_pairs={{0,8},{8,0},{16,24},{24,16},{1,9},{9,1},{17,25},{25,17},{2,10},{10... | collective-permute-start | bytes 1572872 | tf_op jit(solution)/shard_map/ppermute | solution.py:629
  420.3 13.0 %collective-permute-start.37 = (bf16[1024,256]{1,0:T(8,128)(2,1)}, bf16[1024,256]{1,0:T(8,128)(2,1)}, u32[]{:S(2)}, u32[]{:S(2)}) collective-permute-start(bf16[1024,256]{1,0:T(8,128)(2,1)} %collective-permute-done.33.refs_5_), channel_id=1, source_target_pairs={{0,16},{8,24},{16,0},{24,8},{1,17},{9,25},{17,1},{25,9},{2,18},{10... | collective-permute-start | bytes 1572872 | tf_op jit(solution)/shard_map/ppermute | solution.py:629
  420.9 12.4 %collective-permute-start.38 = (f32[2,2048]{1,0:T(2,128)S(1)}, f32[2,2048]{1,0:T(2,128)S(1)}, u32[]{:S(2)}, u32[]{:S(2)}) collective-permute-start(f32[2,2048]{1,0:T(2,128)S(1)} %fusion.9), channel_id=1, source_target_pairs={{0,16},{8,24},{16,0},{24,8},{1,17},{9,25},{17,1},{25,9},{2,18},{10... | collective-permute-start | bytes 49160 | tf_op jit(solution)/shard_map/ppermute | solution.py:629
  422.6 5.5 %copy-start.10 = (bf16[1024,256]{1,0:T(8,128)(2,1)S(1)}, bf16[1024,256]{1,0:T(8,128)(2,1)}, u32[]{:S(2)}) copy-start(bf16[1024,256]{1,0:T(8,128)(2,1)} %copy-done.9) | copy-start | bytes 1572868
  422.6 5.5 %copy-start.14 = (bf16[1024,256]{1,0:T(8,128)(2,1)S(1)}, bf16[1024,256]{1,0:T(8,128)(2,1)}, u32[]{:S(2)}) copy-start(bf16[1024,256]{1,0:T(8,128)(2,1)} %copy-done.13) | copy-start | bytes 1572868
  422.6 5.5 %copy-start.16 = (bf16[1024,256]{1,0:T(8,128)(2,1)S(1)}, bf16[1024,256]{1,0:T(8,128)(2,1)}, u32[]{:S(2)}) copy-start(bf16[1024,256]{1,0:T(8,128)(2,1)} %copy-done.15) | copy-start | bytes 1572868
  (36 other events, 81.6 us)
Sparse Core Ops, SparseCore 0:
  10.3 40.9 all-gather.3
  72.1 44.5 reduce-scatter.4
  119.8 37.2 all-gather.5
  195.7 37.4 reduce-scatter.6
  254.0 36.2 all-gather.7
  293.0 39.1 reduce-scatter.8
  335.1 44.1 reduce-scatter.10

commit v4 on v3

--- a/solution.py
+++ b/solution.py
@@ -333,15 +333,19 @@
     return strips, -(-rows // (strips * 2 * SUB)) * 2 * SUB
 
 
-def unpack_kernel(heads, strips, packed_ref, square_ref, small_ref, stacked_ref):
+def unpack_kernel(heads, strips, packed_ref, square_ref, taps_ref, *refs):
+    line_refs, stacked_ref = refs[:-1], refs[-1]
     depth, size = packed_ref.shape[0], square_ref.shape[-1]
     for k in range(strips):
         stacked_ref[pl.ds(k * depth, depth), :] = packed_ref[:, k * size : (k + 1) * size]
     for k in range(2 * heads):
         square_ref[k] = stacked_ref[pl.ds(k * size, size), :]
-    small_ref[...] = jnp.concatenate(
+    small = jnp.concatenate(
         [stacked_ref[pl.ds(2 * heads * size + h * SUB, SUB), :] for h in range(heads)], axis=1
     )
+    taps_ref[...] = small[len(line_refs) :]
+    for k, line_ref in enumerate(line_refs):
+        line_ref[...] = small[k]
 
 
 def unpack_strips(packed, heads, size):
@@ -350,8 +354,9 @@
         lambda *refs: unpack_kernel(heads, strips, *refs),
         out_shape=[
             jax.ShapeDtypeStruct((2 * heads, size, size), WIDE),
-            jax.ShapeDtypeStruct((SUB, heads * size), WIDE),
-        ],
+            jax.ShapeDtypeStruct((SUB - 4, heads * size), WIDE),
+        ]
+        + [jax.ShapeDtypeStruct((heads * size,), WIDE)] * 4,
         scratch_shapes=[pltpu.VMEM((strips * depth, size), WIDE)],
         compiler_params=pltpu.CompilerParams(vmem_limit_bytes=16 * 1024 * 1024),
         cost_estimate=NO_COST,
@@ -472,23 +477,85 @@
     return (at[k], 0)
 
 
-def second_kernel(_, gate_low_ref, up_low_ref, gate_w_ref, up_w_ref, out_ref):
-    total = times_transposed(gate_low_ref[...], gate_w_ref[...]) + times_transposed(up_low_ref[...], up_w_ref[...])
-    out_ref[...] = total.astype(LOW)
-
-
-def second_partial(gate_low, up_low, gate_weight, up_weight):
-    count, units = gate_low.shape
-    features = gate_weight.shape[0]
-    return call_blocks(
-        second_kernel,
-        features // TILE,
-        jnp.zeros((1,), jnp.int32),
-        [((count, units), whole)] * 2 + [((TILE, units), down)] * 2,
-        [(jax.ShapeDtypeStruct((count, features), LOW), (count, TILE), across)],
-        (gate_low, up_low, gate_weight, up_weight),
-        ROOM,
-    )[0]
+def early_kernel(spots_ref, *refs):
+    rows_hbm, lows_hbm, weights_hbm, refs = refs[0], refs[1:3], refs[3:5], refs[5:]
+    partial_hbm, sends_hbm, refs = refs[0], refs[1:3], refs[3:]
+    rows_refs, low_refs, weight_refs, partial_ref, send_refs = refs[0:2], refs[2:4], refs[4:6], refs[6], refs[7:9]
+    in_sems, out_sems = refs[9:]
+    features = partial_ref.shape[1]
+    tiles = features // TILE
+    half = features // 2
+    low_copies = [pltpu.make_async_copy(lows_hbm[k], low_refs[k], in_sems.at[k]) for k in range(2)]
+    weight_copies = [
+        [
+            pltpu.make_async_copy(
+                weights_hbm[k].at[pl.ds(t * TILE, TILE), :],
+                weight_refs[k].at[pl.ds(t * TILE, TILE), :],
+                in_sems.at[2 + 2 * t + k],
+            )
+            for k in range(2)
+        ]
+        for t in range(tiles)
+    ]
+    row_copies = [
+        pltpu.make_async_copy(
+            rows_hbm.at[:, pl.ds(pl.multiple_of(spots_ref[k] * half, half), half)],
+            rows_refs[k],
+            in_sems.at[2 + 2 * tiles + k],
+        )
+        for k in range(2)
+    ]
+    for copy in low_copies + [copy for pair in weight_copies for copy in pair] + row_copies:
+        copy.start()
+    for copy in low_copies:
+        copy.wait()
+    departures = []
+    for t in range(tiles):
+        here = pl.ds(t * TILE, TILE)
+        for copy in weight_copies[t]:
+            copy.wait()
+        total = times_transposed(low_refs[0][...], weight_refs[0][here, :])
+        total += times_transposed(low_refs[1][...], weight_refs[1][here, :])
+        partial_ref[:, here] = total.astype(LOW)
+        departures.append(pltpu.make_async_copy(partial_ref.at[:, here], partial_hbm.at[:, here], out_sems.at[t]))
+        departures[-1].start()
+    for k in range(2):
+        row_copies[k].wait()
+        for t in range(half // TILE):
+            here = pl.ds(t * TILE, TILE)
+            send_refs[k][here, :] = transposed_times(rows_refs[k][:, here], low_refs[k][...]).astype(LOW)
+            departures.append(
+                pltpu.make_async_copy(
+                    send_refs[k].at[here, :], sends_hbm[k].at[here, :], out_sems.at[tiles + k * (half // TILE) + t]
+                )
+            )
+            departures[-1].start()
+    for departure in departures:
+        departure.wait()
+
+
+def early_products(rows, gate_low, up_low, gate_weight, up_weight, spots):
+    count, features = rows.shape
+    units = gate_low.shape[1]
+    half = features // 2
+    made = [((count, features), LOW), ((half, units), LOW), ((half, units), LOW)]
+    anywhere = pl.BlockSpec(memory_space=pl.ANY)
+    return pl.pallas_call(
+        early_kernel,
+        in_specs=[pl.BlockSpec(memory_space=pltpu.SMEM)] + [anywhere] * 5,
+        out_specs=[anywhere] * 3,
+        out_shape=[jax.ShapeDtypeStruct(*one) for one in made],
+        scratch_shapes=[pltpu.VMEM((count, half), LOW)] * 2
+        + [pltpu.VMEM((count, units), LOW)] * 2
+        + [pltpu.VMEM((features, units), LOW)] * 2
+        + [pltpu.VMEM(*one) for one in made]
+        + [
+            pltpu.SemaphoreType.DMA((4 + 2 * (features // TILE),)),
+            pltpu.SemaphoreType.DMA((2 * (features // TILE),)),
+        ],
+        compiler_params=pltpu.CompilerParams(vmem_limit_bytes=ROOM * 1024 * 1024),
+        cost_estimate=NO_COST,
+    )(spots, rows, gate_low, up_low, gate_weight, up_weight)
 
 
 def gradient_kernel(_, left_ref, right_ref, out_ref):
@@ -530,7 +597,7 @@
         [(block, down), (block, down), ((1, features), whole)],
         outs if added is not None else outs[:1],
         (start, start if added is None else added, gain[None]),
-        16,
+        ROOM,
     )
 
 
@@ -563,7 +630,7 @@
         [(jax.ShapeDtypeStruct((rows, features), kind), block, down) for kind in (LOW, WIDE)]
         + [(jax.ShapeDtypeStruct(line, WIDE), line, whole)],
         (start, grad, added, gain[None]),
-        16,
+        ROOM,
     )
 
 
@@ -583,16 +650,30 @@
     return lax.all_gather(values, "mp", axis=0, tiled=True)
 
 
-def place_kernel(pieces, kept, splits, where_ref, *refs):
-    out_refs = refs[pieces + kept :]
-    for k in range(pieces):
-
-        @pl.when(pl.program_id(0) == k)
-        def _():
-            start = 0
-            for out_ref, rows in zip(out_refs, splits):
-                out_ref[...] = refs[k][pl.ds(start, rows), :].astype(out_ref.dtype)
-                start += rows
+def place_kernel(count, axis, splits, kept, spots_ref, *refs):
+    sources, outs, refs = refs[:count], refs[count + kept : count + kept + len(splits)], refs[count + kept + len(splits) :]
+    in_sems, out_sems = refs[-2:]
+    size = sources[0].shape[axis]
+    same = sources[0].dtype == outs[0].dtype
+    held, wide = ((), ()) if same else (refs[:count], refs[count : 2 * count])
+    arrivals = [pltpu.make_async_copy(sources[k], held[k], in_sems.at[k]) for k in range(len(held))]
+    for arrival in arrivals:
+        arrival.start()
+    departures = []
+    for k in range(count):
+        if not same:
+            arrivals[k].wait()
+            wide[k][...] = held[k][...].astype(wide[k].dtype)
+        here = pl.ds(pl.multiple_of(spots_ref[k] * size, size), size)
+        start = 0
+        for j, rows in enumerate(splits):
+            part = (sources[k] if same else wide[k]).at[pl.ds(start, rows), :]
+            target = outs[j].at[here, :] if axis == 0 else outs[j].at[:, here]
+            departures.append(pltpu.make_async_copy(part, target, out_sems.at[k * len(splits) + j]))
+            departures[-1].start()
+            start += rows
+    for departure in departures:
+        departure.wait()
 
 
 def place(pieces, spots, total, axis, splits, kind, onto=()):
@@ -602,20 +683,17 @@
     outs = [
         jax.ShapeDtypeStruct((r * total, columns) if axis == 0 else (r, columns * total), kind) for r in splits
     ]
-    spot = (lambda k, at: (at[k], 0)) if axis == 0 else (lambda k, at: (0, at[k]))
-    room = rows * columns * (2 * 2 * count + 4 * 2) + 3 * 1024 * 1024
+    anywhere = pl.BlockSpec(memory_space=pl.ANY)
+    scratch = [] if pieces[0].dtype == kind else [pltpu.VMEM((rows, columns), LOW)] * count + [pltpu.VMEM((rows, columns), kind)] * count
     return pl.pallas_call(
-        lambda *refs: place_kernel(count, len(onto), splits, *refs),
-        grid_spec=pltpu.PrefetchScalarGridSpec(
-            num_scalar_prefetch=1,
-            grid=(count,),
-            in_specs=[pl.BlockSpec((rows, columns), lambda k, at: (0, 0))] * count
-            + [pl.BlockSpec(memory_space=pl.ANY)] * len(onto),
-            out_specs=[pl.BlockSpec((r, columns), spot) for r in splits],
-        ),
+        lambda *refs: place_kernel(count, axis, splits, len(onto), *refs),
+        in_specs=[pl.BlockSpec(memory_space=pltpu.SMEM)] + [anywhere] * (count + len(onto)),
+        out_specs=[anywhere] * len(outs),
         out_shape=outs,
+        scratch_shapes=scratch
+        + [pltpu.SemaphoreType.DMA((count,)), pltpu.SemaphoreType.DMA((count * len(splits),))],
         input_output_aliases={1 + count + k: k for k in range(len(onto))},
-        compiler_params=pltpu.CompilerParams(vmem_limit_bytes=room),
+        compiler_params=pltpu.CompilerParams(vmem_limit_bytes=rows * columns * 6 * count + 4 * 1024 * 1024),
         cost_estimate=NO_COST,
     )(jnp.stack(spots).astype(jnp.int32), *pieces, *onto)
 
@@ -665,11 +743,13 @@
 
     def land(self, got):
         self.step += 1
-        total = (self.kept.astype(WIDE) + got.astype(WIDE)).astype(LOW)
         if self.step < len(self.order):
-            self.send, self.kept = split_for(total, self.axis, self.order[self.step])
+            pairs = [split_for(values, self.axis, self.order[self.step]) for values in (self.kept, got)]
+            self.send, self.kept = (
+                (left.astype(WIDE) + right.astype(WIDE)).astype(LOW) for left, right in zip(*pairs)
+            )
         else:
-            self.pieces = {0: total}
+            self.pieces = {0: (self.kept.astype(WIDE) + got.astype(WIDE)).astype(LOW)}
 
     def forwards(self, level):
         made = []
@@ -689,14 +769,18 @@
 
 def exchange(reducing=(), gathered=(), extras=()):
     gots = [part.reduce() for part in reducing]
-    kepts = [part.kept for part in reducing]
-    made = lax.optimization_barrier((*gots, *[piece for _, _, piece in gathered], *extras, *kepts))
-    for part, got, kept in zip(reducing, made, made[len(made) - len(kepts) :]):
+    made = lax.optimization_barrier(
+        (*[part.kept for part in reducing], *gots, *[piece for _, _, piece in gathered], *extras)
+    )
+    for part, kept in zip(reducing, made):
         part.kept = kept
+    made = made[len(gots) :]
+    for part, got in zip(reducing, made):
         part.land(got)
-    for (part, mask, _), piece in zip(gathered, made[len(gots) :]):
+    made = made[len(gots) :]
+    for (part, mask, _), piece in zip(gathered, made):
         part.pieces[mask] = piece
-    return made[len(gots) + len(gathered) : len(made) - len(kepts)]
+    return made[len(gathered) :]
 
 
 def reduce_fully(parts):
@@ -769,9 +853,8 @@
     inlet_w = spread_blocks(inlet_weight)
     branches = jnp.concatenate([branch_gate.T, branch_input.T])
 
-    first_rows = tie(first_rows, rate_w, inlet_w, extra, branches)
-    spots = quarter_spots()
-    scalars = jnp.concatenate([spots, lengths[0]])[None]
+    scalars = jnp.concatenate([quarter_spots(), lengths[0]])[None]
+    first_rows = tie(first_rows, rate_w, inlet_w, extra, branches, scalars)
     block_partial, mixed, conv, rate, inlet, state, both = forward_mix(
         scalars, first_rows, branches, block_out, conv_weight, rate_w, inlet_w, extra
     )
@@ -807,20 +890,22 @@
     second_rows, d_hidden = lax.optimization_barrier((second_rows, d_hidden))
     gate_act = times(second_rows, gate_weight)
     up_act = times(second_rows, up_weight)
-    value, bend = gelu_pair(gate_act)
-    hidden = (value * up_act).astype(LOW)
-    gate_low = (d_hidden * up_act * bend).astype(LOW)
-    up_low = (d_hidden * value).astype(LOW)
-
+    hidden = (gelu(gate_act) * up_act).astype(LOW)
     down_parts = []
     for turn, half in enumerate(halves(transposed_times(hidden, grad_rows).astype(LOW), 1)):
         down_parts.append(Part(*split_for(half, 1, order_of(turn)[0]), 1, turn))
+    gate_act, up_act, d_hidden = lax.optimization_barrier(
+        (gate_act, up_act, d_hidden, *[part.send for part in down_parts])
+    )[:3]
+    value, bend = gelu_pair(gate_act)
+    gate_low = (d_hidden * up_act * bend).astype(LOW)
+    up_low = (d_hidden * value).astype(LOW)
+
     late_rows = tie(second_rows, *[part.send for part in down_parts])
     uppers = [upper_of(order_of(turn)[0]) for turn in range(2)]
-    gate_send = gradient_half(late_rows, gate_low, 1 - uppers[0])
-    up_send = gradient_half(tie(late_rows, gate_send), up_low, 1 - uppers[1])
-    partial = second_partial(tie(gate_low, gate_send, up_send), up_low, gate_weight, up_weight)
-    partial, gate_send, up_send = exchange(down_parts, extras=(partial, gate_send, up_send))
+    spots = jnp.stack([1 - upper for upper in uppers]).astype(jnp.int32)
+    made = early_products(late_rows, gate_low, up_low, gate_weight, up_weight, spots)
+    partial, gate_send, up_send = exchange(down_parts, extras=made)
 
     second_input = sum_rows(partial)
     late_rows = tie(second_rows, partial)
@@ -848,15 +933,16 @@
         (middle_rows, block_out, both, conv, rate, inlet, state, mixed, first_rows, branches),
         (conv_weight, rate_w, inlet_w, extra, first_gain[None], second_gain_grad),
     )
-    first_partial, *quarters = exchange(gathered=start_gather(wide_parts, 1), extras=made)
-    first_input = sum_rows(tie(first_partial, out_sum))
+    first_partial, *quarters = made
+    (first_partial,) = exchange(gathered=start_gather(wide_parts, 1), extras=(first_partial,))
+    first_input = sum_rows(first_partial)
     output = (own_middle + out_sum.astype(WIDE)).astype(LOW)
 
     late = column_parts(quarters)
     wide_rest = start_gather(wide_parts, 2)
     exchange(late)
     down_rest = start_gather(down_parts, 2)
-    first_input, output = exchange(late, wide_rest + down_rest, (first_input, output))
+    (first_input,) = exchange(late, wide_rest + down_rest, (first_input,))
     gather_fully(mlp, 3)
     reduce_fully(late)
     first_input = first_input.astype(WIDE)
@@ -874,14 +960,14 @@
     own = [0] + [1 << bit for bit in range(dp_bits())]
     splits = (width, width, width, quarters[0].shape[0] - 3 * width)
     halfway = finish(late, 1, splits, own)
-    made = exchange(gathered=start_gather(late, 2), extras=(swap(gains, 1), up_grad, *halfway))
+    made = exchange(gathered=start_gather(late, 2), extras=(swap(gains, 1), up_grad, *halfway, output))
     gather_fully(late, 3)
-    gains, up_grad = gains + made[0], made[1]
+    gains, up_grad, output = gains + made[0], made[1], made[-1]
     for bit in range(2, dp_bits()):
         gains = gains + swap(gains, bit)
     rest = [mask for mask in late[0].pieces if mask not in own]
-    branch_gate_grad, branch_input_grad, block_grad, packed = finish(late, 1, splits, rest, made[2:])
-    square, small = unpack_strips(packed, heads, width // heads)
+    branch_gate_grad, branch_input_grad, block_grad, packed = finish(late, 1, splits, rest, made[2:-1])
+    square, taps_grad, *lines = unpack_strips(packed, heads, width // heads)
     square = square.reshape(2, heads, *square.shape[1:])
     return (
         output,
@@ -889,13 +975,13 @@
         gains[0],
         branch_gate_grad.T,
         branch_input_grad.T,
-        small[4 : 4 + taps_count],
-        small[0],
+        taps_grad,
+        lines[0],
         square[0],
-        small[1],
+        lines[1],
         square[1],
-        small[2],
-        small[3],
+        lines[2],
+        lines[3],
         block_grad,
         gains[1],
         gate_grad,

time: 450 us -> 435 us (0.967)
  waiting for transfers between devices: 181 us -> 196 us
  starting transfers between devices: 50.2 us -> 35.6 us
  local copies, waits for them, and re-layouts: 34.8 us -> 21.5 us
  Pallas kernels: 101 us -> 94.7 us
    pallas_call x8 -> x5, Pallas kernels: 31 us -> 16.6 us  [call_blocks(): pl.pallas_call(body, grid_spec=pltpu.PrefetchScalarGridSpec(num_scalar_pr...]
    all_gather x3, starting transfers between devices: 13.2 us -> 0.12 us  [all_rows(): return lax.all_gather(values, 'mp', axis=0, tiled=True)]
    reduce_scatter x4, waiting for transfers between devices: 32.2 us -> 44.8 us  [sum_rows(): lax.psum_scatter(values.astype(LOW), 'mp', scatter_dimension=0, tiled=True)]
    unnamed x108 -> x90, local copies, waits for them, and re-layouts: 19 us -> 10.4 us
    pallas_call x6 -> x7, Pallas kernels: 28.3 us -> 35.5 us  [the longest x6 23.1 us: place(): pl.pallas_call(lambda *refs: place_kernel(count, axis, splits, len(onto),...]
    select_n x7 -> x1, other arithmetic: 8.31 us -> 1.52 us  [split_for(): return (jnp.where(upper, first, second), jnp.where(upper, second, first))]
    convert_element_type x11 -> x12, other arithmetic: 21.4 us -> 27.6 us  [the longest x6 17 us: land(): (left.astype(WIDE) + right.astype(WIDE)).astype(LOW)]
  transfers between devices with their start and end apart: 46 -> 46, of which waited for: 17 -> 18; matrix products, arithmetic and copies ran while one was open for 13% -> 14% of each run, Pallas kernels for 22% -> 20%
where the time goes in v4:
time: 435 us; the launch traced here: 428 us
  waiting for transfers between devices  196 us (45%)
  Pallas kernels  94.7 us (22%)
  other arithmetic  44.9 us (10%)
  starting transfers between devices  35.6 us (8%)
  local copies, waits for them, and re-layouts  21.5 us (5%)
  matrix products  19.7 us (5%)
  between operations  15.3 us (4%)
    ppermute x32, waiting for transfers between devices, swap(): return lax.ppermute(values, 'dp', [(i, i ^ 1 << bit) for i in range(count)])  81.6 us
    all_gather x3, waiting for transfers between devices, all_rows(): return lax.all_gather(values, 'mp', axis=0, tiled=True)  50.8 us
    reduce_scatter x4, waiting for transfers between devices, sum_rows(): lax.psum_scatter(values.astype(LOW), 'mp', scatter_dimension=0, tiled=True)  44.8 us
    ppermute x32, starting transfers between devices, swap(): return lax.ppermute(values, 'dp', [(i, i ^ 1 << bit) for i in range(count)])  31.7 us
    pallas_call x1, Pallas kernels, backward_mix(): pl.pallas_call(lambda *refs: backward_kernel(heads, owners, *refs), in_sp...  24.7 us
    pallas_call x6, Pallas kernels, place(): pl.pallas_call(lambda *refs: place_kernel(count, axis, splits, len(onto),...  23.1 us
    pallas_call x1, Pallas kernels, forward_mix(): pl.pallas_call(forward_kernel, in_specs=[pl.BlockSpec(memory_space=pltpu....  17.1 us
    convert_element_type x6, other arithmetic, land(): (left.astype(WIDE) + right.astype(WIDE)).astype(LOW)  17 us
  transfers between devices with their start and end apart: 46, of which 18 were waited for; matrix products, arithmetic and copies ran while one was open for 14% of the time, Pallas kernels for 20%

profile of v4, /device:TPU:0, one launch (start us, length us, event | category | flops | bytes accessed | tf_op | source)
XLA Modules:
  0.0 428.2 jit_solution(582265278158862678)
XLA Ops:
  7.2 2.2 shard_map.305
  19.6 3.7 pad_maximum_fusion.refs_1_.refs_10_
  23.3 28.0 %all-gather.4.cloned.1.call-done.refs_0_.refs_9_ = bf16[768,2048]{1,0:T(8,128)(2,1)} async-done(((bf16[96,2048]{1,0:T(8,128)(2,1)}), bf16[768,2048]{1,0:T(8,128)(2,1)}) %all-gather.4.cloned.1.call-update) | async-done | bytes 3145744 | tf_op jit(solution)/shard_map/all_gather | solution.py:650
  51.3 1.3 collective-permute-start.1
  53.3 17.1 %shard_map.306 = (bf16[768,2048]{1,0:T(8,128)(2,1)}, bf16[768,320]{1,0:T(8,128)(2,1)}, bf16[768,320]{1,0:T(8,128)(2,1)}, f32[768,320]{1,0:T(8,128)}, f32[768,320...) custom-call(s32[1,7]{1,0:T(1,128)} %bitcast.67, bf16[768,2048]{1,0:T(8,128)(2,1)} %all-gather.4.cloned.1.call-done.refs_0_.refs_9_, ...), custom_call_target="tpu_custom_call" | custom-call | tf_op jit(solution)/shard_map/pallas_call | solution.py:395
  70.5 1.4 collective-permute-done.refs_3_
  76.0 14.6 %collective-permute-done.2.refs_5_ = bf16[96,2048]{1,0:T(8,128)(2,1)} collective-permute-done((bf16[96,2048]{1,0:T(8,128)(2,1)}, bf16[96,2048]{1,0:T(8,128)(2,1)}, u32[]{:S(2)}, u32[]{:S(2)}) %collective-permute-start.2) | collective-permute-done | bytes 393248 | tf_op jit(solution)/shard_map/ppermute | solution.py:810
  90.6 26.0 %reduce-scatter.5.cloned.1.call-done.added_ref = bf16[96,2048]{1,0:T(8,128)(2,1)} async-done(((bf16[768,2048]{1,0:T(8,128)(2,1)}), bf16[96,2048]{1,0:T(8,128)(2,1)}) %reduce-scatter.5.cloned.1.call-update) | async-done | bytes 393232 | tf_op jit(solution)/shard_map/reduce_scatter | solution.py:646
  116.6 2.1 shard_map.307
  119.2 1.9 collective-permute-done.6.refs_6_
  125.1 2.4 shard_map.308
  127.5 1.7 copy-done.1
  129.1 4.1 fusion.17
  133.3 22.9 %all-gather.6.cloned.1.call-done.refs_0_.left_ref = bf16[768,2048]{1,0:T(8,128)(2,1)} async-done(((bf16[96,2048]{1,0:T(8,128)(2,1)}), bf16[768,2048]{1,0:T(8,128)(2,1)}) %all-gather.6.cloned.1.call-update) | async-done | bytes 3145744 | tf_op jit(solution)/shard_map/all_gather | solution.py:650
  156.1 5.6 %fusion.18 = f32[768,768]{1,0:T(8,128)S(1)} fusion(bf16[768,2048]{1,0:T(8,128)(2,1)} %all-gather.6.cloned.1.call-done.refs_0_.left_ref, bf16[2048,768]{1,0:T(8,128)(2,1)} %refs_3_.3), kind=kOutput, calls=%fused_computation.68 | convolution fusion | flops 2415919104 | bytes 8650752 | tf_op jit(solution)/shard_map/dot_general | solution.py:27
  161.8 2.9 fusion.5
  164.7 2.9 convolution_convert_fusion
  167.6 1.5 broadcast_select_fusion
  169.1 1.5 collective-permute-start.8
  170.6 1.5 collective-permute-start.7
  172.7 2.9 multiply_convert_fusion
  175.6 12.4 %shard_map.309 = (bf16[768,2048]{1,0:T(8,128)(2,1)}, bf16[1024,768]{1,0:T(8,128)(2,1)}, bf16[1024,768]{1,0:T(8,128)(2,1)}) custom-call(s32[2]{0:T(128)} %pad_add_fusion.spots_ref, bf16[768,2048]{1,0:T(8,128)(2,1)} %all-gather.6.cloned.1.call-done.refs_0_.left_ref, bf16[768,768]{1,0:T(8,128)(2,1)} %get-tuple-element.296.refs_1_.right_ref, ...), custom_call_target="tpu_custom_call" | custom-call | tf_op jit(solution)/shard_map/pallas_call | solution.py:543
  190.2 1.5 collective-permute-start.11
  192.3 2.4 add_convert_fusion.16
  194.7 1.5 collective-permute-start.9
  196.2 2.3 add_convert_fusion.15
  200.2 4.8 %shard_map.311 = bf16[1024,768]{1,0:T(8,128)(2,1)} custom-call(s32[2]{0:T(128)} %pad_add_fusion.2._, bf16[768,2048]{1,0:T(8,128)(2,1)} %all-gather.6.cloned.1.call-done.refs_0_.left_ref, bf16[768,768]{1,0:T(8,128)(2,1)} %get-tuple-element.295.refs_2_.right_ref), custom_call_target="tpu_custom_call" | custom-call | tf_op jit(solution)/shard_map/pallas_call | solution.py:446
  205.0 4.8 %shard_map.310 = bf16[1024,768]{1,0:T(8,128)(2,1)} custom-call(s32[2]{0:T(128)} %pad_add_fusion.1._, bf16[768,2048]{1,0:T(8,128)(2,1)} %all-gather.6.cloned.1.call-done.refs_0_.left_ref, bf16[768,768]{1,0:T(8,128)(2,1)} %get-tuple-element.296.refs_1_.right_ref), custom_call_target="tpu_custom_call" | custom-call | tf_op jit(solution)/shard_map/pallas_call | solution.py:446
  209.8 18.8 %reduce-scatter.7.cloned.1.call-done.grad_ref = bf16[96,2048]{1,0:T(8,128)(2,1)} async-done(((bf16[768,2048]{1,0:T(8,128)(2,1)}), bf16[96,2048]{1,0:T(8,128)(2,1)}) %reduce-scatter.7.cloned.1.call-update) | async-done | bytes 393232 | tf_op jit(solution)/shard_map/reduce_scatter | solution.py:646
  228.6 2.7 shard_map.312
  231.2 4.3 %collective-permute-done.9 = bf16[768,256]{1,0:T(8,128)(2,1)} collective-permute-done((bf16[768,256]{1,0:T(8,128)(2,1)S(1)}, bf16[768,256]{1,0:T(8,128)(2,1)}, u32[]{:S(2)}, u32[]{:S(2)}) %collective-permute-start.9) | collective-permute-done | bytes 393248 | tf_op jit(solution)/shard_map/ppermute | solution.py:707
  235.7 1.2 add_convert_fusion.13.refs_5_
  238.4 3.7 add_convert_fusion.3
  243.2 3.1 add_convert_fusion.2
  246.3 1.5 collective-permute-start.14
  247.8 1.9 add_convert_fusion.14.refs_1_
  251.9 4.2 fusion.19
  256.1 16.0 %collective-permute-done.16.refs_3_ = bf16[768,256]{1,0:T(8,128)(2,1)} collective-permute-done((bf16[768,256]{1,0:T(8,128)(2,1)}, bf16[768,256]{1,0:T(8,128)(2,1)}, u32[]{:S(2)}, u32[]{:S(2)}) %collective-permute-start.16) | collective-permute-done | bytes 393248 | tf_op jit(solution)/shard_map/ppermute | solution.py:707
  272.1 2.5 add_convert_fusion.refs_1_
  275.6 1.2 collective-permute-start.25
  276.8 2.2 add_convert_fusion.1.refs_1_
  280.9 24.7 %shard_map.313 = (bf16[896,2048]{1,0:T(8,128)(2,1)}, bf16[1024,512]{1,0:T(8,128)(2,1)}, bf16[1024,512]{1,0:T(8,128)(2,1)}, bf16[1024,512]{1,0:T(8,128)(2,1)}, bf16[1024,512]{1,0:T(8,128)(2,1)}) custom-call(s32[1,7]{1,0:T(1,128)} %bitcast.68, bf16[768,2048]{1,0:T(8,128)(2,1)} %all-gather.8.cloned.1.call-done.refs_1_, bf16[320,2048]{1,0:T(8,128)(2,1)} %refs_2_.3, ...), custom_call_target="tpu_custom_call" | custom-call | tf_op jit(solution)/shard_map/pallas_call | solution.py:421
  305.6 6.3 %collective-permute-done.24.refs_3_ = bf16[512,768]{1,0:T(8,128)(2,1)} collective-permute-done((bf16[512,768]{1,0:T(8,128)(2,1)}, bf16[512,768]{1,0:T(8,128)(2,1)}, u32[]{:S(2)}, u32[]{:S(2)}) %collective-permute-start.24) | collective-permute-done | bytes 786464 | tf_op jit(solution)/shard_map/ppermute | solution.py:707
  312.7 1.5 collective-permute-start.19
  315.9 1.5 collective-permute-start.27
  317.4 1.5 collective-permute-start.28
  318.9 20.3 %collective-permute-done.19 = bf16[1024,512]{1,0:T(8,128)(2,1)} collective-permute-done((bf16[1024,512]{1,0:T(8,128)(2,1)}, bf16[1024,512]{1,0:T(8,128)(2,1)}, u32[]{:S(2)}, u32[]{:S(2)}) %collective-permute-start.19) | collective-permute-done | bytes 1048608 | tf_op jit(solution)/shard_map/ppermute | solution.py:707
  339.2 1.5 collective-permute-done.20
  340.7 2.9 add_convert_fusion.9
  344.1 2.6 add_convert_fusion.8
  347.6 1.2 collective-permute-start.30
  350.8 24.2 %collective-permute-done.30.refs_8_ = bf16[768,256]{1,0:T(8,128)(2,1)} collective-permute-done((bf16[768,256]{1,0:T(8,128)(2,1)}, bf16[768,256]{1,0:T(8,128)(2,1)}, u32[]{:S(2)}, u32[]{:S(2)}) %collective-permute-start.30) | collective-permute-done | bytes 393248 | tf_op jit(solution)/shard_map/ppermute | solution.py:707
  375.0 1.4 add_convert_fusion.6.refs_4_
  377.5 1.3 add_convert_fusion.7.refs_1_
  378.9 1.7 collective-permute-start.32
  380.6 1.4 collective-permute-start.31
  384.8 4.5 %shard_map.314 = f32[2048,768]{1,0:T(8,128)} custom-call(s32[4]{0:T(128)S(1)} %pad_add_fusion.3.refs_0_, bf16[512,768]{1,0:T(8,128)(2,1)} %add_convert_fusion.1.refs_1_, bf16[512,768]{1,0:T(8,128)(2,1)} %collective-permute-done.23.refs_2_, bf16[512,768]{1,0:T(8,128)(2,1)} %collective-permute-done.24.refs_3_, bf16[512,768]{1,0:T(8,128)(2,1)} %collective-permute-done.27.refs_4_), custom_call_target="tpu_custom_call" | custom-call | tf_op jit(solution)/shard_map/pallas_call | solution.py:688
  389.4 4.4 %shard_map.315 = f32[768,2048]{1,0:T(8,128)} custom-call(s32[8]{0:T(128)S(1)} %stack.186.refs_0_, bf16[768,256]{1,0:T(8,128)(2,1)} %add_convert_fusion.14.refs_1_, bf16[768,256]{1,0:T(8,128)(2,1)} %collective-permute-done.15.refs_2_, bf16[768,256]{1,0:T(8,128)(2,1)} %collective-permute-done.16.refs_3_, bf16[768,256]{1,0:T(8,128)(2,1)} %collective-permute-done.29.refs_4_, ...), custom_call_target="tpu_custom_call" | custom-call | tf_op jit(solution)/shard_map/pallas_call | solution.py:688
  393.8 6.4 %collective-permute-done.35 = f32[2,2048]{1,0:T(2,128)S(1)} collective-permute-done((f32[2,2048]{1,0:T(2,128)S(1)}, f32[2,2048]{1,0:T(2,128)S(1)}, u32[]{:S(2)}, u32[]{:S(2)}) %collective-permute-start.35) | collective-permute-done | bytes 16416 | tf_op jit(solution)/shard_map/ppermute | solution.py:707
  402.3 1.4 collective-permute-start.37
  404.5 2.1 add_convert_fusion.12
  406.5 4.6 %shard_map.316 = f32[2048,768]{1,0:T(8,128)} custom-call(s32[4]{0:T(128)S(1)} %pad_add_fusion.4.refs_0_, bf16[512,768]{1,0:T(8,128)(2,1)} %add_convert_fusion.refs_1_, bf16[512,768]{1,0:T(8,128)(2,1)} %collective-permute-done.25.refs_2_, bf16[512,768]{1,0:T(8,128)(2,1)} %collective-permute-done.26.refs_3_, bf16[512,768]{1,0:T(8,128)(2,1)} %collective-permute-done.28.refs_4_), custom_call_target="tpu_custom_call" | custom-call | tf_op jit(solution)/shard_map/pallas_call | solution.py:688
  411.3 4.1 shard_map.317
  416.1 3.0 shard_map.318
  (200 shorter events, 47.3 us)
Async XLA Ops:
  7.2 122.0 %copy-start = (bf16[768,2048]{1,0:T(8,128)(2,1)S(1)}, bf16[768,2048]{1,0:T(8,128)(2,1)}, u32[]{:S(2)}) copy-start(bf16[768,2048]{1,0:T(8,128)(2,1)} %param.42) | copy-start | bytes 9437188
  7.2 44.1 %all-gather.4.cloned.1.call-start = ((), (), s32[]{:S(2)}) async-start(), calls=%async_computation.4 | async-start | bytes 3538944 | tf_op jit(solution)/shard_map/all_gather | solution.py:650
  9.5 8.9 %copy-start.42 = (s32[1,3]{1,0:T(1,128)S(1)}, s32[1,3]{1,0:T(1,128)}, u32[]{:S(2)}) copy-start(s32[1,3]{1,0:T(1,128)} %param.27) | copy-start | bytes 40
  9.5 107.1 %reduce-scatter.5.cloned.1.call-start = ((), (), s32[]{:S(2)}) async-start(), calls=%async_computation.5 | async-start | bytes 3538944 | tf_op jit(solution)/shard_map/reduce_scatter | solution.py:646
  19.6 31.6 %copy-start.7 = (bf16[96,2048]{1,0:T(8,128)(2,1)S(1)}, bf16[96,2048]{1,0:T(8,128)(2,1)}, u32[]{:S(2)}) copy-start(bf16[96,2048]{1,0:T(8,128)(2,1)} %added_ref.3) | copy-start | bytes 1179652
  51.3 19.2 %collective-permute-start.1 = (bf16[96,2048]{1,0:T(8,128)(2,1)S(1)}, bf16[96,2048]{1,0:T(8,128)(2,1)S(1)}, u32[]{:S(2)}, u32[]{:S(2)}) collective-permute-start(bf16[96,2048]{1,0:T(8,128)(2,1)S(1)} %copy-done.7), channel_id=1, source_target_pairs={{0,6},{1,7},{2,0},{3,1},{4,2},{5,3},{6,4},{7,5},{8,14},{9,15},{10,... | collective-permute-start | bytes 1179656 | tf_op jit(solution)/shard_map/ppermute | solution.py:810
  52.6 19.2 %collective-permute-start = (bf16[96,2048]{1,0:T(8,128)(2,1)S(1)}, bf16[96,2048]{1,0:T(8,128)(2,1)}, u32[]{:S(2)}, u32[]{:S(2)}) collective-permute-start(bf16[96,2048]{1,0:T(8,128)(2,1)S(1)} %copy-done.7), channel_id=1, source_target_pairs={{0,2},{1,3},{2,4},{3,5},{4,6},{5,7},{6,0},{7,1},{8,10},{9,11},{10,... | collective-permute-start | bytes 1179656 | tf_op jit(solution)/shard_map/ppermute | solution.py:810
  71.9 84.3 %all-gather.6.cloned.1.call-start = ((), (), s32[]{:S(2)}) async-start(), calls=%async_computation.6 | async-start | bytes 3538944 | tf_op jit(solution)/shard_map/all_gather | solution.py:650
  71.9 1.8 collective-permute-start.3
  72.0 2.5 collective-permute-start.5
  72.5 2.7 collective-permute-start.4
  72.6 18.0 %collective-permute-start.2 = (bf16[96,2048]{1,0:T(8,128)(2,1)}, bf16[96,2048]{1,0:T(8,128)(2,1)}, u32[]{:S(2)}, u32[]{:S(2)}) collective-permute-start(bf16[96,2048]{1,0:T(8,128)(2,1)} %collective-permute-done.refs_3_), channel_id=1, source_target_pairs={{0,2},{1,3},{2,4},{3,5},{4,6},{5,7},{6,0},{7,1},{8,10},{9,11},{10,... | collective-permute-start | bytes 1179656 | tf_op jit(solution)/shard_map/ppermute | solution.py:810
  118.7 109.9 %reduce-scatter.7.cloned.1.call-start = ((), (), s32[]{:S(2)}) async-start(), calls=%async_computation.7 | async-start | bytes 3538944 | tf_op jit(solution)/shard_map/reduce_scatter | solution.py:646
  118.9 2.1 collective-permute-start.6
  156.1 5.6 %copy-start.27 = (bf16[2048,768]{1,0:T(8,128)(2,1)S(1)}, bf16[2048,768]{1,0:T(8,128)(2,1)}, u32[]{:S(2)}) copy-start(bf16[2048,768]{1,0:T(8,128)(2,1)} %refs_4_.1) | copy-start | bytes 9437188
  169.1 20.0 %collective-permute-start.8 = (bf16[768,512]{1,0:T(8,128)(2,1)}, bf16[768,512]{1,0:T(8,128)(2,1)}, u32[]{:S(2)}, u32[]{:S(2)}) collective-permute-start(bf16[768,512]{1,0:T(8,128)(2,1)} %get-tuple-element.301), channel_id=1, source_target_pairs={{0,16},{8,24},{16,0},{24,8},{1,17},{9,25},{17,1},{25,9},{2,18},{10... | collective-permute-start | bytes 2359304 | tf_op jit(solution)/shard_map/ppermute | solution.py:707
  170.6 19.5 %collective-permute-start.7 = (bf16[768,512]{1,0:T(8,128)(2,1)S(1)}, bf16[768,512]{1,0:T(8,128)(2,1)}, u32[]{:S(2)}, u32[]{:S(2)}) collective-permute-start(bf16[768,512]{1,0:T(8,128)(2,1)S(1)} %get-tuple-element.303), channel_id=1, source_target_pairs={{0,8},{8,0},{16,24},{24,16},{1,9},{9,1},{17,25},{25,17},{2,10},{10... | collective-permute-start | bytes 2359304 | tf_op jit(solution)/shard_map/ppermute | solution.py:707
  190.1 82.0 %all-gather.8.cloned.1.call-start = ((), (), s32[]{:S(2)}) async-start(), calls=%async_computation.8 | async-start | bytes 3538944 | tf_op jit(solution)/shard_map/all_gather | solution.py:650
  190.2 6.0 %copy-start.28 = (bf16[768,512]{1,0:T(8,128)(2,1)S(1)}, bf16[768,512]{1,0:T(8,128)(2,1)}, u32[]{:S(2)}) copy-start(bf16[768,512]{1,0:T(8,128)(2,1)} %get-tuple-element.203) | copy-start | bytes 2359300
  190.2 45.4 %collective-permute-start.11 = (bf16[1024,768]{1,0:T(8,128)(2,1)}, bf16[1024,768]{1,0:T(8,128)(2,1)}, u32[]{:S(2)}, u32[]{:S(2)}) collective-permute-start(bf16[1024,768]{1,0:T(8,128)(2,1)} %get-tuple-element.207), channel_id=1, source_target_pairs={{0,8},{8,0},{16,24},{24,16},{1,9},{9,1},{17,25},{25,17},{2,10},{10... | collective-permute-start | bytes 4718600 | tf_op jit(solution)/shard_map/ppermute | solution.py:707
  191.7 43.9 %collective-permute-start.12 = (bf16[1024,768]{1,0:T(8,128)(2,1)}, bf16[1024,768]{1,0:T(8,128)(2,1)}, u32[]{:S(2)}, u32[]{:S(2)}) collective-permute-start(bf16[1024,768]{1,0:T(8,128)(2,1)} %get-tuple-element.208), channel_id=1, source_target_pairs={{0,16},{8,24},{16,0},{24,8},{1,17},{9,25},{17,1},{25,9},{2,18},{10... | collective-permute-start | bytes 4718600 | tf_op jit(solution)/shard_map/ppermute | solution.py:707
  194.7 40.9 %collective-permute-start.9 = (bf16[768,256]{1,0:T(8,128)(2,1)S(1)}, bf16[768,256]{1,0:T(8,128)(2,1)}, u32[]{:S(2)}, u32[]{:S(2)}) collective-permute-start(bf16[768,256]{1,0:T(8,128)(2,1)S(1)} %get-tuple-element.311), channel_id=1, source_target_pairs={{0,16},{8,24},{16,0},{24,8},{1,17},{9,25},{17,1},{25,9},{2,18},{10... | collective-permute-start | bytes 1179656 | tf_op jit(solution)/shard_map/ppermute | solution.py:707
  198.5 37.1 %collective-permute-start.10 = (bf16[768,256]{1,0:T(8,128)(2,1)}, bf16[768,256]{1,0:T(8,128)(2,1)}, u32[]{:S(2)}, u32[]{:S(2)}) collective-permute-start(bf16[768,256]{1,0:T(8,128)(2,1)} %get-tuple-element.309), channel_id=1, source_target_pairs={{0,8},{8,0},{16,24},{24,16},{1,9},{9,1},{17,25},{25,17},{2,10},{10... | collective-permute-start | bytes 1179656 | tf_op jit(solution)/shard_map/ppermute | solution.py:707
  235.6 139.4 %reduce-scatter.9.cloned.1.call-start = ((), (), s32[]{:S(2)}) async-start(), calls=%async_computation.9 | async-start | bytes 4128768 | tf_op jit(solution)/shard_map/reduce_scatter | solution.py:646
  236.9 6.3 %copy-start.25 = (bf16[1024,768]{1,0:T(8,128)(2,1)S(1)}, bf16[1024,768]{1,0:T(8,128)(2,1)}, u32[]{:S(2)}) copy-start(bf16[1024,768]{1,0:T(8,128)(2,1)} %shard_map.311) | copy-start | bytes 4718596
  236.9 13.3 %collective-permute-start.18 = (bf16[768,256]{1,0:T(8,128)(2,1)S(1)}, bf16[768,256]{1,0:T(8,128)(2,1)S(1)}, u32[]{:S(2)}, u32[]{:S(2)}) collective-permute-start(bf16[768,256]{1,0:T(8,128)(2,1)S(1)} %add_convert_fusion.13.refs_5_), channel_id=1, source_target_pairs={{0,16},{8,24},{16,0},{24,8},{1,17},{9,25},{17,1},{25,9},{2,18},{10... | collective-permute-start | bytes 1179656 | tf_op jit(solution)/shard_map/ppermute | solution.py:707
  237.8 18.3 %collective-permute-start.17 = (bf16[768,256]{1,0:T(8,128)(2,1)S(1)}, bf16[768,256]{1,0:T(8,128)(2,1)}, u32[]{:S(2)}, u32[]{:S(2)}) collective-permute-start(bf16[768,256]{1,0:T(8,128)(2,1)S(1)} %add_convert_fusion.13.refs_5_), channel_id=1, source_target_pairs={{0,8},{8,0},{16,24},{24,16},{1,9},{9,1},{17,25},{25,17},{2,10},{10... | collective-permute-start | bytes 1179656 | tf_op jit(solution)/shard_map/ppermute | solution.py:707
  242.0 5.7 %copy-start.30 = (bf16[768,256]{1,0:T(8,128)(2,1)S(1)}, bf16[768,256]{1,0:T(8,128)(2,1)}, u32[]{:S(2)}) copy-start(bf16[768,256]{1,0:T(8,128)(2,1)} %get-tuple-element.217) | copy-start | bytes 1179652
  242.0 9.8 %copy-start.44 = (bf16[768,768]{1,0:T(8,128)(2,1)S(1)}, bf16[768,768]{1,0:T(8,128)(2,1)}, u32[]{:S(2)}) copy-start(bf16[768,768]{1,0:T(8,128)(2,1)} %copy-done.43) | copy-start | bytes 3538948
  242.0 30.0 %collective-permute-start.13 = (bf16[512,768]{1,0:T(8,128)(2,1)}, bf16[512,768]{1,0:T(8,128)(2,1)}, u32[]{:S(2)}, u32[]{:S(2)}) collective-permute-start(bf16[512,768]{1,0:T(8,128)(2,1)} %get-tuple-element.299), channel_id=1, source_target_pairs={{0,16},{8,24},{16,0},{24,8},{1,17},{9,25},{17,1},{25,9},{2,18},{10... | collective-permute-start | bytes 2359304 | tf_op jit(solution)/shard_map/ppermute | solution.py:707
  246.3 25.8 %collective-permute-start.14 = (bf16[512,768]{1,0:T(8,128)(2,1)}, bf16[512,768]{1,0:T(8,128)(2,1)}, u32[]{:S(2)}, u32[]{:S(2)}) collective-permute-start(bf16[512,768]{1,0:T(8,128)(2,1)} %get-tuple-element.297), channel_id=1, source_target_pairs={{0,8},{8,0},{16,24},{24,16},{1,9},{9,1},{17,25},{25,17},{2,10},{10... | collective-permute-start | bytes 2359304 | tf_op jit(solution)/shard_map/ppermute | solution.py:707
  249.6 22.4 %collective-permute-start.16 = (bf16[768,256]{1,0:T(8,128)(2,1)}, bf16[768,256]{1,0:T(8,128)(2,1)}, u32[]{:S(2)}, u32[]{:S(2)}) collective-permute-start(bf16[768,256]{1,0:T(8,128)(2,1)} %add_convert_fusion.14.refs_1_), channel_id=1, source_target_pairs={{0,8},{8,0},{16,24},{24,16},{1,9},{9,1},{17,25},{25,17},{2,10},{10... | collective-permute-start | bytes 1179656 | tf_op jit(solution)/shard_map/ppermute | solution.py:707
  251.0 21.1 %collective-permute-start.15 = (bf16[768,256]{1,0:T(8,128)(2,1)}, bf16[768,256]{1,0:T(8,128)(2,1)}, u32[]{:S(2)}, u32[]{:S(2)}) collective-permute-start(bf16[768,256]{1,0:T(8,128)(2,1)} %add_convert_fusion.14.refs_1_), channel_id=1, source_target_pairs={{0,16},{8,24},{16,0},{24,8},{1,17},{9,25},{17,1},{25,9},{2,18},{10... | collective-permute-start | bytes 1179656 | tf_op jit(solution)/shard_map/ppermute | solution.py:707
  274.6 30.9 %collective-permute-start.26 = (bf16[512,768]{1,0:T(8,128)(2,1)}, bf16[512,768]{1,0:T(8,128)(2,1)}, u32[]{:S(2)}, u32[]{:S(2)}) collective-permute-start(bf16[512,768]{1,0:T(8,128)(2,1)} %add_convert_fusion.refs_1_), channel_id=1, source_target_pairs={{0,16},{8,24},{16,0},{24,8},{1,17},{9,25},{17,1},{25,9},{2,18},{10... | collective-permute-start | bytes 2359304 | tf_op jit(solution)/shard_map/ppermute | solution.py:707
  275.6 30.0 %collective-permute-start.25 = (bf16[512,768]{1,0:T(8,128)(2,1)}, bf16[512,768]{1,0:T(8,128)(2,1)}, u32[]{:S(2)}, u32[]{:S(2)}) collective-permute-start(bf16[512,768]{1,0:T(8,128)(2,1)} %add_convert_fusion.refs_1_), channel_id=1, source_target_pairs={{0,8},{8,0},{16,24},{24,16},{1,9},{9,1},{17,25},{25,17},{2,10},{10... | collective-permute-start | bytes 2359304 | tf_op jit(solution)/shard_map/ppermute | solution.py:707
  279.0 32.9 %collective-permute-start.24 = (bf16[512,768]{1,0:T(8,128)(2,1)}, bf16[512,768]{1,0:T(8,128)(2,1)}, u32[]{:S(2)}, u32[]{:S(2)}) collective-permute-start(bf16[512,768]{1,0:T(8,128)(2,1)} %add_convert_fusion.1.refs_1_), channel_id=1, source_target_pairs={{0,8},{8,0},{16,24},{24,16},{1,9},{9,1},{17,25},{25,17},{2,10},{10... | collective-permute-start | bytes 2359304 | tf_op jit(solution)/shard_map/ppermute | solution.py:707
  279.8 32.1 %collective-permute-start.23 = (bf16[512,768]{1,0:T(8,128)(2,1)}, bf16[512,768]{1,0:T(8,128)(2,1)}, u32[]{:S(2)}, u32[]{:S(2)}) collective-permute-start(bf16[512,768]{1,0:T(8,128)(2,1)} %add_convert_fusion.1.refs_1_), channel_id=1, source_target_pairs={{0,16},{8,24},{16,0},{24,8},{1,17},{9,25},{17,1},{25,9},{2,18},{10... | collective-permute-start | bytes 2359304 | tf_op jit(solution)/shard_map/ppermute | solution.py:707
  312.0 92.5 %reduce-scatter.11.cloned.1.call-start = ((), (), s32[]{:S(2)}) async-start(), calls=%async_computation.10 | async-start | bytes 3538944 | tf_op jit(solution)/shard_map/reduce_scatter | solution.py:646
  312.7 26.5 %collective-permute-start.19 = (bf16[1024,512]{1,0:T(8,128)(2,1)}, bf16[1024,512]{1,0:T(8,128)(2,1)}, u32[]{:S(2)}, u32[]{:S(2)}) collective-permute-start(bf16[1024,512]{1,0:T(8,128)(2,1)} %get-tuple-element.233), channel_id=1, source_target_pairs={{0,8},{8,0},{16,24},{24,16},{1,9},{9,1},{17,25},{25,17},{2,10},{10... | collective-permute-start | bytes 3145736 | tf_op jit(solution)/shard_map/ppermute | solution.py:707
  314.2 26.4 %collective-permute-start.20 = (bf16[1024,512]{1,0:T(8,128)(2,1)}, bf16[1024,512]{1,0:T(8,128)(2,1)}, u32[]{:S(2)}, u32[]{:S(2)}) collective-permute-start(bf16[1024,512]{1,0:T(8,128)(2,1)} %get-tuple-element.234), channel_id=1, source_target_pairs={{0,16},{8,24},{16,0},{24,8},{1,17},{9,25},{17,1},{25,9},{2,18},{10... | collective-permute-start | bytes 3145736 | tf_op jit(solution)/shard_map/ppermute | solution.py:707
  314.8 29.3 %copy-start.31 = (bf16[1024,512]{1,0:T(8,128)(2,1)S(1)}, bf16[1024,512]{1,0:T(8,128)(2,1)}, u32[]{:S(2)}) copy-start(bf16[1024,512]{1,0:T(8,128)(2,1)} %get-tuple-element.237) | copy-start | bytes 3145732
  315.4 32.2 %collective-permute-start.29 = (bf16[768,256]{1,0:T(8,128)(2,1)}, bf16[768,256]{1,0:T(8,128)(2,1)}, u32[]{:S(2)}, u32[]{:S(2)}) collective-permute-start(bf16[768,256]{1,0:T(8,128)(2,1)} %collective-permute-done.15.refs_2_), channel_id=1, source_target_pairs={{0,8},{8,0},{16,24},{24,16},{1,9},{9,1},{17,25},{25,17},{2,10},{10... | collective-permute-start | bytes 1179656 | tf_op jit(solution)/shard_map/ppermute | solution.py:707
  315.9 59.0 %collective-permute-start.27 = (bf16[512,768]{1,0:T(8,128)(2,1)}, bf16[512,768]{1,0:T(8,128)(2,1)}, u32[]{:S(2)}, u32[]{:S(2)}) collective-permute-start(bf16[512,768]{1,0:T(8,128)(2,1)} %collective-permute-done.23.refs_2_), channel_id=1, source_target_pairs={{0,8},{8,0},{16,24},{24,16},{1,9},{9,1},{17,25},{25,17},{2,10},{10... | collective-permute-start | bytes 2359304 | tf_op jit(solution)/shard_map/ppermute | solution.py:707
  317.4 57.6 %collective-permute-start.28 = (bf16[512,768]{1,0:T(8,128)(2,1)}, bf16[512,768]{1,0:T(8,128)(2,1)}, u32[]{:S(2)}, u32[]{:S(2)}) collective-permute-start(bf16[512,768]{1,0:T(8,128)(2,1)} %collective-permute-done.25.refs_2_), channel_id=1, source_target_pairs={{0,16},{8,24},{16,0},{24,8},{1,17},{9,25},{17,1},{25,9},{2,18},{10... | collective-permute-start | bytes 2359304 | tf_op jit(solution)/shard_map/ppermute | solution.py:707
  343.5 31.4 %collective-permute-start.21 = (bf16[1024,256]{1,0:T(8,128)(2,1)}, bf16[1024,256]{1,0:T(8,128)(2,1)}, u32[]{:S(2)}, u32[]{:S(2)}) collective-permute-start(bf16[1024,256]{1,0:T(8,128)(2,1)} %get-tuple-element.307), channel_id=1, source_target_pairs={{0,16},{8,24},{16,0},{24,8},{1,17},{9,25},{17,1},{25,9},{2,18},{10... | collective-permute-start | bytes 1572872 | tf_op jit(solution)/shard_map/ppermute | solution.py:707
  346.7 28.3 %collective-permute-start.22 = (bf16[1024,256]{1,0:T(8,128)(2,1)}, bf16[1024,256]{1,0:T(8,128)(2,1)}, u32[]{:S(2)}, u32[]{:S(2)}) collective-permute-start(bf16[1024,256]{1,0:T(8,128)(2,1)} %get-tuple-element.305), channel_id=1, source_target_pairs={{0,8},{8,0},{16,24},{24,16},{1,9},{9,1},{17,25},{25,17},{2,10},{10... | collective-permute-start | bytes 1572872 | tf_op jit(solution)/shard_map/ppermute | solution.py:707
  347.6 27.3 %collective-permute-start.30 = (bf16[768,256]{1,0:T(8,128)(2,1)}, bf16[768,256]{1,0:T(8,128)(2,1)}, u32[]{:S(2)}, u32[]{:S(2)}) collective-permute-start(bf16[768,256]{1,0:T(8,128)(2,1)} %collective-permute-done.17.refs_6_), channel_id=1, source_target_pairs={{0,16},{8,24},{16,0},{24,8},{1,17},{9,25},{17,1},{25,9},{2,18},{10... | collective-permute-start | bytes 1179656 | tf_op jit(solution)/shard_map/ppermute | solution.py:707
  375.0 7.0 %copy-start.33 = (bf16[112,2048]{1,0:T(8,128)(2,1)S(1)}, bf16[112,2048]{1,0:T(8,128)(2,1)}, u32[]{:S(2)}) copy-start(bf16[112,2048]{1,0:T(8,128)(2,1)} %reduce-scatter.9.cloned.1.call-done) | copy-start | bytes 1376260
  375.0 7.1 %copy-start.24 = (bf16[96,2048]{1,0:T(8,128)(2,1)S(1)}, bf16[96,2048]{1,0:T(8,128)(2,1)}, u32[]{:S(2)}) copy-start(bf16[96,2048]{1,0:T(8,128)(2,1)} %start_ref.3) | copy-start | bytes 1179652
  375.0 7.1 %copy-start.41 = (f32[96]{0:T(128)S(1)}, f32[96]{0:T(128)}, u32[]{:S(2)}) copy-start(f32[96]{0:T(128)} %add_rsqrt_fusion) | copy-start | bytes 1156
  376.5 8.3 %copy-start.3 = (bf16[1024,256]{1,0:T(8,128)(2,1)}, bf16[1024,256]{1,0:T(8,128)(2,1)S(1)}, u32[]{:S(2)}) copy-start(bf16[1024,256]{1,0:T(8,128)(2,1)S(1)} %add_convert_fusion.6.refs_4_) | copy-start | bytes 1572868
  376.5 7.2 %copy-start.32 = (f32[96,2048]{1,0:T(8,128)S(1)}, f32[96,2048]{1,0:T(8,128)}, u32[]{:S(2)}) copy-start(f32[96,2048]{1,0:T(8,128)} %get-tuple-element.259) | copy-start | bytes 2359300
  376.5 7.2 %copy-start.34 = (f32[2048]{0:T(1024)S(1)}, f32[2048]{0:T(1024)}, u32[]{:S(2)}) copy-start(f32[2048]{0:T(1024)} %param.28) | copy-start | bytes 24580
  376.5 23.7 %collective-permute-start.34 = (bf16[1024,256]{1,0:T(8,128)(2,1)S(1)}, bf16[1024,256]{1,0:T(8,128)(2,1)S(1)}, u32[]{:S(2)}, u32[]{:S(2)}) collective-permute-start(bf16[1024,256]{1,0:T(8,128)(2,1)S(1)} %add_convert_fusion.6.refs_4_), channel_id=1, source_target_pairs={{0,16},{8,24},{16,0},{24,8},{1,17},{9,25},{17,1},{25,9},{2,18},{10... | collective-permute-start | bytes 1572872 | tf_op jit(solution)/shard_map/ppermute | solution.py:707
  377.2 23.9 %collective-permute-start.33 = (bf16[1024,256]{1,0:T(8,128)(2,1)S(1)}, bf16[1024,256]{1,0:T(8,128)(2,1)}, u32[]{:S(2)}, u32[]{:S(2)}) collective-permute-start(bf16[1024,256]{1,0:T(8,128)(2,1)S(1)} %add_convert_fusion.6.refs_4_), channel_id=1, source_target_pairs={{0,8},{8,0},{16,24},{24,16},{1,9},{9,1},{17,25},{25,17},{2,10},{10... | collective-permute-start | bytes 1572872 | tf_op jit(solution)/shard_map/ppermute | solution.py:707
  378.9 5.9 %copy-start.5 = (bf16[1024,256]{1,0:T(8,128)(2,1)}, bf16[1024,256]{1,0:T(8,128)(2,1)S(1)}, u32[]{:S(2)}) copy-start(bf16[1024,256]{1,0:T(8,128)(2,1)S(1)} %add_convert_fusion.7.refs_1_) | copy-start | bytes 1572868
  378.9 22.2 %collective-permute-start.32 = (bf16[1024,256]{1,0:T(8,128)(2,1)S(1)}, bf16[1024,256]{1,0:T(8,128)(2,1)S(1)}, u32[]{:S(2)}, u32[]{:S(2)}) collective-permute-start(bf16[1024,256]{1,0:T(8,128)(2,1)S(1)} %add_convert_fusion.7.refs_1_), channel_id=1, source_target_pairs={{0,8},{8,0},{16,24},{24,16},{1,9},{9,1},{17,25},{25,17},{2,10},{10... | collective-permute-start | bytes 1572872 | tf_op jit(solution)/shard_map/ppermute | solution.py:707
  380.6 21.2 %collective-permute-start.31 = (bf16[1024,256]{1,0:T(8,128)(2,1)S(1)}, bf16[1024,256]{1,0:T(8,128)(2,1)}, u32[]{:S(2)}, u32[]{:S(2)}) collective-permute-start(bf16[1024,256]{1,0:T(8,128)(2,1)S(1)} %add_convert_fusion.7.refs_1_), channel_id=1, source_target_pairs={{0,16},{8,24},{16,0},{24,8},{1,17},{9,25},{17,1},{25,9},{2,18},{10... | collective-permute-start | bytes 1572872 | tf_op jit(solution)/shard_map/ppermute | solution.py:707
  383.2 20.6 %copy-start.35 = (f32[1,2048]{1,0:T(1,128)}, f32[1,2048]{1,0:T(1,128)S(1)}, u32[]{:S(2)}) copy-start(f32[1,2048]{1,0:T(1,128)S(1)} %get-tuple-element.313) | copy-start | bytes 24580
  383.2 20.6 %copy-start.37 = (f32[1,2048]{1,0:T(1,128)}, f32[1,2048]{1,0:T(1,128)S(1)}, u32[]{:S(2)}) copy-start(f32[1,2048]{1,0:T(1,128)S(1)} %get-tuple-element.314) | copy-start | bytes 24580
  383.2 17.0 %collective-permute-start.35 = (f32[2,2048]{1,0:T(2,128)S(1)}, f32[2,2048]{1,0:T(2,128)S(1)}, u32[]{:S(2)}, u32[]{:S(2)}) collective-permute-start(f32[2,2048]{1,0:T(2,128)S(1)} %pad_maximum_fusion.1), channel_id=1, source_target_pairs={{0,8},{8,0},{16,24},{24,16},{1,9},{9,1},{17,25},{25,17},{2,10},{10... | collective-permute-start | bytes 49160 | tf_op jit(solution)/shard_map/ppermute | solution.py:707
  401.8 13.6 %collective-permute-start.36 = (bf16[1024,256]{1,0:T(8,128)(2,1)}, bf16[1024,256]{1,0:T(8,128)(2,1)}, u32[]{:S(2)}, u32[]{:S(2)}) collective-permute-start(bf16[1024,256]{1,0:T(8,128)(2,1)} %collective-permute-done.31.refs_2_), channel_id=1, source_target_pairs={{0,8},{8,0},{16,24},{24,16},{1,9},{9,1},{17,25},{25,17},{2,10},{10... | collective-permute-start | bytes 1572872 | tf_op jit(solution)/shard_map/ppermute | solution.py:707
  402.3 13.1 %collective-permute-start.37 = (bf16[1024,256]{1,0:T(8,128)(2,1)}, bf16[1024,256]{1,0:T(8,128)(2,1)}, u32[]{:S(2)}, u32[]{:S(2)}) collective-permute-start(bf16[1024,256]{1,0:T(8,128)(2,1)} %collective-permute-done.33.refs_5_), channel_id=1, source_target_pairs={{0,16},{8,24},{16,0},{24,8},{1,17},{9,25},{17,1},{25,9},{2,18},{10... | collective-permute-start | bytes 1572872 | tf_op jit(solution)/shard_map/ppermute | solution.py:707
  403.8 11.6 %collective-permute-start.38 = (f32[2,2048]{1,0:T(2,128)S(1)}, f32[2,2048]{1,0:T(2,128)S(1)}, u32[]{:S(2)}, u32[]{:S(2)}) collective-permute-start(f32[2,2048]{1,0:T(2,128)S(1)} %fusion.14), channel_id=1, source_target_pairs={{0,16},{8,24},{16,0},{24,8},{1,17},{9,25},{17,1},{25,9},{2,18},{10... | collective-permute-start | bytes 49160 | tf_op jit(solution)/shard_map/ppermute | solution.py:707
  (27 other events, 77.2 us)
Sparse Core Ops, SparseCore 0:
  10.3 40.9 all-gather.3
  72.0 44.5 reduce-scatter.4
  118.8 37.2 all-gather.5
  190.3 38.2 reduce-scatter.6
  235.7 35.5 all-gather.7
  312.1 43.0 reduce-scatter.8
  358.0 38.6 reduce-scatter.10

commit v5 on v4

--- a/solution.py
+++ b/solution.py
@@ -20,7 +20,7 @@
 SPARE = 16
 ROOM = 60
 TILE = 512
-LOAD = 192
+LOAD = 384
 
 
 def times(left, right):
@@ -57,11 +57,11 @@
     return scale * (lifted - unit * jnp.mean(lifted * unit, axis=-1, keepdims=True))
 
 
-def one_minus_exp(y):
-    series = 1.0 - y * (1.0 / 9.0)
-    for order in range(8, 1, -1):
+def one_minus_square(carry, y):
+    series = 1.0 - y * (1.0 / 6.0)
+    for order in range(5, 1, -1):
         series = 1.0 - y * (1.0 / order) * series
-    return jnp.where(y < 0.5, y * series, 1.0 - jnp.exp(-y))
+    return jnp.where(y < 0.25, y * series, 1.0 - carry * carry)
 
 
 def row_positions(scalars_ref, base, rows, width):
@@ -76,9 +76,9 @@
 
 def gates(rate, inlet, soft, fresh):
     log_a = -rate * soft
-    carry = jnp.where(fresh, 0.0, jnp.exp(log_a))
-    scale = jnp.where(fresh, 1.0, jnp.sqrt(one_minus_exp(-2.0 * log_a)))
-    return carry, scale
+    carry = jnp.exp(log_a)
+    scale = jnp.where(fresh, 1.0, jnp.sqrt(one_minus_square(carry, -2.0 * log_a)))
+    return jnp.where(fresh, 0.0, carry), scale
 
 
 def forward_kernel(scalars_ref, *refs):
@@ -91,18 +91,24 @@
     features = first_ref.shape[1]
     pieces = count // LOAD
     arrivals = [
-        pltpu.make_async_copy(sources[1], branches_ref, in_sems.at[pieces]),
+        *[
+            pltpu.make_async_copy(
+                sources[1].at[pl.ds(k * width, width), :], branches_ref.at[pl.ds(k * width, width), :], in_sems.at[pieces + k]
+            )
+            for k in range(2)
+        ],
         *[
             pltpu.make_async_copy(sources[0].at[pl.ds(k * LOAD, LOAD), :], first_ref.at[pl.ds(k * LOAD, LOAD), :], in_sems.at[k])
             for k in range(pieces)
         ],
-        pltpu.make_async_copy(sources[2], block_ref, in_sems.at[pieces + 1]),
+        pltpu.make_async_copy(sources[2], block_ref, in_sems.at[pieces + 2]),
     ]
     for arrival in arrivals:
         arrival.start()
-    arrivals[0].wait()
+    for arrival in arrivals[:2]:
+        arrival.wait()
     for k in range(pieces):
-        arrivals[1 + k].wait()
+        arrivals[2 + k].wait()
         here = pl.ds(k * LOAD, LOAD)
         both_ref[here, :] = times_transposed(first_ref[here, :], branches_ref[...])
     departures = [pltpu.make_async_copy(both_ref, out_refs[6], out_sems.at[0])]
@@ -128,13 +134,8 @@
 
     lax.fori_loop(0, count // CHUNK, convolve, 0)
 
-    def open_gates(at, _):
-        here = pl.ds(pl.multiple_of(at * ROWS, ROWS), ROWS)
-        rate_ref[here, :] = jax.nn.sigmoid(times(conv_ref[here, :], rate_w_ref[...]) + rate_b)
-        inlet_ref[here, :] = jax.nn.sigmoid(times(conv_ref[here, :], inlet_w_ref[...]) + inlet_b)
-        return _
-
-    lax.fori_loop(0, count // ROWS, open_gates, 0)
+    rate_ref[...] = jax.nn.sigmoid(times(conv_ref[...], rate_w_ref[...]) + rate_b)
+    inlet_ref[...] = jax.nn.sigmoid(times(conv_ref[...], inlet_w_ref[...]) + inlet_b)
     for k, (ref, out_ref) in enumerate(((conv_ref, out_refs[2]), (rate_ref, out_refs[3]), (inlet_ref, out_refs[4]))):
         departures.append(pltpu.make_async_copy(ref, out_ref, out_sems.at[1 + k]))
         departures[-1].start()
@@ -333,13 +334,14 @@
     return strips, -(-rows // (strips * 2 * SUB)) * 2 * SUB
 
 
-def unpack_kernel(heads, strips, packed_ref, square_ref, taps_ref, *refs):
+def unpack_kernel(heads, strips, packed_ref, rate_ref, inlet_ref, taps_ref, *refs):
     line_refs, stacked_ref = refs[:-1], refs[-1]
-    depth, size = packed_ref.shape[0], square_ref.shape[-1]
+    depth, size = packed_ref.shape[0], rate_ref.shape[-1]
     for k in range(strips):
         stacked_ref[pl.ds(k * depth, depth), :] = packed_ref[:, k * size : (k + 1) * size]
-    for k in range(2 * heads):
-        square_ref[k] = stacked_ref[pl.ds(k * size, size), :]
+    for h in range(heads):
+        rate_ref[h] = stacked_ref[pl.ds(h * size, size), :]
+        inlet_ref[h] = stacked_ref[pl.ds((heads + h) * size, size), :]
     small = jnp.concatenate(
         [stacked_ref[pl.ds(2 * heads * size + h * SUB, SUB), :] for h in range(heads)], axis=1
     )
@@ -353,7 +355,8 @@
     return pl.pallas_call(
         lambda *refs: unpack_kernel(heads, strips, *refs),
         out_shape=[
-            jax.ShapeDtypeStruct((2 * heads, size, size), WIDE),
+            jax.ShapeDtypeStruct((heads, size, size), WIDE),
+            jax.ShapeDtypeStruct((heads, size, size), WIDE),
             jax.ShapeDtypeStruct((SUB - 4, heads * size), WIDE),
         ]
         + [jax.ShapeDtypeStruct((heads * size,), WIDE)] * 4,
@@ -401,7 +404,7 @@
         + [pltpu.VMEM(*one) for one in made]
         + [
             pltpu.VMEM((count + SUB, width), WIDE),
-            pltpu.SemaphoreType.DMA((count // LOAD + 2,)),
+            pltpu.SemaphoreType.DMA((count // LOAD + 3,)),
             pltpu.SemaphoreType.DMA((6 + features // TILE,)),
         ],
         compiler_params=pltpu.CompilerParams(vmem_limit_bytes=ROOM * 1024 * 1024),
@@ -693,7 +696,9 @@
         scratch_shapes=scratch
         + [pltpu.SemaphoreType.DMA((count,)), pltpu.SemaphoreType.DMA((count * len(splits),))],
         input_output_aliases={1 + count + k: k for k in range(len(onto))},
-        compiler_params=pltpu.CompilerParams(vmem_limit_bytes=rows * columns * 6 * count + 4 * 1024 * 1024),
+        compiler_params=pltpu.CompilerParams(
+            vmem_limit_bytes=ROOM * 1024 * 1024 if onto else rows * columns * 6 * count + 4 * 1024 * 1024
+        ),
         cost_estimate=NO_COST,
     )(jnp.stack(spots).astype(jnp.int32), *pieces, *onto)
 
@@ -744,10 +749,12 @@
     def land(self, got):
         self.step += 1
         if self.step < len(self.order):
-            pairs = [split_for(values, self.axis, self.order[self.step]) for values in (self.kept, got)]
-            self.send, self.kept = (
-                (left.astype(WIDE) + right.astype(WIDE)).astype(LOW) for left, right in zip(*pairs)
-            )
+            bit = self.order[self.step]
+            kept, sent = (split_for(values, self.axis, bit)[0] for values in (self.kept, got))
+            self.send = (kept.astype(WIDE) + sent.astype(WIDE)).astype(LOW)
+            kept, got, _ = lax.optimization_barrier((self.kept, got, self.send))
+            kept, got = (split_for(values, self.axis, bit)[1] for values in (kept, got))
+            self.kept = (kept.astype(WIDE) + got.astype(WIDE)).astype(LOW)
         else:
             self.pieces = {0: (self.kept.astype(WIDE) + got.astype(WIDE)).astype(LOW)}
 
@@ -864,21 +871,20 @@
     block_partial, onward[1], backward[1] = lax.optimization_barrier((block_partial, onward[1], backward[1]))
 
     block_sum = sum_rows(block_partial)
+    shards = {hop: piece for hop, piece in onward.items()} | {-hop: piece for hop, piece in backward.items()}
+    made = lax.optimization_barrier((block_sum, *[other_core(piece) for piece in shards.values()]))
+    block_sum = made[0]
+    others = dict(zip(shards, made[1:]))
+    own_second, own_middle = normed(tokens, second_gain, block_sum)
+    second_rows = all_rows(own_second)
+
+    onward[1], backward[1] = lax.optimization_barrier((onward[1], backward[1], own_second))[:2]
     for hop in range(2, chips // 2 + 1):
         onward[hop] = next_chip(onward[hop - 1], 1)
+        shards[hop], others[hop] = onward[hop], other_core(onward[hop])
         if 2 * hop < chips:
             backward[hop] = next_chip(backward[hop - 1], -1)
-    shards = {hop: piece for hop, piece in onward.items()} | {-hop: piece for hop, piece in backward.items()}
-    near_hops = [hop for hop in shards if abs(hop) < 2]
-    far_hops = [hop for hop in shards if abs(hop) >= 2]
-    made = lax.optimization_barrier(
-        (block_sum, *[shards[hop] for hop in far_hops], *[other_core(shards[hop]) for hop in near_hops])
-    )
-    block_sum = made[0]
-    shards |= dict(zip(far_hops, made[1:]))
-    others = dict(zip(near_hops, made[1 + len(far_hops) :])) | {hop: other_core(shards[hop]) for hop in far_hops}
-    own_second, own_middle = normed(tokens, second_gain, block_sum)
-    second_rows = all_rows(own_second)
+            shards[-hop], others[-hop] = backward[hop], other_core(backward[hop])
     me = lax.axis_index("mp")
     blocks, places = [], []
     for hop in shards:
@@ -967,8 +973,7 @@
         gains = gains + swap(gains, bit)
     rest = [mask for mask in late[0].pieces if mask not in own]
     branch_gate_grad, branch_input_grad, block_grad, packed = finish(late, 1, splits, rest, made[2:-1])
-    square, taps_grad, *lines = unpack_strips(packed, heads, width // heads)
-    square = square.reshape(2, heads, *square.shape[1:])
+    rate_w_grad, inlet_w_grad, taps_grad, *lines = unpack_strips(packed, heads, width // heads)
     return (
         output,
         input_grad,
@@ -977,9 +982,9 @@
         branch_input_grad.T,
         taps_grad,
         lines[0],
-        square[0],
+        rate_w_grad,
         lines[1],
-        square[1],
+        inlet_w_grad,
         lines[2],
         lines[3],
         block_grad,

time: 435 us -> 430 us (0.989)
  waiting for transfers between devices: 196 us -> 182 us
  other arithmetic: 44.9 us -> 52.2 us
  local copies, waits for them, and re-layouts: 21.5 us -> 26.5 us
    all_gather x3, waiting for transfers between devices: 50.8 us -> 39.1 us  [all_rows(): return lax.all_gather(values, 'mp', axis=0, tiled=True)]
    ppermute x32, waiting for transfers between devices: 81.6 us -> 71.1 us  [swap(): return lax.ppermute(values, 'dp', [(i, i ^ 1 << bit) for i in range(count)])]
    convert_element_type x6 -> x11, other arithmetic: 17 us -> 25.7 us  [the longest x6 13.4 us: land(): self.send = (kept.astype(WIDE) + sent.astype(WIDE)).astype(LOW)]
    reduce_scatter x4, waiting for transfers between devices: 44.8 us -> 51.6 us  [sum_rows(): lax.psum_scatter(values.astype(LOW), 'mp', scatter_dimension=0, tiled=True)]
    unnamed x90 -> x110, local copies, waits for them, and re-layouts: 10.4 us -> 16.3 us
  transfers between devices with their start and end apart: 46 -> 46, of which waited for: 18 -> 22; matrix products, arithmetic and copies ran while one was open for 14% -> 16% of each run, Pallas kernels for 20% -> 20%
where the time goes in v5:
time: 430 us; the launch traced here: 423 us
  waiting for transfers between devices  182 us (42%)
  Pallas kernels  92.1 us (21%)
  other arithmetic  52.2 us (12%)
  starting transfers between devices  35.9 us (8%)
  local copies, waits for them, and re-layouts  26.5 us (6%)
  matrix products  19.7 us (5%)
  between operations  15.1 us (4%)
    ppermute x32, waiting for transfers between devices, swap(): return lax.ppermute(values, 'dp', [(i, i ^ 1 << bit) for i in range(count)])  71.1 us
    reduce_scatter x4, waiting for transfers between devices, sum_rows(): lax.psum_scatter(values.astype(LOW), 'mp', scatter_dimension=0, tiled=True)  51.6 us
    all_gather x3, waiting for transfers between devices, all_rows(): return lax.all_gather(values, 'mp', axis=0, tiled=True)  39.1 us
    ppermute x32, starting transfers between devices, swap(): return lax.ppermute(values, 'dp', [(i, i ^ 1 << bit) for i in range(count)])  32.1 us
    pallas_call x1, Pallas kernels, backward_mix(): pl.pallas_call(lambda *refs: backward_kernel(heads, owners, *refs), in_sp...  24.1 us
    pallas_call x6, Pallas kernels, place(): pl.pallas_call(lambda *refs: place_kernel(count, axis, splits, len(onto),...  22.8 us
    pallas_call x5, Pallas kernels, call_blocks(): pl.pallas_call(body, grid_spec=pltpu.PrefetchScalarGridSpec(num_scalar_pr...  16.6 us
    unnamed x110, local copies, waits for them, and re-layouts  16.3 us
  transfers between devices with their start and end apart: 46, of which 22 were waited for; matrix products, arithmetic and copies ran while one was open for 16% of the time, Pallas kernels for 20%

profile of v5, /device:TPU:0, one launch (start us, length us, event | category | flops | bytes accessed | tf_op | source)
XLA Modules:
  0.0 423.0 jit_solution(17373194541299554146)
XLA Ops:
  7.3 2.2 shard_map.305
  19.6 3.7 pad_maximum_fusion.refs_1_.refs_10_
  23.3 28.0 %all-gather.4.cloned.1.call-done.refs_0_.refs_9_ = bf16[768,2048]{1,0:T(8,128)(2,1)} async-done(((bf16[96,2048]{1,0:T(8,128)(2,1)}), bf16[768,2048]{1,0:T(8,128)(2,1)}) %all-gather.4.cloned.1.call-update) | async-done | bytes 3145744 | tf_op jit(solution)/shard_map/all_gather | solution.py:653
  53.3 15.2 %shard_map.306 = (bf16[768,2048]{1,0:T(8,128)(2,1)}, bf16[768,320]{1,0:T(8,128)(2,1)}, bf16[768,320]{1,0:T(8,128)(2,1)}, f32[768,320]{1,0:T(8,128)}, f32[768,320...) custom-call(s32[1,7]{1,0:T(1,128)} %bitcast.67, bf16[768,2048]{1,0:T(8,128)(2,1)} %all-gather.4.cloned.1.call-done.refs_0_.refs_9_, ...), custom_call_target="tpu_custom_call" | custom-call | tf_op jit(solution)/shard_map/pallas_call | solution.py:398
  68.5 3.3 collective-permute-done.refs_3_
  76.0 35.7 %reduce-scatter.5.cloned.1.call-done.added_ref = bf16[96,2048]{1,0:T(8,128)(2,1)} async-done(((bf16[768,2048]{1,0:T(8,128)(2,1)}), bf16[96,2048]{1,0:T(8,128)(2,1)}) %reduce-scatter.5.cloned.1.call-update) | async-done | bytes 393232 | tf_op jit(solution)/shard_map/reduce_scatter | solution.py:649
  111.7 2.1 shard_map.307
  114.4 12.7 %collective-permute-done.5.refs_7_ = bf16[96,2048]{1,0:T(8,128)(2,1)} collective-permute-done((bf16[96,2048]{1,0:T(8,128)(2,1)}, bf16[96,2048]{1,0:T(8,128)(2,1)}, u32[]{:S(2)}, u32[]{:S(2)}) %collective-permute-start.5) | collective-permute-done | bytes 393248 | tf_op jit(solution)/shard_map/ppermute | solution.py:817
  127.2 2.0 collective-permute-done.6.refs_8_
  133.2 2.8 shard_map.308
  136.0 1.7 copy-done.2
  137.7 4.1 fusion.16
  141.8 11.2 %all-gather.6.cloned.1.call-done.refs_0_.left_ref = bf16[768,2048]{1,0:T(8,128)(2,1)} async-done(((bf16[96,2048]{1,0:T(8,128)(2,1)}), bf16[768,2048]{1,0:T(8,128)(2,1)}) %all-gather.6.cloned.1.call-update) | async-done | bytes 3145744 | tf_op jit(solution)/shard_map/all_gather | solution.py:653
  153.0 5.6 %fusion.17 = f32[768,768]{1,0:T(8,128)S(1)} fusion(bf16[768,2048]{1,0:T(8,128)(2,1)} %all-gather.6.cloned.1.call-done.refs_0_.left_ref, bf16[2048,768]{1,0:T(8,128)(2,1)} %refs_3_.3), kind=kOutput, calls=%fused_computation.67 | convolution fusion | flops 2415919104 | bytes 8650752 | tf_op jit(solution)/shard_map/dot_general | solution.py:27
  158.6 2.9 fusion.5
  161.5 2.9 convolution_convert_fusion
  164.5 1.5 broadcast_select_fusion
  166.0 1.5 collective-permute-start.8
  169.4 2.8 multiply_convert_fusion
  172.3 12.4 %shard_map.309 = (bf16[768,2048]{1,0:T(8,128)(2,1)}, bf16[1024,768]{1,0:T(8,128)(2,1)}, bf16[1024,768]{1,0:T(8,128)(2,1)}) custom-call(s32[2]{0:T(128)} %pad_add_fusion.spots_ref, bf16[768,2048]{1,0:T(8,128)(2,1)} %all-gather.6.cloned.1.call-done.refs_0_.left_ref, bf16[768,768]{1,0:T(8,128)(2,1)} %get-tuple-element.322.refs_1_.right_ref, ...), custom_call_target="tpu_custom_call" | custom-call | tf_op jit(solution)/shard_map/pallas_call | solution.py:546
  187.1 1.4 collective-permute-start.11
  189.7 2.5 add_convert_fusion.16
  192.6 2.1 add_convert_fusion.18
  194.6 1.5 collective-permute-start.9
  196.7 4.8 %shard_map.311 = bf16[1024,768]{1,0:T(8,128)(2,1)} custom-call(s32[2]{0:T(128)} %pad_add_fusion.2._, bf16[768,2048]{1,0:T(8,128)(2,1)} %all-gather.6.cloned.1.call-done.refs_0_.left_ref, bf16[768,768]{1,0:T(8,128)(2,1)} %get-tuple-element.321.refs_2_.right_ref), custom_call_target="tpu_custom_call" | custom-call | tf_op jit(solution)/shard_map/pallas_call | solution.py:449
  201.5 4.8 %shard_map.310 = bf16[1024,768]{1,0:T(8,128)(2,1)} custom-call(s32[2]{0:T(128)} %pad_add_fusion.1._, bf16[768,2048]{1,0:T(8,128)(2,1)} %all-gather.6.cloned.1.call-done.refs_0_.left_ref, bf16[768,768]{1,0:T(8,128)(2,1)} %get-tuple-element.322.refs_1_.right_ref), custom_call_target="tpu_custom_call" | custom-call | tf_op jit(solution)/shard_map/pallas_call | solution.py:449
  206.3 2.9 add_convert_fusion.15
  209.2 15.9 %reduce-scatter.7.cloned.1.call-done.grad_ref = bf16[96,2048]{1,0:T(8,128)(2,1)} async-done(((bf16[768,2048]{1,0:T(8,128)(2,1)}), bf16[96,2048]{1,0:T(8,128)(2,1)}) %reduce-scatter.7.cloned.1.call-update) | async-done | bytes 393232 | tf_op jit(solution)/shard_map/reduce_scatter | solution.py:649
  225.1 2.7 shard_map.312
  227.8 3.5 collective-permute-done.10
  235.4 2.0 add_convert_fusion.14.refs_1_
  238.7 2.7 add_convert_fusion.3
  242.2 2.7 add_convert_fusion.5
  246.3 4.2 fusion.18
  251.1 3.1 add_convert_fusion.4
  254.2 1.8 add_convert_fusion.2
  256.0 14.0 %collective-permute-done.15.refs_2_ = bf16[768,256]{1,0:T(8,128)(2,1)} collective-permute-done((bf16[768,256]{1,0:T(8,128)(2,1)}, bf16[768,256]{1,0:T(8,128)(2,1)}, u32[]{:S(2)}, u32[]{:S(2)}) %collective-permute-start.15) | collective-permute-done | bytes 393248 | tf_op jit(solution)/shard_map/ppermute | solution.py:712
  270.1 1.4 add_convert_fusion.refs_1_
  277.0 24.1 %shard_map.313 = (bf16[896,2048]{1,0:T(8,128)(2,1)}, bf16[1024,512]{1,0:T(8,128)(2,1)}, bf16[1024,512]{1,0:T(8,128)(2,1)}, bf16[1024,512]{1,0:T(8,128)(2,1)}, bf16[1024,512]{1,0:T(8,128)(2,1)}) custom-call(s32[1,7]{1,0:T(1,128)} %bitcast.68, bf16[768,2048]{1,0:T(8,128)(2,1)} %all-gather.8.cloned.1.call-done.refs_1_, bf16[320,2048]{1,0:T(8,128)(2,1)} %refs_2_.3, ...), custom_call_target="tpu_custom_call" | custom-call | tf_op jit(solution)/shard_map/pallas_call | solution.py:424
  301.2 6.0 %collective-permute-done.24.refs_3_ = bf16[512,768]{1,0:T(8,128)(2,1)} collective-permute-done((bf16[512,768]{1,0:T(8,128)(2,1)S(1)}, bf16[512,768]{1,0:T(8,128)(2,1)}, u32[]{:S(2)}, u32[]{:S(2)}) %collective-permute-start.24) | collective-permute-done | bytes 786464 | tf_op jit(solution)/shard_map/ppermute | solution.py:712
  308.0 1.5 collective-permute-start.19
  313.3 1.5 collective-permute-start.30
  314.7 1.5 collective-permute-start.27
  316.2 18.2 %collective-permute-done.19 = bf16[1024,512]{1,0:T(8,128)(2,1)} collective-permute-done((bf16[1024,512]{1,0:T(8,128)(2,1)}, bf16[1024,512]{1,0:T(8,128)(2,1)}, u32[]{:S(2)}, u32[]{:S(2)}) %collective-permute-start.19) | collective-permute-done | bytes 1048608 | tf_op jit(solution)/shard_map/ppermute | solution.py:712
  335.9 1.9 add_convert_fusion.11
  338.5 1.5 add_convert_fusion.9
  339.9 2.9 collective-permute-done.29.refs_4_
  342.8 1.5 collective-permute-start.22
  344.3 2.3 add_convert_fusion.10
  346.5 2.3 add_convert_fusion.8
  349.6 10.1 %collective-permute-done.27.refs_4_ = bf16[512,768]{1,0:T(8,128)(2,1)S(1)} collective-permute-done((bf16[512,768]{1,0:T(8,128)(2,1)}, bf16[512,768]{1,0:T(8,128)(2,1)S(1)}, u32[]{:S(2)}, u32[]{:S(2)}) %collective-permute-start.27) | collective-permute-done | bytes 786464 | tf_op jit(solution)/shard_map/ppermute | solution.py:712
  362.0 5.4 %collective-permute-done.22 = bf16[1024,256]{1,0:T(8,128)(2,1)} collective-permute-done((bf16[1024,256]{1,0:T(8,128)(2,1)S(1)}, bf16[1024,256]{1,0:T(8,128)(2,1)}, u32[]{:S(2)}, u32[]{:S(2)}) %collective-permute-start.22) | collective-permute-done | bytes 524320 | tf_op jit(solution)/shard_map/ppermute | solution.py:712
  368.7 1.4 add_convert_fusion.6.refs_4_
  372.5 1.7 collective-permute-start.32
  374.2 1.4 collective-permute-start.31
  375.7 1.4 fusion.8
  378.9 4.4 %shard_map.314 = f32[2048,768]{1,0:T(8,128)} custom-call(s32[4]{0:T(128)S(1)} %pad_add_fusion.3.refs_0_, bf16[512,768]{1,0:T(8,128)(2,1)S(1)} %add_convert_fusion.1.refs_1_, bf16[512,768]{1,0:T(8,128)(2,1)} %collective-permute-done.23.refs_2_, bf16[512,768]{1,0:T(8,128)(2,1)} %collective-permute-done.24.refs_3_, bf16[512,768]{1,0:T(8,128)(2,1)S(1)} %copy-done.14), custom_call_target="tpu_custom_call" | custom-call | tf_op jit(solution)/shard_map/pallas_call | solution.py:691
  383.3 4.4 %shard_map.315 = f32[768,2048]{1,0:T(8,128)} custom-call(s32[8]{0:T(128)S(1)} %stack.186.refs_0_, bf16[768,256]{1,0:T(8,128)(2,1)} %add_convert_fusion.14.refs_1_, bf16[768,256]{1,0:T(8,128)(2,1)} %collective-permute-done.15.refs_2_, bf16[768,256]{1,0:T(8,128)(2,1)} %collective-permute-done.16.refs_3_, bf16[768,256]{1,0:T(8,128)(2,1)S(1)} %copy-done.20, ...), custom_call_target="tpu_custom_call" | custom-call | tf_op jit(solution)/shard_map/pallas_call | solution.py:691
  387.7 4.8 %collective-permute-done.35 = f32[2,2048]{1,0:T(2,128)S(1)} collective-permute-done((f32[2,2048]{1,0:T(2,128)S(1)}, f32[2,2048]{1,0:T(2,128)S(1)}, u32[]{:S(2)}, u32[]{:S(2)}) %collective-permute-start.35) | collective-permute-done | bytes 16416 | tf_op jit(solution)/shard_map/ppermute | solution.py:712
  394.5 1.5 collective-permute-start.37
  396.7 2.1 add_convert_fusion.12
  401.0 3.6 shard_map.316
  404.7 4.1 shard_map.317
  410.3 3.4 shard_map.318
  (224 shorter events, 65.0 us)
Async XLA Ops:
  7.2 130.5 %copy-start = (bf16[768,2048]{1,0:T(8,128)(2,1)S(1)}, bf16[768,2048]{1,0:T(8,128)(2,1)}, u32[]{:S(2)}) copy-start(bf16[768,2048]{1,0:T(8,128)(2,1)} %param.42) | copy-start | bytes 9437188
  7.2 44.1 %all-gather.4.cloned.1.call-start = ((), (), s32[]{:S(2)}) async-start(), calls=%async_computation.4 | async-start | bytes 3538944 | tf_op jit(solution)/shard_map/all_gather | solution.py:653
  9.5 8.9 %copy-start.52 = (s32[1,3]{1,0:T(1,128)S(1)}, s32[1,3]{1,0:T(1,128)}, u32[]{:S(2)}) copy-start(s32[1,3]{1,0:T(1,128)} %param.27) | copy-start | bytes 40
  9.5 102.2 %reduce-scatter.5.cloned.1.call-start = ((), (), s32[]{:S(2)}) async-start(), calls=%async_computation.5 | async-start | bytes 3538944 | tf_op jit(solution)/shard_map/reduce_scatter | solution.py:649
  19.6 31.6 %copy-start.6 = (bf16[96,2048]{1,0:T(8,128)(2,1)S(1)}, bf16[96,2048]{1,0:T(8,128)(2,1)}, u32[]{:S(2)}) copy-start(bf16[96,2048]{1,0:T(8,128)(2,1)} %added_ref.3) | copy-start | bytes 1179652
  51.3 17.2 %collective-permute-start.1 = (bf16[96,2048]{1,0:T(8,128)(2,1)S(1)}, bf16[96,2048]{1,0:T(8,128)(2,1)S(1)}, u32[]{:S(2)}, u32[]{:S(2)}) collective-permute-start(bf16[96,2048]{1,0:T(8,128)(2,1)S(1)} %copy-done.6), channel_id=1, source_target_pairs={{0,6},{1,7},{2,0},{3,1},{4,2},{5,3},{6,4},{7,5},{8,14},{9,15},{10,... | collective-permute-start | bytes 1179656 | tf_op jit(solution)/shard_map/ppermute | solution.py:817
  52.6 19.2 %collective-permute-start = (bf16[96,2048]{1,0:T(8,128)(2,1)S(1)}, bf16[96,2048]{1,0:T(8,128)(2,1)}, u32[]{:S(2)}, u32[]{:S(2)}) collective-permute-start(bf16[96,2048]{1,0:T(8,128)(2,1)S(1)} %copy-done.6), channel_id=1, source_target_pairs={{0,2},{1,3},{2,4},{3,5},{4,6},{5,7},{6,0},{7,1},{8,10},{9,11},{10,... | collective-permute-start | bytes 1179656 | tf_op jit(solution)/shard_map/ppermute | solution.py:817
  71.9 81.1 %all-gather.6.cloned.1.call-start = ((), (), s32[]{:S(2)}) async-start(), calls=%async_computation.6 | async-start | bytes 3538944 | tf_op jit(solution)/shard_map/all_gather | solution.py:653
  71.9 1.8 collective-permute-start.2
  72.0 2.5 collective-permute-start.3
  72.5 2.7 collective-permute-start.4
  113.8 111.3 %reduce-scatter.7.cloned.1.call-start = ((), (), s32[]{:S(2)}) async-start(), calls=%async_computation.7 | async-start | bytes 3538944 | tf_op jit(solution)/shard_map/reduce_scatter | solution.py:649
  113.9 13.3 %collective-permute-start.5 = (bf16[96,2048]{1,0:T(8,128)(2,1)}, bf16[96,2048]{1,0:T(8,128)(2,1)}, u32[]{:S(2)}, u32[]{:S(2)}) collective-permute-start(bf16[96,2048]{1,0:T(8,128)(2,1)} %collective-permute-done.refs_3_), channel_id=1, source_target_pairs={{0,2},{1,3},{2,4},{3,5},{4,6},{5,7},{6,0},{7,1},{8,10},{9,11},{10,... | collective-permute-start | bytes 1179656 | tf_op jit(solution)/shard_map/ppermute | solution.py:817
  127.2 2.1 collective-permute-start.6
  166.0 20.0 %collective-permute-start.8 = (bf16[768,512]{1,0:T(8,128)(2,1)}, bf16[768,512]{1,0:T(8,128)(2,1)}, u32[]{:S(2)}, u32[]{:S(2)}) collective-permute-start(bf16[768,512]{1,0:T(8,128)(2,1)} %get-tuple-element.323), channel_id=1, source_target_pairs={{0,16},{8,24},{16,0},{24,8},{1,17},{9,25},{17,1},{25,9},{2,18},{10... | collective-permute-start | bytes 2359304 | tf_op jit(solution)/shard_map/ppermute | solution.py:712
  167.5 19.5 %collective-permute-start.7 = (bf16[768,512]{1,0:T(8,128)(2,1)S(1)}, bf16[768,512]{1,0:T(8,128)(2,1)}, u32[]{:S(2)}, u32[]{:S(2)}) collective-permute-start(bf16[768,512]{1,0:T(8,128)(2,1)S(1)} %get-tuple-element.325), channel_id=1, source_target_pairs={{0,8},{8,0},{16,24},{24,16},{1,9},{9,1},{17,25},{25,17},{2,10},{10... | collective-permute-start | bytes 2359304 | tf_op jit(solution)/shard_map/ppermute | solution.py:712
  187.0 83.0 %all-gather.8.cloned.1.call-start = ((), (), s32[]{:S(2)}) async-start(), calls=%async_computation.8 | async-start | bytes 3538944 | tf_op jit(solution)/shard_map/all_gather | solution.py:653
  187.1 45.3 %collective-permute-start.11 = (bf16[1024,768]{1,0:T(8,128)(2,1)}, bf16[1024,768]{1,0:T(8,128)(2,1)}, u32[]{:S(2)}, u32[]{:S(2)}) collective-permute-start(bf16[1024,768]{1,0:T(8,128)(2,1)} %get-tuple-element.224), channel_id=1, source_target_pairs={{0,8},{8,0},{16,24},{24,16},{1,9},{9,1},{17,25},{25,17},{2,10},{10... | collective-permute-start | bytes 4718600 | tf_op jit(solution)/shard_map/ppermute | solution.py:712
  188.5 43.9 %collective-permute-start.12 = (bf16[1024,768]{1,0:T(8,128)(2,1)}, bf16[1024,768]{1,0:T(8,128)(2,1)}, u32[]{:S(2)}, u32[]{:S(2)}) collective-permute-start(bf16[1024,768]{1,0:T(8,128)(2,1)} %get-tuple-element.225), channel_id=1, source_target_pairs={{0,16},{8,24},{16,0},{24,8},{1,17},{9,25},{17,1},{25,9},{2,18},{10... | collective-permute-start | bytes 4718600 | tf_op jit(solution)/shard_map/ppermute | solution.py:712
  192.3 39.0 %collective-permute-start.10 = (bf16[768,256]{1,0:T(8,128)(2,1)}, bf16[768,256]{1,0:T(8,128)(2,1)}, u32[]{:S(2)}, u32[]{:S(2)}) collective-permute-start(bf16[768,256]{1,0:T(8,128)(2,1)} %add_convert_fusion.16), channel_id=1, source_target_pairs={{0,8},{8,0},{16,24},{24,16},{1,9},{9,1},{17,25},{25,17},{2,10},{10... | collective-permute-start | bytes 1179656 | tf_op jit(solution)/shard_map/ppermute | solution.py:712
  194.6 37.7 %collective-permute-start.9 = (bf16[768,256]{1,0:T(8,128)(2,1)}, bf16[768,256]{1,0:T(8,128)(2,1)}, u32[]{:S(2)}, u32[]{:S(2)}) collective-permute-start(bf16[768,256]{1,0:T(8,128)(2,1)} %add_convert_fusion.18), channel_id=1, source_target_pairs={{0,16},{8,24},{16,0},{24,8},{1,17},{9,25},{17,1},{25,9},{2,18},{10... | collective-permute-start | bytes 1179656 | tf_op jit(solution)/shard_map/ppermute | solution.py:712
  232.4 136.3 %reduce-scatter.9.cloned.1.call-start = ((), (), s32[]{:S(2)}) async-start(), calls=%async_computation.9 | async-start | bytes 4128768 | tf_op jit(solution)/shard_map/reduce_scatter | solution.py:649
  232.4 6.2 %copy-start.33 = (bf16[1024,768]{1,0:T(8,128)(2,1)S(1)}, bf16[1024,768]{1,0:T(8,128)(2,1)}, u32[]{:S(2)}) copy-start(bf16[1024,768]{1,0:T(8,128)(2,1)} %shard_map.311) | copy-start | bytes 4718596
  233.8 8.4 %copy-start.35 = (bf16[1024,768]{1,0:T(8,128)(2,1)S(1)}, bf16[1024,768]{1,0:T(8,128)(2,1)}, u32[]{:S(2)}) copy-start(bf16[1024,768]{1,0:T(8,128)(2,1)} %shard_map.310) | copy-start | bytes 4718596
  233.8 16.6 %collective-permute-start.18 = (bf16[768,256]{1,0:T(8,128)(2,1)S(1)}, bf16[768,256]{1,0:T(8,128)(2,1)}, u32[]{:S(2)}, u32[]{:S(2)}) collective-permute-start(bf16[768,256]{1,0:T(8,128)(2,1)S(1)} %add_convert_fusion.13.refs_5_), channel_id=1, source_target_pairs={{0,16},{8,24},{16,0},{24,8},{1,17},{9,25},{17,1},{25,9},{2,18},{10... | collective-permute-start | bytes 1179656 | tf_op jit(solution)/shard_map/ppermute | solution.py:712
  234.7 21.3 %collective-permute-start.17 = (bf16[768,256]{1,0:T(8,128)(2,1)S(1)}, bf16[768,256]{1,0:T(8,128)(2,1)}, u32[]{:S(2)}, u32[]{:S(2)}) collective-permute-start(bf16[768,256]{1,0:T(8,128)(2,1)S(1)} %add_convert_fusion.13.refs_5_), channel_id=1, source_target_pairs={{0,8},{8,0},{16,24},{24,16},{1,9},{9,1},{17,25},{25,17},{2,10},{10... | collective-permute-start | bytes 1179656 | tf_op jit(solution)/shard_map/ppermute | solution.py:712
  237.3 18.7 %collective-permute-start.16 = (bf16[768,256]{1,0:T(8,128)(2,1)}, bf16[768,256]{1,0:T(8,128)(2,1)}, u32[]{:S(2)}, u32[]{:S(2)}) collective-permute-start(bf16[768,256]{1,0:T(8,128)(2,1)} %add_convert_fusion.14.refs_1_), channel_id=1, source_target_pairs={{0,8},{8,0},{16,24},{24,16},{1,9},{9,1},{17,25},{25,17},{2,10},{10... | collective-permute-start | bytes 1179656 | tf_op jit(solution)/shard_map/ppermute | solution.py:712
  241.4 28.7 %collective-permute-start.14 = (bf16[512,768]{1,0:T(8,128)(2,1)}, bf16[512,768]{1,0:T(8,128)(2,1)}, u32[]{:S(2)}, u32[]{:S(2)}) collective-permute-start(bf16[512,768]{1,0:T(8,128)(2,1)} %add_convert_fusion.3), channel_id=1, source_target_pairs={{0,8},{8,0},{16,24},{24,16},{1,9},{9,1},{17,25},{25,17},{2,10},{10... | collective-permute-start | bytes 2359304 | tf_op jit(solution)/shard_map/ppermute | solution.py:712
  244.9 25.2 %collective-permute-start.13 = (bf16[512,768]{1,0:T(8,128)(2,1)}, bf16[512,768]{1,0:T(8,128)(2,1)}, u32[]{:S(2)}, u32[]{:S(2)}) collective-permute-start(bf16[512,768]{1,0:T(8,128)(2,1)} %add_convert_fusion.5), channel_id=1, source_target_pairs={{0,16},{8,24},{16,0},{24,8},{1,17},{9,25},{17,1},{25,9},{2,18},{10... | collective-permute-start | bytes 2359304 | tf_op jit(solution)/shard_map/ppermute | solution.py:712
  250.4 19.6 %collective-permute-start.15 = (bf16[768,256]{1,0:T(8,128)(2,1)}, bf16[768,256]{1,0:T(8,128)(2,1)}, u32[]{:S(2)}, u32[]{:S(2)}) collective-permute-start(bf16[768,256]{1,0:T(8,128)(2,1)} %add_convert_fusion.14.refs_1_), channel_id=1, source_target_pairs={{0,16},{8,24},{16,0},{24,8},{1,17},{9,25},{17,1},{25,9},{2,18},{10... | collective-permute-start | bytes 1179656 | tf_op jit(solution)/shard_map/ppermute | solution.py:712
  271.5 29.6 %collective-permute-start.26 = (bf16[512,768]{1,0:T(8,128)(2,1)S(1)}, bf16[512,768]{1,0:T(8,128)(2,1)S(1)}, u32[]{:S(2)}, u32[]{:S(2)}) collective-permute-start(bf16[512,768]{1,0:T(8,128)(2,1)S(1)} %add_convert_fusion.refs_1_), channel_id=1, source_target_pairs={{0,16},{8,24},{16,0},{24,8},{1,17},{9,25},{17,1},{25,9},{2,18},{10... | collective-permute-start | bytes 2359304 | tf_op jit(solution)/shard_map/ppermute | solution.py:712
  272.5 28.7 %collective-permute-start.25 = (bf16[512,768]{1,0:T(8,128)(2,1)S(1)}, bf16[512,768]{1,0:T(8,128)(2,1)S(1)}, u32[]{:S(2)}, u32[]{:S(2)}) collective-permute-start(bf16[512,768]{1,0:T(8,128)(2,1)S(1)} %add_convert_fusion.refs_1_), channel_id=1, source_target_pairs={{0,8},{8,0},{16,24},{24,16},{1,9},{9,1},{17,25},{25,17},{2,10},{10... | collective-permute-start | bytes 2359304 | tf_op jit(solution)/shard_map/ppermute | solution.py:712
  275.1 32.0 %collective-permute-start.24 = (bf16[512,768]{1,0:T(8,128)(2,1)S(1)}, bf16[512,768]{1,0:T(8,128)(2,1)}, u32[]{:S(2)}, u32[]{:S(2)}) collective-permute-start(bf16[512,768]{1,0:T(8,128)(2,1)S(1)} %add_convert_fusion.1.refs_1_), channel_id=1, source_target_pairs={{0,8},{8,0},{16,24},{24,16},{1,9},{9,1},{17,25},{25,17},{2,10},{10... | collective-permute-start | bytes 2359304 | tf_op jit(solution)/shard_map/ppermute | solution.py:712
  275.9 31.3 %collective-permute-start.23 = (bf16[512,768]{1,0:T(8,128)(2,1)S(1)}, bf16[512,768]{1,0:T(8,128)(2,1)}, u32[]{:S(2)}, u32[]{:S(2)}) collective-permute-start(bf16[512,768]{1,0:T(8,128)(2,1)S(1)} %add_convert_fusion.1.refs_1_), channel_id=1, source_target_pairs={{0,16},{8,24},{16,0},{24,8},{1,17},{9,25},{17,1},{25,9},{2,18},{10... | collective-permute-start | bytes 2359304 | tf_op jit(solution)/shard_map/ppermute | solution.py:712
  301.1 6.8 %copy-start.7 = (bf16[512,768]{1,0:T(8,128)(2,1)}, bf16[512,768]{1,0:T(8,128)(2,1)S(1)}, u32[]{:S(2)}) copy-start(bf16[512,768]{1,0:T(8,128)(2,1)S(1)} %collective-permute-done.26.refs_3_) | copy-start | bytes 2359300
  301.2 33.3 %copy-start.9 = (bf16[512,768]{1,0:T(8,128)(2,1)}, bf16[512,768]{1,0:T(8,128)(2,1)S(1)}, u32[]{:S(2)}) copy-start(bf16[512,768]{1,0:T(8,128)(2,1)S(1)} %collective-permute-done.25.refs_2_) | copy-start | bytes 2359300
  307.2 89.4 %reduce-scatter.11.cloned.1.call-start = ((), (), s32[]{:S(2)}) async-start(), calls=%async_computation.10 | async-start | bytes 3538944 | tf_op jit(solution)/shard_map/reduce_scatter | solution.py:649
  308.0 26.5 %collective-permute-start.19 = (bf16[1024,512]{1,0:T(8,128)(2,1)}, bf16[1024,512]{1,0:T(8,128)(2,1)}, u32[]{:S(2)}, u32[]{:S(2)}) collective-permute-start(bf16[1024,512]{1,0:T(8,128)(2,1)} %get-tuple-element.254), channel_id=1, source_target_pairs={{0,8},{8,0},{16,24},{24,16},{1,9},{9,1},{17,25},{25,17},{2,10},{10... | collective-permute-start | bytes 3145736 | tf_op jit(solution)/shard_map/ppermute | solution.py:712
  309.5 26.4 %collective-permute-start.20 = (bf16[1024,512]{1,0:T(8,128)(2,1)}, bf16[1024,512]{1,0:T(8,128)(2,1)}, u32[]{:S(2)}, u32[]{:S(2)}) collective-permute-start(bf16[1024,512]{1,0:T(8,128)(2,1)} %get-tuple-element.255), channel_id=1, source_target_pairs={{0,16},{8,24},{16,0},{24,8},{1,17},{9,25},{17,1},{25,9},{2,18},{10... | collective-permute-start | bytes 3145736 | tf_op jit(solution)/shard_map/ppermute | solution.py:712
  310.2 28.2 %copy-start.37 = (bf16[1024,512]{1,0:T(8,128)(2,1)S(1)}, bf16[1024,512]{1,0:T(8,128)(2,1)}, u32[]{:S(2)}) copy-start(bf16[1024,512]{1,0:T(8,128)(2,1)} %get-tuple-element.262) | copy-start | bytes 3145732
  312.7 30.1 %collective-permute-start.29 = (bf16[768,256]{1,0:T(8,128)(2,1)}, bf16[768,256]{1,0:T(8,128)(2,1)S(1)}, u32[]{:S(2)}, u32[]{:S(2)}) collective-permute-start(bf16[768,256]{1,0:T(8,128)(2,1)} %collective-permute-done.15.refs_2_), channel_id=1, source_target_pairs={{0,8},{8,0},{16,24},{24,16},{1,9},{9,1},{17,25},{25,17},{2,10},{10... | collective-permute-start | bytes 1179656 | tf_op jit(solution)/shard_map/ppermute | solution.py:712
  313.3 35.5 %collective-permute-start.30 = (bf16[768,256]{1,0:T(8,128)(2,1)}, bf16[768,256]{1,0:T(8,128)(2,1)S(1)}, u32[]{:S(2)}, u32[]{:S(2)}) collective-permute-start(bf16[768,256]{1,0:T(8,128)(2,1)} %collective-permute-done.17.refs_6_), channel_id=1, source_target_pairs={{0,16},{8,24},{16,0},{24,8},{1,17},{9,25},{17,1},{25,9},{2,18},{10... | collective-permute-start | bytes 1179656 | tf_op jit(solution)/shard_map/ppermute | solution.py:712
  314.7 44.9 %collective-permute-start.27 = (bf16[512,768]{1,0:T(8,128)(2,1)}, bf16[512,768]{1,0:T(8,128)(2,1)S(1)}, u32[]{:S(2)}, u32[]{:S(2)}) collective-permute-start(bf16[512,768]{1,0:T(8,128)(2,1)} %collective-permute-done.23.refs_2_), channel_id=1, source_target_pairs={{0,8},{8,0},{16,24},{24,16},{1,9},{9,1},{17,25},{25,17},{2,10},{10... | collective-permute-start | bytes 2359304 | tf_op jit(solution)/shard_map/ppermute | solution.py:712
  334.5 26.6 %collective-permute-start.28 = (bf16[512,768]{1,0:T(8,128)(2,1)S(1)}, bf16[512,768]{1,0:T(8,128)(2,1)S(1)}, u32[]{:S(2)}, u32[]{:S(2)}) collective-permute-start(bf16[512,768]{1,0:T(8,128)(2,1)S(1)} %collective-permute-done.25.refs_2_), channel_id=1, source_target_pairs={{0,16},{8,24},{16,0},{24,8},{1,17},{9,25},{17,1},{25,9},{2,18},{10... | collective-permute-start | bytes 2359304 | tf_op jit(solution)/shard_map/ppermute | solution.py:712
  335.9 8.3 %copy-start.38 = (bf16[1024,512]{1,0:T(8,128)(2,1)S(1)}, bf16[1024,512]{1,0:T(8,128)(2,1)}, u32[]{:S(2)}) copy-start(bf16[1024,512]{1,0:T(8,128)(2,1)} %get-tuple-element.258) | copy-start | bytes 3145732
  337.8 30.8 %collective-permute-start.21 = (bf16[1024,256]{1,0:T(8,128)(2,1)S(1)}, bf16[1024,256]{1,0:T(8,128)(2,1)}, u32[]{:S(2)}, u32[]{:S(2)}) collective-permute-start(bf16[1024,256]{1,0:T(8,128)(2,1)S(1)} %add_convert_fusion.11), channel_id=1, source_target_pairs={{0,16},{8,24},{16,0},{24,8},{1,17},{9,25},{17,1},{25,9},{2,18},{10... | collective-permute-start | bytes 1572872 | tf_op jit(solution)/shard_map/ppermute | solution.py:712
  342.8 6.0 %copy-start.19 = (bf16[768,256]{1,0:T(8,128)(2,1)}, bf16[768,256]{1,0:T(8,128)(2,1)S(1)}, u32[]{:S(2)}) copy-start(bf16[768,256]{1,0:T(8,128)(2,1)S(1)} %collective-permute-done.29.refs_4_) | copy-start | bytes 1179652
  342.8 24.6 %collective-permute-start.22 = (bf16[1024,256]{1,0:T(8,128)(2,1)S(1)}, bf16[1024,256]{1,0:T(8,128)(2,1)}, u32[]{:S(2)}, u32[]{:S(2)}) collective-permute-start(bf16[1024,256]{1,0:T(8,128)(2,1)S(1)} %add_convert_fusion.9), channel_id=1, source_target_pairs={{0,8},{8,0},{16,24},{24,16},{1,9},{9,1},{17,25},{25,17},{2,10},{10... | collective-permute-start | bytes 1572872 | tf_op jit(solution)/shard_map/ppermute | solution.py:712
  368.6 7.0 %copy-start.43 = (bf16[112,2048]{1,0:T(8,128)(2,1)S(1)}, bf16[112,2048]{1,0:T(8,128)(2,1)}, u32[]{:S(2)}) copy-start(bf16[112,2048]{1,0:T(8,128)(2,1)} %reduce-scatter.9.cloned.1.call-done) | copy-start | bytes 1376260
  370.0 7.7 %copy-start.32 = (bf16[96,2048]{1,0:T(8,128)(2,1)S(1)}, bf16[96,2048]{1,0:T(8,128)(2,1)}, u32[]{:S(2)}) copy-start(bf16[96,2048]{1,0:T(8,128)(2,1)} %start_ref.3) | copy-start | bytes 1179652
  370.1 7.7 %copy-start.42 = (f32[96,2048]{1,0:T(8,128)S(1)}, f32[96,2048]{1,0:T(8,128)}, u32[]{:S(2)}) copy-start(f32[96,2048]{1,0:T(8,128)} %get-tuple-element.284) | copy-start | bytes 2359300
  370.1 7.6 %copy-start.44 = (f32[2048]{0:T(1024)S(1)}, f32[2048]{0:T(1024)}, u32[]{:S(2)}) copy-start(f32[2048]{0:T(1024)} %param.28) | copy-start | bytes 24580
  370.1 7.6 %copy-start.51 = (f32[96]{0:T(128)S(1)}, f32[96]{0:T(128)}, u32[]{:S(2)}) copy-start(f32[96]{0:T(128)} %add_rsqrt_fusion) | copy-start | bytes 1156
  370.1 22.4 %collective-permute-start.34 = (bf16[1024,256]{1,0:T(8,128)(2,1)S(1)}, bf16[1024,256]{1,0:T(8,128)(2,1)S(1)}, u32[]{:S(2)}, u32[]{:S(2)}) collective-permute-start(bf16[1024,256]{1,0:T(8,128)(2,1)S(1)} %add_convert_fusion.6.refs_4_), channel_id=1, source_target_pairs={{0,16},{8,24},{16,0},{24,8},{1,17},{9,25},{17,1},{25,9},{2,18},{10... | collective-permute-start | bytes 1572872 | tf_op jit(solution)/shard_map/ppermute | solution.py:712
  370.7 22.6 %collective-permute-start.33 = (bf16[1024,256]{1,0:T(8,128)(2,1)S(1)}, bf16[1024,256]{1,0:T(8,128)(2,1)S(1)}, u32[]{:S(2)}, u32[]{:S(2)}) collective-permute-start(bf16[1024,256]{1,0:T(8,128)(2,1)S(1)} %add_convert_fusion.6.refs_4_), channel_id=1, source_target_pairs={{0,8},{8,0},{16,24},{24,16},{1,9},{9,1},{17,25},{25,17},{2,10},{10... | collective-permute-start | bytes 1572872 | tf_op jit(solution)/shard_map/ppermute | solution.py:712
  372.5 20.8 %collective-permute-start.32 = (bf16[1024,256]{1,0:T(8,128)(2,1)S(1)}, bf16[1024,256]{1,0:T(8,128)(2,1)S(1)}, u32[]{:S(2)}, u32[]{:S(2)}) collective-permute-start(bf16[1024,256]{1,0:T(8,128)(2,1)S(1)} %add_convert_fusion.7.refs_1_), channel_id=1, source_target_pairs={{0,8},{8,0},{16,24},{24,16},{1,9},{9,1},{17,25},{25,17},{2,10},{10... | collective-permute-start | bytes 1572872 | tf_op jit(solution)/shard_map/ppermute | solution.py:712
  374.2 19.9 %collective-permute-start.31 = (bf16[1024,256]{1,0:T(8,128)(2,1)S(1)}, bf16[1024,256]{1,0:T(8,128)(2,1)}, u32[]{:S(2)}, u32[]{:S(2)}) collective-permute-start(bf16[1024,256]{1,0:T(8,128)(2,1)S(1)} %add_convert_fusion.7.refs_1_), channel_id=1, source_target_pairs={{0,16},{8,24},{16,0},{24,8},{1,17},{9,25},{17,1},{25,9},{2,18},{10... | collective-permute-start | bytes 1572872 | tf_op jit(solution)/shard_map/ppermute | solution.py:712
  377.1 18.9 %copy-start.45 = (f32[1,2048]{1,0:T(1,128)}, f32[1,2048]{1,0:T(1,128)S(1)}, u32[]{:S(2)}) copy-start(f32[1,2048]{1,0:T(1,128)S(1)} %get-tuple-element.327) | copy-start | bytes 24580
  377.2 18.8 %copy-start.47 = (f32[1,2048]{1,0:T(1,128)}, f32[1,2048]{1,0:T(1,128)S(1)}, u32[]{:S(2)}) copy-start(f32[1,2048]{1,0:T(1,128)S(1)} %get-tuple-element.328) | copy-start | bytes 24580
  377.2 15.3 %collective-permute-start.35 = (f32[2,2048]{1,0:T(2,128)S(1)}, f32[2,2048]{1,0:T(2,128)S(1)}, u32[]{:S(2)}, u32[]{:S(2)}) collective-permute-start(f32[2,2048]{1,0:T(2,128)S(1)} %pad_maximum_fusion.1), channel_id=1, source_target_pairs={{0,8},{8,0},{16,24},{24,16},{1,9},{9,1},{17,25},{25,17},{2,10},{10... | collective-permute-start | bytes 49160 | tf_op jit(solution)/shard_map/ppermute | solution.py:712
  383.3 15.4 %copy-start.8 = (bf16[512,768]{1,0:T(8,128)(2,1)S(1)}, bf16[512,768]{1,0:T(8,128)(2,1)}, u32[]{:S(2)}) copy-start(bf16[512,768]{1,0:T(8,128)(2,1)} %copy-done.7) | copy-start | bytes 2359300
  394.1 15.5 %collective-permute-start.36 = (bf16[1024,256]{1,0:T(8,128)(2,1)}, bf16[1024,256]{1,0:T(8,128)(2,1)}, u32[]{:S(2)}, u32[]{:S(2)}) collective-permute-start(bf16[1024,256]{1,0:T(8,128)(2,1)} %collective-permute-done.31.refs_2_), channel_id=1, source_target_pairs={{0,8},{8,0},{16,24},{24,16},{1,9},{9,1},{17,25},{25,17},{2,10},{10... | collective-permute-start | bytes 1572872 | tf_op jit(solution)/shard_map/ppermute | solution.py:712
  394.5 15.1 %collective-permute-start.37 = (bf16[1024,256]{1,0:T(8,128)(2,1)S(1)}, bf16[1024,256]{1,0:T(8,128)(2,1)}, u32[]{:S(2)}, u32[]{:S(2)}) collective-permute-start(bf16[1024,256]{1,0:T(8,128)(2,1)S(1)} %collective-permute-done.33.refs_5_), channel_id=1, source_target_pairs={{0,16},{8,24},{16,0},{24,8},{1,17},{9,25},{17,1},{25,9},{2,18},{10... | collective-permute-start | bytes 1572872 | tf_op jit(solution)/shard_map/ppermute | solution.py:712
  396.0 13.6 %collective-permute-start.38 = (f32[2,2048]{1,0:T(2,128)S(1)}, f32[2,2048]{1,0:T(2,128)S(1)}, u32[]{:S(2)}, u32[]{:S(2)}) collective-permute-start(f32[2,2048]{1,0:T(2,128)S(1)} %fusion.14), channel_id=1, source_target_pairs={{0,16},{8,24},{16,0},{24,8},{1,17},{9,25},{17,1},{25,9},{2,18},{10... | collective-permute-start | bytes 49160 | tf_op jit(solution)/shard_map/ppermute | solution.py:712
  (37 other events, 100.7 us)
Sparse Core Ops, SparseCore 0:
  10.3 40.9 all-gather.3
  72.0 39.6 reduce-scatter.4
  113.9 39.0 all-gather.5
  187.2 37.9 reduce-scatter.6
  232.5 35.3 all-gather.7
  307.3 43.0 reduce-scatter.8
  353.3 38.6 reduce-scatter.10

commit v6 on v5

--- a/solution.py
+++ b/solution.py
@@ -861,14 +861,16 @@
     branches = jnp.concatenate([branch_gate.T, branch_input.T])
 
     scalars = jnp.concatenate([quarter_spots(), lengths[0]])[None]
-    first_rows = tie(first_rows, rate_w, inlet_w, extra, branches, scalars)
+    onward = {0: out_grad}
+    first_rows, onward[1] = lax.optimization_barrier(
+        (first_rows, next_chip(out_grad, 1), rate_w, inlet_w, extra, branches, scalars)
+    )[:2]
     block_partial, mixed, conv, rate, inlet, state, both = forward_mix(
         scalars, first_rows, branches, block_out, conv_weight, rate_w, inlet_w, extra
     )
     chips = lax.axis_size("mp") // 2
-    onward, backward = {0: tie(out_grad, first_rows)}, {}
-    onward[1], backward[1] = next_chip(onward[0], 1), next_chip(onward[0], -1)
-    block_partial, onward[1], backward[1] = lax.optimization_barrier((block_partial, onward[1], backward[1]))
+    backward = {1: next_chip(tie(onward[0], first_rows), -1)}
+    block_partial, backward[1] = lax.optimization_barrier((block_partial, backward[1]))
 
     block_sum = sum_rows(block_partial)
     shards = {hop: piece for hop, piece in onward.items()} | {-hop: piece for hop, piece in backward.items()}

time: 430 us -> 426 us (level)
  waiting for transfers between devices: 182 us -> 173 us
    all_gather x3, waiting for transfers between devices: 39.1 us -> 34.8 us  [all_rows(): return lax.all_gather(values, 'mp', axis=0, tiled=True)]
    unnamed x110 -> x118, local copies, waits for them, and re-layouts: 16.3 us -> 17 us
  transfers between devices with their start and end apart: 46 -> 46, of which waited for: 22 -> 21; matrix products, arithmetic and copies ran while one was open for 16% -> 16% of each run, Pallas kernels for 20% -> 20%
where the time goes in v6:
time: 426 us; the launch traced here: 419 us
  waiting for transfers between devices  173 us (41%)
  Pallas kernels  92.1 us (22%)
  other arithmetic  51.3 us (12%)
  starting transfers between devices  38.5 us (9%)
  local copies, waits for them, and re-layouts  29.4 us (7%)
  matrix products  19.7 us (5%)
  between operations  15.2 us (4%)
    ppermute x32, waiting for transfers between devices, swap(): return lax.ppermute(values, 'dp', [(i, i ^ 1 << bit) for i in range(count)])  70.9 us
    reduce_scatter x4, waiting for transfers between devices, sum_rows(): lax.psum_scatter(values.astype(LOW), 'mp', scatter_dimension=0, tiled=True)  51.1 us
    all_gather x3, waiting for transfers between devices, all_rows(): return lax.all_gather(values, 'mp', axis=0, tiled=True)  34.8 us
    ppermute x32, starting transfers between devices, swap(): return lax.ppermute(values, 'dp', [(i, i ^ 1 << bit) for i in range(count)])  32.2 us
    pallas_call x1, Pallas kernels, backward_mix(): pl.pallas_call(lambda *refs: backward_kernel(heads, owners, *refs), in_sp...  24.1 us
    pallas_call x6, Pallas kernels, place(): pl.pallas_call(lambda *refs: place_kernel(count, axis, splits, len(onto),...  22.8 us
    unnamed x118, local copies, waits for them, and re-layouts  17 us
    pallas_call x5, Pallas kernels, call_blocks(): pl.pallas_call(body, grid_spec=pltpu.PrefetchScalarGridSpec(num_scalar_pr...  16.6 us
  transfers between devices with their start and end apart: 46, of which 21 were waited for; matrix products, arithmetic and copies ran while one was open for 16% of the time, Pallas kernels for 20%

profile of v6, /device:TPU:0, one launch (start us, length us, event | category | flops | bytes accessed | tf_op | source)
XLA Modules:
  0.0 419.3 jit_solution(14995847824948074361)
XLA Ops:
  7.3 2.2 shard_map.305
  9.6 3.1 collective-permute-start
  16.1 1.5 bitcast_dynamic-update-slice_fusion.1
  18.8 1.9 reshape.211.refs_5_.refs_13_
  24.3 3.6 pad_maximum_fusion.refs_1_.refs_10_
  27.8 23.5 %all-gather.4.cloned.1.call-done.refs_0_.refs_9_ = bf16[768,2048]{1,0:T(8,128)(2,1)} async-done(((bf16[96,2048]{1,0:T(8,128)(2,1)}), bf16[768,2048]{1,0:T(8,128)(2,1)}) %all-gather.4.cloned.1.call-update) | async-done | bytes 3145744 | tf_op jit(solution)/shard_map/all_gather | solution.py:653
  51.3 1.5 collective-permute-start.1
  52.8 15.2 %shard_map.306 = (bf16[768,2048]{1,0:T(8,128)(2,1)}, bf16[768,320]{1,0:T(8,128)(2,1)}, bf16[768,320]{1,0:T(8,128)(2,1)}, f32[768,320]{1,0:T(8,128)}, f32[768,320...) custom-call(s32[1,7]{1,0:T(1,128)} %bitcast.67, bf16[768,2048]{1,0:T(8,128)(2,1)} %all-gather.4.cloned.1.call-done.refs_0_.refs_9_, ...), custom_call_target="tpu_custom_call" | custom-call | tf_op jit(solution)/shard_map/pallas_call | solution.py:398
  72.9 35.2 %reduce-scatter.5.cloned.1.call-done.added_ref = bf16[96,2048]{1,0:T(8,128)(2,1)} async-done(((bf16[768,2048]{1,0:T(8,128)(2,1)}), bf16[96,2048]{1,0:T(8,128)(2,1)}) %reduce-scatter.5.cloned.1.call-update) | async-done | bytes 393232 | tf_op jit(solution)/shard_map/reduce_scatter | solution.py:649
  108.1 2.1 shard_map.307
  110.9 12.6 %collective-permute-done.5.refs_7_ = bf16[96,2048]{1,0:T(8,128)(2,1)} collective-permute-done((bf16[96,2048]{1,0:T(8,128)(2,1)}, bf16[96,2048]{1,0:T(8,128)(2,1)}, u32[]{:S(2)}, u32[]{:S(2)}) %collective-permute-start.5) | collective-permute-done | bytes 393248 | tf_op jit(solution)/shard_map/ppermute | solution.py:817
  123.5 2.0 collective-permute-done.6.refs_8_
  129.5 2.8 shard_map.308
  132.3 1.7 copy-done.2
  134.0 4.1 fusion.16
  138.1 11.3 %all-gather.6.cloned.1.call-done.refs_0_.left_ref = bf16[768,2048]{1,0:T(8,128)(2,1)} async-done(((bf16[96,2048]{1,0:T(8,128)(2,1)}), bf16[768,2048]{1,0:T(8,128)(2,1)}) %all-gather.6.cloned.1.call-update) | async-done | bytes 3145744 | tf_op jit(solution)/shard_map/all_gather | solution.py:653
  149.4 5.6 %fusion.17 = f32[768,768]{1,0:T(8,128)S(1)} fusion(bf16[768,2048]{1,0:T(8,128)(2,1)} %all-gather.6.cloned.1.call-done.refs_0_.left_ref, bf16[2048,768]{1,0:T(8,128)(2,1)} %refs_3_.3), kind=kOutput, calls=%fused_computation.67 | convolution fusion | flops 2415919104 | bytes 8650752 | tf_op jit(solution)/shard_map/dot_general | solution.py:27
  155.0 2.9 fusion.5
  158.0 2.9 convolution_convert_fusion
  160.9 1.5 broadcast_select_fusion
  162.4 1.5 collective-permute-start.8
  165.9 2.8 multiply_convert_fusion
  168.8 12.4 %shard_map.309 = (bf16[768,2048]{1,0:T(8,128)(2,1)}, bf16[1024,768]{1,0:T(8,128)(2,1)}, bf16[1024,768]{1,0:T(8,128)(2,1)}) custom-call(s32[2]{0:T(128)} %pad_add_fusion.spots_ref, bf16[768,2048]{1,0:T(8,128)(2,1)} %all-gather.6.cloned.1.call-done.refs_0_.left_ref, bf16[768,768]{1,0:T(8,128)(2,1)} %get-tuple-element.322.refs_1_.right_ref, ...), custom_call_target="tpu_custom_call" | custom-call | tf_op jit(solution)/shard_map/pallas_call | solution.py:546
  183.5 1.5 collective-permute-start.11
  186.1 2.5 add_convert_fusion.16
  189.0 2.1 add_convert_fusion.18
  191.0 1.5 collective-permute-start.9
  193.1 4.8 %shard_map.311 = bf16[1024,768]{1,0:T(8,128)(2,1)} custom-call(s32[2]{0:T(128)} %pad_add_fusion.2._, bf16[768,2048]{1,0:T(8,128)(2,1)} %all-gather.6.cloned.1.call-done.refs_0_.left_ref, bf16[768,768]{1,0:T(8,128)(2,1)} %get-tuple-element.321.refs_2_.right_ref), custom_call_target="tpu_custom_call" | custom-call | tf_op jit(solution)/shard_map/pallas_call | solution.py:449
  197.9 4.8 %shard_map.310 = bf16[1024,768]{1,0:T(8,128)(2,1)} custom-call(s32[2]{0:T(128)} %pad_add_fusion.1._, bf16[768,2048]{1,0:T(8,128)(2,1)} %all-gather.6.cloned.1.call-done.refs_0_.left_ref, bf16[768,768]{1,0:T(8,128)(2,1)} %get-tuple-element.322.refs_1_.right_ref), custom_call_target="tpu_custom_call" | custom-call | tf_op jit(solution)/shard_map/pallas_call | solution.py:449
  202.7 2.9 add_convert_fusion.15
  205.6 15.9 %reduce-scatter.7.cloned.1.call-done.grad_ref = bf16[96,2048]{1,0:T(8,128)(2,1)} async-done(((bf16[768,2048]{1,0:T(8,128)(2,1)}), bf16[96,2048]{1,0:T(8,128)(2,1)}) %reduce-scatter.7.cloned.1.call-update) | async-done | bytes 393232 | tf_op jit(solution)/shard_map/reduce_scatter | solution.py:649
  221.5 2.7 shard_map.312
  224.2 3.5 collective-permute-done.10
  231.7 2.0 add_convert_fusion.14.refs_1_
  235.2 2.7 add_convert_fusion.3
  238.5 2.7 add_convert_fusion.5
  242.6 4.2 fusion.18
  247.5 3.1 add_convert_fusion.4
  250.6 1.8 add_convert_fusion.2
  252.4 14.1 %collective-permute-done.15.refs_2_ = bf16[768,256]{1,0:T(8,128)(2,1)} collective-permute-done((bf16[768,256]{1,0:T(8,128)(2,1)}, bf16[768,256]{1,0:T(8,128)(2,1)}, u32[]{:S(2)}, u32[]{:S(2)}) %collective-permute-start.15) | collective-permute-done | bytes 393248 | tf_op jit(solution)/shard_map/ppermute | solution.py:712
  273.5 24.1 %shard_map.313 = (bf16[896,2048]{1,0:T(8,128)(2,1)}, bf16[1024,512]{1,0:T(8,128)(2,1)}, bf16[1024,512]{1,0:T(8,128)(2,1)}, bf16[1024,512]{1,0:T(8,128)(2,1)}, bf16[1024,512]{1,0:T(8,128)(2,1)}) custom-call(s32[1,7]{1,0:T(1,128)} %bitcast.68, bf16[768,2048]{1,0:T(8,128)(2,1)} %all-gather.8.cloned.1.call-done.refs_1_, bf16[320,2048]{1,0:T(8,128)(2,1)} %refs_2_.3, ...), custom_call_target="tpu_custom_call" | custom-call | tf_op jit(solution)/shard_map/pallas_call | solution.py:424
  297.7 5.9 %collective-permute-done.24.refs_3_ = bf16[512,768]{1,0:T(8,128)(2,1)} collective-permute-done((bf16[512,768]{1,0:T(8,128)(2,1)S(1)}, bf16[512,768]{1,0:T(8,128)(2,1)}, u32[]{:S(2)}, u32[]{:S(2)}) %collective-permute-start.24) | collective-permute-done | bytes 786464 | tf_op jit(solution)/shard_map/ppermute | solution.py:712
  304.4 1.5 collective-permute-start.19
  309.6 1.5 collective-permute-start.30
  311.1 1.5 collective-permute-start.27
  312.6 18.2 %collective-permute-done.19 = bf16[1024,512]{1,0:T(8,128)(2,1)} collective-permute-done((bf16[1024,512]{1,0:T(8,128)(2,1)}, bf16[1024,512]{1,0:T(8,128)(2,1)}, u32[]{:S(2)}, u32[]{:S(2)}) %collective-permute-start.19) | collective-permute-done | bytes 1048608 | tf_op jit(solution)/shard_map/ppermute | solution.py:712
  332.3 1.9 add_convert_fusion.11
  334.8 1.5 add_convert_fusion.9
  336.3 2.9 collective-permute-done.29.refs_4_
  339.2 1.5 collective-permute-start.22
  340.6 2.3 add_convert_fusion.10
  342.9 2.3 add_convert_fusion.8
  345.9 10.1 %collective-permute-done.27.refs_4_ = bf16[512,768]{1,0:T(8,128)(2,1)S(1)} collective-permute-done((bf16[512,768]{1,0:T(8,128)(2,1)}, bf16[512,768]{1,0:T(8,128)(2,1)S(1)}, u32[]{:S(2)}, u32[]{:S(2)}) %collective-permute-start.27) | collective-permute-done | bytes 786464 | tf_op jit(solution)/shard_map/ppermute | solution.py:712
  358.4 5.3 %collective-permute-done.22 = bf16[1024,256]{1,0:T(8,128)(2,1)} collective-permute-done((bf16[1024,256]{1,0:T(8,128)(2,1)S(1)}, bf16[1024,256]{1,0:T(8,128)(2,1)}, u32[]{:S(2)}, u32[]{:S(2)}) %collective-permute-start.22) | collective-permute-done | bytes 524320 | tf_op jit(solution)/shard_map/ppermute | solution.py:712
  368.8 1.6 collective-permute-start.32
  370.4 1.5 collective-permute-start.31
  375.2 4.4 %shard_map.314 = f32[2048,768]{1,0:T(8,128)} custom-call(s32[4]{0:T(128)S(1)} %pad_add_fusion.3.refs_0_, bf16[512,768]{1,0:T(8,128)(2,1)S(1)} %add_convert_fusion.1.refs_1_, bf16[512,768]{1,0:T(8,128)(2,1)} %collective-permute-done.23.refs_2_, bf16[512,768]{1,0:T(8,128)(2,1)} %collective-permute-done.24.refs_3_, bf16[512,768]{1,0:T(8,128)(2,1)S(1)} %copy-done.14), custom_call_target="tpu_custom_call" | custom-call | tf_op jit(solution)/shard_map/pallas_call | solution.py:691
  379.6 4.4 %shard_map.315 = f32[768,2048]{1,0:T(8,128)} custom-call(s32[8]{0:T(128)S(1)} %stack.186.refs_0_, bf16[768,256]{1,0:T(8,128)(2,1)} %add_convert_fusion.14.refs_1_, bf16[768,256]{1,0:T(8,128)(2,1)} %collective-permute-done.15.refs_2_, bf16[768,256]{1,0:T(8,128)(2,1)} %collective-permute-done.16.refs_3_, bf16[768,256]{1,0:T(8,128)(2,1)S(1)} %copy-done.20, ...), custom_call_target="tpu_custom_call" | custom-call | tf_op jit(solution)/shard_map/pallas_call | solution.py:691
  384.0 4.7 %collective-permute-done.35 = f32[2,2048]{1,0:T(2,128)S(1)} collective-permute-done((f32[2,2048]{1,0:T(2,128)S(1)}, f32[2,2048]{1,0:T(2,128)S(1)}, u32[]{:S(2)}, u32[]{:S(2)}) %collective-permute-start.35) | collective-permute-done | bytes 16416 | tf_op jit(solution)/shard_map/ppermute | solution.py:712
  390.8 1.5 collective-permute-start.37
  392.9 2.1 add_convert_fusion.12
  397.3 3.6 shard_map.316
  401.0 4.1 shard_map.317
  406.6 3.4 shard_map.318
  (232 shorter events, 65.9 us)
Async XLA Ops:
  7.2 126.8 %copy-start = (bf16[768,2048]{1,0:T(8,128)(2,1)S(1)}, bf16[768,2048]{1,0:T(8,128)(2,1)}, u32[]{:S(2)}) copy-start(bf16[768,2048]{1,0:T(8,128)(2,1)} %param.42) | copy-start | bytes 9437188
  7.2 10.4 %copy-start.52 = (f32[320]{0:T(512)S(1)}, f32[320]{0:T(512)}, u32[]{:S(2)}) copy-start(f32[320]{0:T(512)} %param.37) | copy-start | bytes 3844
  7.2 10.5 %copy-start.53 = (f32[320]{0:T(512)S(1)}, f32[320]{0:T(512)}, u32[]{:S(2)}) copy-start(f32[320]{0:T(512)} %param.32) | copy-start | bytes 3844
  7.2 10.5 %copy-start.54 = (f32[320]{0:T(512)S(1)}, f32[320]{0:T(512)}, u32[]{:S(2)}) copy-start(f32[320]{0:T(512)} %param.34) | copy-start | bytes 3844
  7.2 10.5 %copy-start.55 = (f32[320]{0:T(512)S(1)}, f32[320]{0:T(512)}, u32[]{:S(2)}) copy-start(f32[320]{0:T(512)} %param.36) | copy-start | bytes 3844
  7.2 44.1 %all-gather.4.cloned.1.call-start = ((), (), s32[]{:S(2)}) async-start(), calls=%async_computation.4 | async-start | bytes 3538944 | tf_op jit(solution)/shard_map/all_gather | solution.py:653
  9.5 13.5 %copy-start.56 = (s32[1,3]{1,0:T(1,128)S(1)}, s32[1,3]{1,0:T(1,128)}, u32[]{:S(2)}) copy-start(s32[1,3]{1,0:T(1,128)} %param.27) | copy-start | bytes 40
  9.5 98.5 %reduce-scatter.5.cloned.1.call-start = ((), (), s32[]{:S(2)}) async-start(), calls=%async_computation.5 | async-start | bytes 3538944 | tf_op jit(solution)/shard_map/reduce_scatter | solution.py:649
  9.6 18.2 %collective-permute-start = (bf16[96,2048]{1,0:T(8,128)(2,1)}, bf16[96,2048]{1,0:T(8,128)(2,1)}, u32[]{:S(2)}, u32[]{:S(2)}) collective-permute-start(bf16[96,2048]{1,0:T(8,128)(2,1)} %added_ref.3), channel_id=1, source_target_pairs={{0,2},{1,3},{2,4},{3,5},{4,6},{5,7},{6,0},{7,1},{8,10},{9,11},{10,... | collective-permute-start | bytes 1179656 | tf_op jit(solution)/shard_map/ppermute | solution.py:817
  24.3 27.1 %copy-start.6 = (bf16[96,2048]{1,0:T(8,128)(2,1)S(1)}, bf16[96,2048]{1,0:T(8,128)(2,1)}, u32[]{:S(2)}) copy-start(bf16[96,2048]{1,0:T(8,128)(2,1)} %added_ref.3) | copy-start | bytes 1179652
  51.3 16.7 %collective-permute-start.1 = (bf16[96,2048]{1,0:T(8,128)(2,1)S(1)}, bf16[96,2048]{1,0:T(8,128)(2,1)S(1)}, u32[]{:S(2)}, u32[]{:S(2)}) collective-permute-start(bf16[96,2048]{1,0:T(8,128)(2,1)S(1)} %copy-done.6), channel_id=1, source_target_pairs={{0,6},{1,7},{2,0},{3,1},{4,2},{5,3},{6,4},{7,5},{8,14},{9,15},{10,... | collective-permute-start | bytes 1179656 | tf_op jit(solution)/shard_map/ppermute | solution.py:817
  68.8 80.6 %all-gather.6.cloned.1.call-start = ((), (), s32[]{:S(2)}) async-start(), calls=%async_computation.6 | async-start | bytes 3538944 | tf_op jit(solution)/shard_map/all_gather | solution.py:653
  68.8 1.8 collective-permute-start.2
  68.9 2.5 collective-permute-start.3
  69.4 2.7 collective-permute-start.4
  110.2 111.3 %reduce-scatter.7.cloned.1.call-start = ((), (), s32[]{:S(2)}) async-start(), calls=%async_computation.7 | async-start | bytes 3538944 | tf_op jit(solution)/shard_map/reduce_scatter | solution.py:649
  110.3 13.2 %collective-permute-start.5 = (bf16[96,2048]{1,0:T(8,128)(2,1)}, bf16[96,2048]{1,0:T(8,128)(2,1)}, u32[]{:S(2)}, u32[]{:S(2)}) collective-permute-start(bf16[96,2048]{1,0:T(8,128)(2,1)} %collective-permute-done.refs_3_), channel_id=1, source_target_pairs={{0,2},{1,3},{2,4},{3,5},{4,6},{5,7},{6,0},{7,1},{8,10},{9,11},{10,... | collective-permute-start | bytes 1179656 | tf_op jit(solution)/shard_map/ppermute | solution.py:817
  123.5 2.1 collective-permute-start.6
  162.4 20.0 %collective-permute-start.8 = (bf16[768,512]{1,0:T(8,128)(2,1)}, bf16[768,512]{1,0:T(8,128)(2,1)}, u32[]{:S(2)}, u32[]{:S(2)}) collective-permute-start(bf16[768,512]{1,0:T(8,128)(2,1)} %get-tuple-element.323), channel_id=1, source_target_pairs={{0,16},{8,24},{16,0},{24,8},{1,17},{9,25},{17,1},{25,9},{2,18},{10... | collective-permute-start | bytes 2359304 | tf_op jit(solution)/shard_map/ppermute | solution.py:712
  163.9 19.5 %collective-permute-start.7 = (bf16[768,512]{1,0:T(8,128)(2,1)S(1)}, bf16[768,512]{1,0:T(8,128)(2,1)}, u32[]{:S(2)}, u32[]{:S(2)}) collective-permute-start(bf16[768,512]{1,0:T(8,128)(2,1)S(1)} %get-tuple-element.325), channel_id=1, source_target_pairs={{0,8},{8,0},{16,24},{24,16},{1,9},{9,1},{17,25},{25,17},{2,10},{10... | collective-permute-start | bytes 2359304 | tf_op jit(solution)/shard_map/ppermute | solution.py:712
  183.4 83.1 %all-gather.8.cloned.1.call-start = ((), (), s32[]{:S(2)}) async-start(), calls=%async_computation.8 | async-start | bytes 3538944 | tf_op jit(solution)/shard_map/all_gather | solution.py:653
  183.5 45.4 %collective-permute-start.11 = (bf16[1024,768]{1,0:T(8,128)(2,1)}, bf16[1024,768]{1,0:T(8,128)(2,1)}, u32[]{:S(2)}, u32[]{:S(2)}) collective-permute-start(bf16[1024,768]{1,0:T(8,128)(2,1)} %get-tuple-element.224), channel_id=1, source_target_pairs={{0,8},{8,0},{16,24},{24,16},{1,9},{9,1},{17,25},{25,17},{2,10},{10... | collective-permute-start | bytes 4718600 | tf_op jit(solution)/shard_map/ppermute | solution.py:712
  185.0 43.9 %collective-permute-start.12 = (bf16[1024,768]{1,0:T(8,128)(2,1)}, bf16[1024,768]{1,0:T(8,128)(2,1)}, u32[]{:S(2)}, u32[]{:S(2)}) collective-permute-start(bf16[1024,768]{1,0:T(8,128)(2,1)} %get-tuple-element.225), channel_id=1, source_target_pairs={{0,16},{8,24},{16,0},{24,8},{1,17},{9,25},{17,1},{25,9},{2,18},{10... | collective-permute-start | bytes 4718600 | tf_op jit(solution)/shard_map/ppermute | solution.py:712
  188.6 39.1 %collective-permute-start.10 = (bf16[768,256]{1,0:T(8,128)(2,1)}, bf16[768,256]{1,0:T(8,128)(2,1)}, u32[]{:S(2)}, u32[]{:S(2)}) collective-permute-start(bf16[768,256]{1,0:T(8,128)(2,1)} %add_convert_fusion.16), channel_id=1, source_target_pairs={{0,8},{8,0},{16,24},{24,16},{1,9},{9,1},{17,25},{25,17},{2,10},{10... | collective-permute-start | bytes 1179656 | tf_op jit(solution)/shard_map/ppermute | solution.py:712
  191.0 37.8 %collective-permute-start.9 = (bf16[768,256]{1,0:T(8,128)(2,1)}, bf16[768,256]{1,0:T(8,128)(2,1)}, u32[]{:S(2)}, u32[]{:S(2)}) collective-permute-start(bf16[768,256]{1,0:T(8,128)(2,1)} %add_convert_fusion.18), channel_id=1, source_target_pairs={{0,16},{8,24},{16,0},{24,8},{1,17},{9,25},{17,1},{25,9},{2,18},{10... | collective-permute-start | bytes 1179656 | tf_op jit(solution)/shard_map/ppermute | solution.py:712
  228.9 136.0 %reduce-scatter.9.cloned.1.call-start = ((), (), s32[]{:S(2)}) async-start(), calls=%async_computation.9 | async-start | bytes 4128768 | tf_op jit(solution)/shard_map/reduce_scatter | solution.py:649
  230.3 8.3 %copy-start.35 = (bf16[1024,768]{1,0:T(8,128)(2,1)S(1)}, bf16[1024,768]{1,0:T(8,128)(2,1)}, u32[]{:S(2)}) copy-start(bf16[1024,768]{1,0:T(8,128)(2,1)} %shard_map.310) | copy-start | bytes 4718596
  230.3 16.5 %collective-permute-start.18 = (bf16[768,256]{1,0:T(8,128)(2,1)S(1)}, bf16[768,256]{1,0:T(8,128)(2,1)}, u32[]{:S(2)}, u32[]{:S(2)}) collective-permute-start(bf16[768,256]{1,0:T(8,128)(2,1)S(1)} %add_convert_fusion.13.refs_5_), channel_id=1, source_target_pairs={{0,16},{8,24},{16,0},{24,8},{1,17},{9,25},{17,1},{25,9},{2,18},{10... | collective-permute-start | bytes 1179656 | tf_op jit(solution)/shard_map/ppermute | solution.py:712
  231.2 21.2 %collective-permute-start.17 = (bf16[768,256]{1,0:T(8,128)(2,1)S(1)}, bf16[768,256]{1,0:T(8,128)(2,1)}, u32[]{:S(2)}, u32[]{:S(2)}) collective-permute-start(bf16[768,256]{1,0:T(8,128)(2,1)S(1)} %add_convert_fusion.13.refs_5_), channel_id=1, source_target_pairs={{0,8},{8,0},{16,24},{24,16},{1,9},{9,1},{17,25},{25,17},{2,10},{10... | collective-permute-start | bytes 1179656 | tf_op jit(solution)/shard_map/ppermute | solution.py:712
  233.7 18.6 %collective-permute-start.16 = (bf16[768,256]{1,0:T(8,128)(2,1)}, bf16[768,256]{1,0:T(8,128)(2,1)}, u32[]{:S(2)}, u32[]{:S(2)}) collective-permute-start(bf16[768,256]{1,0:T(8,128)(2,1)} %add_convert_fusion.14.refs_1_), channel_id=1, source_target_pairs={{0,8},{8,0},{16,24},{24,16},{1,9},{9,1},{17,25},{25,17},{2,10},{10... | collective-permute-start | bytes 1179656 | tf_op jit(solution)/shard_map/ppermute | solution.py:712
  237.9 28.6 %collective-permute-start.14 = (bf16[512,768]{1,0:T(8,128)(2,1)}, bf16[512,768]{1,0:T(8,128)(2,1)}, u32[]{:S(2)}, u32[]{:S(2)}) collective-permute-start(bf16[512,768]{1,0:T(8,128)(2,1)} %add_convert_fusion.3), channel_id=1, source_target_pairs={{0,8},{8,0},{16,24},{24,16},{1,9},{9,1},{17,25},{25,17},{2,10},{10... | collective-permute-start | bytes 2359304 | tf_op jit(solution)/shard_map/ppermute | solution.py:712
  241.3 25.3 %collective-permute-start.13 = (bf16[512,768]{1,0:T(8,128)(2,1)}, bf16[512,768]{1,0:T(8,128)(2,1)}, u32[]{:S(2)}, u32[]{:S(2)}) collective-permute-start(bf16[512,768]{1,0:T(8,128)(2,1)} %add_convert_fusion.5), channel_id=1, source_target_pairs={{0,16},{8,24},{16,0},{24,8},{1,17},{9,25},{17,1},{25,9},{2,18},{10... | collective-permute-start | bytes 2359304 | tf_op jit(solution)/shard_map/ppermute | solution.py:712
  246.8 19.7 %collective-permute-start.15 = (bf16[768,256]{1,0:T(8,128)(2,1)}, bf16[768,256]{1,0:T(8,128)(2,1)}, u32[]{:S(2)}, u32[]{:S(2)}) collective-permute-start(bf16[768,256]{1,0:T(8,128)(2,1)} %add_convert_fusion.14.refs_1_), channel_id=1, source_target_pairs={{0,16},{8,24},{16,0},{24,8},{1,17},{9,25},{17,1},{25,9},{2,18},{10... | collective-permute-start | bytes 1179656 | tf_op jit(solution)/shard_map/ppermute | solution.py:712
  268.0 29.7 %collective-permute-start.26 = (bf16[512,768]{1,0:T(8,128)(2,1)S(1)}, bf16[512,768]{1,0:T(8,128)(2,1)S(1)}, u32[]{:S(2)}, u32[]{:S(2)}) collective-permute-start(bf16[512,768]{1,0:T(8,128)(2,1)S(1)} %add_convert_fusion.refs_1_), channel_id=1, source_target_pairs={{0,16},{8,24},{16,0},{24,8},{1,17},{9,25},{17,1},{25,9},{2,18},{10... | collective-permute-start | bytes 2359304 | tf_op jit(solution)/shard_map/ppermute | solution.py:712
  268.9 28.7 %collective-permute-start.25 = (bf16[512,768]{1,0:T(8,128)(2,1)S(1)}, bf16[512,768]{1,0:T(8,128)(2,1)S(1)}, u32[]{:S(2)}, u32[]{:S(2)}) collective-permute-start(bf16[512,768]{1,0:T(8,128)(2,1)S(1)} %add_convert_fusion.refs_1_), channel_id=1, source_target_pairs={{0,8},{8,0},{16,24},{24,16},{1,9},{9,1},{17,25},{25,17},{2,10},{10... | collective-permute-start | bytes 2359304 | tf_op jit(solution)/shard_map/ppermute | solution.py:712
  271.7 31.9 %collective-permute-start.24 = (bf16[512,768]{1,0:T(8,128)(2,1)S(1)}, bf16[512,768]{1,0:T(8,128)(2,1)}, u32[]{:S(2)}, u32[]{:S(2)}) collective-permute-start(bf16[512,768]{1,0:T(8,128)(2,1)S(1)} %add_convert_fusion.1.refs_1_), channel_id=1, source_target_pairs={{0,8},{8,0},{16,24},{24,16},{1,9},{9,1},{17,25},{25,17},{2,10},{10... | collective-permute-start | bytes 2359304 | tf_op jit(solution)/shard_map/ppermute | solution.py:712
  272.4 31.2 %collective-permute-start.23 = (bf16[512,768]{1,0:T(8,128)(2,1)S(1)}, bf16[512,768]{1,0:T(8,128)(2,1)}, u32[]{:S(2)}, u32[]{:S(2)}) collective-permute-start(bf16[512,768]{1,0:T(8,128)(2,1)S(1)} %add_convert_fusion.1.refs_1_), channel_id=1, source_target_pairs={{0,16},{8,24},{16,0},{24,8},{1,17},{9,25},{17,1},{25,9},{2,18},{10... | collective-permute-start | bytes 2359304 | tf_op jit(solution)/shard_map/ppermute | solution.py:712
  297.6 33.2 %copy-start.9 = (bf16[512,768]{1,0:T(8,128)(2,1)}, bf16[512,768]{1,0:T(8,128)(2,1)S(1)}, u32[]{:S(2)}) copy-start(bf16[512,768]{1,0:T(8,128)(2,1)S(1)} %collective-permute-done.25.refs_2_) | copy-start | bytes 2359300
  303.6 89.3 %reduce-scatter.11.cloned.1.call-start = ((), (), s32[]{:S(2)}) async-start(), calls=%async_computation.10 | async-start | bytes 3538944 | tf_op jit(solution)/shard_map/reduce_scatter | solution.py:649
  304.4 26.5 %collective-permute-start.19 = (bf16[1024,512]{1,0:T(8,128)(2,1)}, bf16[1024,512]{1,0:T(8,128)(2,1)}, u32[]{:S(2)}, u32[]{:S(2)}) collective-permute-start(bf16[1024,512]{1,0:T(8,128)(2,1)} %get-tuple-element.254), channel_id=1, source_target_pairs={{0,8},{8,0},{16,24},{24,16},{1,9},{9,1},{17,25},{25,17},{2,10},{10... | collective-permute-start | bytes 3145736 | tf_op jit(solution)/shard_map/ppermute | solution.py:712
  305.9 26.4 %collective-permute-start.20 = (bf16[1024,512]{1,0:T(8,128)(2,1)}, bf16[1024,512]{1,0:T(8,128)(2,1)}, u32[]{:S(2)}, u32[]{:S(2)}) collective-permute-start(bf16[1024,512]{1,0:T(8,128)(2,1)} %get-tuple-element.255), channel_id=1, source_target_pairs={{0,16},{8,24},{16,0},{24,8},{1,17},{9,25},{17,1},{25,9},{2,18},{10... | collective-permute-start | bytes 3145736 | tf_op jit(solution)/shard_map/ppermute | solution.py:712
  306.6 28.2 %copy-start.37 = (bf16[1024,512]{1,0:T(8,128)(2,1)S(1)}, bf16[1024,512]{1,0:T(8,128)(2,1)}, u32[]{:S(2)}) copy-start(bf16[1024,512]{1,0:T(8,128)(2,1)} %get-tuple-element.262) | copy-start | bytes 3145732
  309.1 30.1 %collective-permute-start.29 = (bf16[768,256]{1,0:T(8,128)(2,1)}, bf16[768,256]{1,0:T(8,128)(2,1)S(1)}, u32[]{:S(2)}, u32[]{:S(2)}) collective-permute-start(bf16[768,256]{1,0:T(8,128)(2,1)} %collective-permute-done.15.refs_2_), channel_id=1, source_target_pairs={{0,8},{8,0},{16,24},{24,16},{1,9},{9,1},{17,25},{25,17},{2,10},{10... | collective-permute-start | bytes 1179656 | tf_op jit(solution)/shard_map/ppermute | solution.py:712
  309.6 35.5 %collective-permute-start.30 = (bf16[768,256]{1,0:T(8,128)(2,1)}, bf16[768,256]{1,0:T(8,128)(2,1)S(1)}, u32[]{:S(2)}, u32[]{:S(2)}) collective-permute-start(bf16[768,256]{1,0:T(8,128)(2,1)} %collective-permute-done.17.refs_6_), channel_id=1, source_target_pairs={{0,16},{8,24},{16,0},{24,8},{1,17},{9,25},{17,1},{25,9},{2,18},{10... | collective-permute-start | bytes 1179656 | tf_op jit(solution)/shard_map/ppermute | solution.py:712
  311.1 44.9 %collective-permute-start.27 = (bf16[512,768]{1,0:T(8,128)(2,1)}, bf16[512,768]{1,0:T(8,128)(2,1)S(1)}, u32[]{:S(2)}, u32[]{:S(2)}) collective-permute-start(bf16[512,768]{1,0:T(8,128)(2,1)} %collective-permute-done.23.refs_2_), channel_id=1, source_target_pairs={{0,8},{8,0},{16,24},{24,16},{1,9},{9,1},{17,25},{25,17},{2,10},{10... | collective-permute-start | bytes 2359304 | tf_op jit(solution)/shard_map/ppermute | solution.py:712
  330.8 26.6 %collective-permute-start.28 = (bf16[512,768]{1,0:T(8,128)(2,1)S(1)}, bf16[512,768]{1,0:T(8,128)(2,1)S(1)}, u32[]{:S(2)}, u32[]{:S(2)}) collective-permute-start(bf16[512,768]{1,0:T(8,128)(2,1)S(1)} %collective-permute-done.25.refs_2_), channel_id=1, source_target_pairs={{0,16},{8,24},{16,0},{24,8},{1,17},{9,25},{17,1},{25,9},{2,18},{10... | collective-permute-start | bytes 2359304 | tf_op jit(solution)/shard_map/ppermute | solution.py:712
  332.3 8.3 %copy-start.38 = (bf16[1024,512]{1,0:T(8,128)(2,1)S(1)}, bf16[1024,512]{1,0:T(8,128)(2,1)}, u32[]{:S(2)}) copy-start(bf16[1024,512]{1,0:T(8,128)(2,1)} %get-tuple-element.258) | copy-start | bytes 3145732
  334.2 30.7 %collective-permute-start.21 = (bf16[1024,256]{1,0:T(8,128)(2,1)S(1)}, bf16[1024,256]{1,0:T(8,128)(2,1)}, u32[]{:S(2)}, u32[]{:S(2)}) collective-permute-start(bf16[1024,256]{1,0:T(8,128)(2,1)S(1)} %add_convert_fusion.11), channel_id=1, source_target_pairs={{0,16},{8,24},{16,0},{24,8},{1,17},{9,25},{17,1},{25,9},{2,18},{10... | collective-permute-start | bytes 1572872 | tf_op jit(solution)/shard_map/ppermute | solution.py:712
  339.2 24.5 %collective-permute-start.22 = (bf16[1024,256]{1,0:T(8,128)(2,1)S(1)}, bf16[1024,256]{1,0:T(8,128)(2,1)}, u32[]{:S(2)}, u32[]{:S(2)}) collective-permute-start(bf16[1024,256]{1,0:T(8,128)(2,1)S(1)} %add_convert_fusion.9), channel_id=1, source_target_pairs={{0,8},{8,0},{16,24},{24,16},{1,9},{9,1},{17,25},{25,17},{2,10},{10... | collective-permute-start | bytes 1572872 | tf_op jit(solution)/shard_map/ppermute | solution.py:712
  366.3 7.7 %copy-start.32 = (bf16[96,2048]{1,0:T(8,128)(2,1)S(1)}, bf16[96,2048]{1,0:T(8,128)(2,1)}, u32[]{:S(2)}) copy-start(bf16[96,2048]{1,0:T(8,128)(2,1)} %start_ref.3) | copy-start | bytes 1179652
  366.3 7.7 %copy-start.42 = (f32[96,2048]{1,0:T(8,128)S(1)}, f32[96,2048]{1,0:T(8,128)}, u32[]{:S(2)}) copy-start(f32[96,2048]{1,0:T(8,128)} %get-tuple-element.284) | copy-start | bytes 2359300
  366.3 7.7 %copy-start.44 = (f32[2048]{0:T(1024)S(1)}, f32[2048]{0:T(1024)}, u32[]{:S(2)}) copy-start(f32[2048]{0:T(1024)} %param.28) | copy-start | bytes 24580
  366.3 7.7 %copy-start.51 = (f32[96]{0:T(128)S(1)}, f32[96]{0:T(128)}, u32[]{:S(2)}) copy-start(f32[96]{0:T(128)} %add_rsqrt_fusion) | copy-start | bytes 1156
  366.3 22.4 %collective-permute-start.34 = (bf16[1024,256]{1,0:T(8,128)(2,1)S(1)}, bf16[1024,256]{1,0:T(8,128)(2,1)S(1)}, u32[]{:S(2)}, u32[]{:S(2)}) collective-permute-start(bf16[1024,256]{1,0:T(8,128)(2,1)S(1)} %add_convert_fusion.6.refs_4_), channel_id=1, source_target_pairs={{0,16},{8,24},{16,0},{24,8},{1,17},{9,25},{17,1},{25,9},{2,18},{10... | collective-permute-start | bytes 1572872 | tf_op jit(solution)/shard_map/ppermute | solution.py:712
  366.9 22.6 %collective-permute-start.33 = (bf16[1024,256]{1,0:T(8,128)(2,1)S(1)}, bf16[1024,256]{1,0:T(8,128)(2,1)S(1)}, u32[]{:S(2)}, u32[]{:S(2)}) collective-permute-start(bf16[1024,256]{1,0:T(8,128)(2,1)S(1)} %add_convert_fusion.6.refs_4_), channel_id=1, source_target_pairs={{0,8},{8,0},{16,24},{24,16},{1,9},{9,1},{17,25},{25,17},{2,10},{10... | collective-permute-start | bytes 1572872 | tf_op jit(solution)/shard_map/ppermute | solution.py:712
  368.8 20.7 %collective-permute-start.32 = (bf16[1024,256]{1,0:T(8,128)(2,1)S(1)}, bf16[1024,256]{1,0:T(8,128)(2,1)S(1)}, u32[]{:S(2)}, u32[]{:S(2)}) collective-permute-start(bf16[1024,256]{1,0:T(8,128)(2,1)S(1)} %add_convert_fusion.7.refs_1_), channel_id=1, source_target_pairs={{0,8},{8,0},{16,24},{24,16},{1,9},{9,1},{17,25},{25,17},{2,10},{10... | collective-permute-start | bytes 1572872 | tf_op jit(solution)/shard_map/ppermute | solution.py:712
  370.4 19.9 %collective-permute-start.31 = (bf16[1024,256]{1,0:T(8,128)(2,1)S(1)}, bf16[1024,256]{1,0:T(8,128)(2,1)}, u32[]{:S(2)}, u32[]{:S(2)}) collective-permute-start(bf16[1024,256]{1,0:T(8,128)(2,1)S(1)} %add_convert_fusion.7.refs_1_), channel_id=1, source_target_pairs={{0,16},{8,24},{16,0},{24,8},{1,17},{9,25},{17,1},{25,9},{2,18},{10... | collective-permute-start | bytes 1572872 | tf_op jit(solution)/shard_map/ppermute | solution.py:712
  373.4 18.9 %copy-start.45 = (f32[1,2048]{1,0:T(1,128)}, f32[1,2048]{1,0:T(1,128)S(1)}, u32[]{:S(2)}) copy-start(f32[1,2048]{1,0:T(1,128)S(1)} %get-tuple-element.327) | copy-start | bytes 24580
  373.4 18.9 %copy-start.47 = (f32[1,2048]{1,0:T(1,128)}, f32[1,2048]{1,0:T(1,128)S(1)}, u32[]{:S(2)}) copy-start(f32[1,2048]{1,0:T(1,128)S(1)} %get-tuple-element.328) | copy-start | bytes 24580
  373.4 15.3 %collective-permute-start.35 = (f32[2,2048]{1,0:T(2,128)S(1)}, f32[2,2048]{1,0:T(2,128)S(1)}, u32[]{:S(2)}, u32[]{:S(2)}) collective-permute-start(f32[2,2048]{1,0:T(2,128)S(1)} %pad_maximum_fusion.1), channel_id=1, source_target_pairs={{0,8},{8,0},{16,24},{24,16},{1,9},{9,1},{17,25},{25,17},{2,10},{10... | collective-permute-start | bytes 49160 | tf_op jit(solution)/shard_map/ppermute | solution.py:712
  379.6 15.4 %copy-start.8 = (bf16[512,768]{1,0:T(8,128)(2,1)S(1)}, bf16[512,768]{1,0:T(8,128)(2,1)}, u32[]{:S(2)}) copy-start(bf16[512,768]{1,0:T(8,128)(2,1)} %copy-done.7) | copy-start | bytes 2359300
  390.3 15.6 %collective-permute-start.36 = (bf16[1024,256]{1,0:T(8,128)(2,1)}, bf16[1024,256]{1,0:T(8,128)(2,1)}, u32[]{:S(2)}, u32[]{:S(2)}) collective-permute-start(bf16[1024,256]{1,0:T(8,128)(2,1)} %collective-permute-done.31.refs_2_), channel_id=1, source_target_pairs={{0,8},{8,0},{16,24},{24,16},{1,9},{9,1},{17,25},{25,17},{2,10},{10... | collective-permute-start | bytes 1572872 | tf_op jit(solution)/shard_map/ppermute | solution.py:712
  390.8 15.1 %collective-permute-start.37 = (bf16[1024,256]{1,0:T(8,128)(2,1)S(1)}, bf16[1024,256]{1,0:T(8,128)(2,1)}, u32[]{:S(2)}, u32[]{:S(2)}) collective-permute-start(bf16[1024,256]{1,0:T(8,128)(2,1)S(1)} %collective-permute-done.33.refs_5_), channel_id=1, source_target_pairs={{0,16},{8,24},{16,0},{24,8},{1,17},{9,25},{17,1},{25,9},{2,18},{10... | collective-permute-start | bytes 1572872 | tf_op jit(solution)/shard_map/ppermute | solution.py:712
  392.3 13.6 %collective-permute-start.38 = (f32[2,2048]{1,0:T(2,128)S(1)}, f32[2,2048]{1,0:T(2,128)S(1)}, u32[]{:S(2)}, u32[]{:S(2)}) collective-permute-start(f32[2,2048]{1,0:T(2,128)S(1)} %fusion.14), channel_id=1, source_target_pairs={{0,16},{8,24},{16,0},{24,8},{1,17},{9,25},{17,1},{25,9},{2,18},{10... | collective-permute-start | bytes 49160 | tf_op jit(solution)/shard_map/ppermute | solution.py:712
  (41 other events, 124.2 us)
Sparse Core Ops, SparseCore 0:
  10.3 40.9 all-gather.3
  68.9 39.1 reduce-scatter.4
  110.3 39.0 all-gather.5
  183.5 37.9 reduce-scatter.6
  229.0 35.2 all-gather.7
  303.7 43.0 reduce-scatter.8
  349.6 38.6 reduce-scatter.10
